TPU v7x, 32 devices: a whole 2x2x4 slice. The times are simulated.
32 devices in a mesh: graph: 8 (over y, x, core), mp: 4 (over z).
Axes of the slice: x: 2, y: 2, z: 4, core: 2. Of those that a mesh axis runs over, the one named last changes fastest.
Arguments:
- edge_feats: bfloat16 [16384, 512], P('graph', 'mp'), may hold values from -6 to 6
- edge_source: int32 [16384], P('graph'), may hold values from 0 to 16383, as said below
- edge_target: int32 [16384], P('graph'), may hold values from 0 to 16383, as said below
- edge_live: int32 [16384], P('graph'), may hold values from 0 to 1, as said below
- trip_partner: int32 [8, 16384], P(None, 'graph'), may hold values from 0 to 16383, as said below
- trip_mask: int32 [8, 16384], P(None, 'graph'), may hold values 0 or 1
- trip_basis: bfloat16 [16384, 128], P('graph'), may hold values from -6 to 6
- atom_feats: bfloat16 [16384, 512], P('graph', 'mp'), may hold values from -6 to 6
- w_msg: bfloat16 [512, 512], P(None, 'mp'), may hold values from -0.25 to 0.25
- w_down: bfloat16 [512, 64], replicated, may hold values from -0.25 to 0.25
- w_bil: bfloat16 [1024, 64], replicated, may hold values from -0.1875 to 0.1875
- w_up: bfloat16 [64, 512], P(None, 'mp'), may hold values from -0.75 to 0.75
- w_atom: bfloat16 [512, 512], P(None, 'mp'), may hold values from -0.25 to 0.25
- w_edge: bfloat16 [512, 512], P(None, 'mp'), may hold values from -0.25 to 0.25
Outputs:
- edge_out: bfloat16 [16384, 512], P('graph', 'mp')
- atom_out: bfloat16 [16384, 512], P('graph', 'mp')
Inputs may be any that keep to these rules, and one draw needn't show every extreme that they name: `edge_target`: edge slots lie in blocks of 256: the slots of graph shard g for destination shard d are slots (g * 8 + d) * 256 onward; every source atom of shard g's slots lies in atoms g * 2048 to (g + 1) * 2048 - 1, every target atom of a block for d in shard d's atoms. `edge_source`: source atoms belong to the shard that holds the slot. `edge_live`: in each block of 256 slots the live slots come first, at least one; in every draw some destination shard gets all 256 slots live from every source shard. `trip_partner`: A partner edge is a slot of the same block of 256 slots as the edge.
All inputs are finite; a program needn't handle non-finite values. No bound on the sum of `trip_mask` on one device may be relied on, other than what follows from the above.
Results may differ from a plain program's by a relative error of at most 0.01.
Values may be sent and summed in bfloat16 or wider, within the bound.
No kernel may reach another device: no remote copies, remote signals or barrier semaphores. Data moves between devices by JAX's collectives and lax.ppermute only.
A program may use at most 192 MiB of HBM per device.

v0:
```python
import math

import jax
import jax.numpy as jnp
from jax import lax
from jax.sharding import PartitionSpec as P

DT = 64
NB = 16
SLOTS = 8
CAP = 256


def local(
    edge_feats,
    edge_source,
    edge_target,
    edge_live,
    trip_partner,
    trip_mask,
    trip_basis,
    atom_feats,
    w_msg,
    w_down,
    w_bil,
    w_up,
    w_atom,
    w_edge,
):
    rows = edge_feats.shape[0]
    width = edge_feats.shape[1]
    atoms_local = atom_feats.shape[0]
    shard = lax.axis_index("graph")
    piece = lax.all_gather(edge_feats, "mp", axis=1, tiled=True)
    hid = jnp.dot(piece, w_msg, preferred_element_type=jnp.float32)
    down = jnp.dot(piece, w_down, preferred_element_type=jnp.float32)
    message = edge_feats.astype(jnp.float32) + jax.nn.silu(hid)
    down_rows = down.astype(jnp.bfloat16)
    blocks = rows // CAP
    group = math.gcd(blocks, 8)
    within_ids = jnp.transpose(trip_partner % CAP).reshape(blocks // group, group, CAP * SLOTS)
    down_blocks = down_rows.reshape(blocks // group, group, CAP, DT)
    columns = jnp.arange(CAP, dtype=jnp.int32)

    def pick_group(operands):
        ids, table = operands
        onehot = (ids[:, :, None] == columns[None, None, :]).astype(jnp.bfloat16)
        return jnp.einsum("gqc,gca->gqa", onehot, table, preferred_element_type=jnp.float32).astype(
            jnp.bfloat16
        )

    picked = lax.map(pick_group, (within_ids, down_blocks)).reshape(rows, SLOTS, DT)
    weights = (
        trip_basis.reshape(rows, SLOTS, NB)
        * jnp.transpose(trip_mask).astype(jnp.bfloat16)[:, :, None]
    )
    mixed = jnp.einsum("esb,esa->eba", weights, picked, preferred_element_type=jnp.float32).astype(
        jnp.bfloat16
    )
    bil = jnp.dot(mixed.reshape(rows, NB * DT), w_bil, preferred_element_type=jnp.float32).astype(
        jnp.bfloat16
    )
    total = message + jnp.dot(bil, w_up, preferred_element_type=jnp.float32)
    outgoing = (total * edge_live.astype(jnp.float32)[:, None]).astype(jnp.bfloat16)
    target_local = edge_target % atoms_local
    incoming, in_ids = (
        lax.all_to_all(outgoing, "graph", split_axis=0, concat_axis=0, tiled=True),
        lax.all_to_all(target_local, "graph", split_axis=0, concat_axis=0, tiled=True),
    )
    block = math.gcd(atoms_local, 512)

    def agg_block(index):
        ids = index * block + jnp.arange(block, dtype=jnp.int32)
        onehot = (ids[:, None] == in_ids[None, :]).astype(jnp.bfloat16)
        return jnp.dot(onehot, incoming, preferred_element_type=jnp.float32)

    agg = lax.map(agg_block, jnp.arange(atoms_local // block, dtype=jnp.int32)).reshape(
        atoms_local, width
    )
    atom_mid = (atom_feats.astype(jnp.float32) + agg).astype(jnp.bfloat16)
    ahid = jnp.dot(
        lax.all_gather(atom_mid, "mp", axis=1, tiled=True),
        w_atom,
        preferred_element_type=jnp.float32,
    )
    atom_out = (atom_mid.astype(jnp.float32) + jax.nn.silu(ahid)).astype(jnp.bfloat16)
    source_rows = jnp.take(atom_out, edge_source - shard * atoms_local, axis=0)
    named = jnp.take(atom_out, in_ids, axis=0)
    target_rows = lax.all_to_all(named, "graph", split_axis=0, concat_axis=0, tiled=True)
    pair = (source_rows.astype(jnp.float32) * target_rows.astype(jnp.float32)).astype(jnp.bfloat16)
    ehid = jnp.dot(
        lax.all_gather(pair, "mp", axis=1, tiled=True), w_edge, preferred_element_type=jnp.float32
    )
    edge_out = (total + jax.nn.silu(ehid)).astype(jnp.bfloat16)
    return (edge_out, atom_out)


def solution(mesh):
    return jax.shard_map(
        local,
        mesh=mesh,
        in_specs=(
            P("graph", "mp"),
            P("graph"),
            P("graph"),
            P("graph"),
            P(None, "graph"),
            P(None, "graph"),
            P("graph", None),
            P("graph", "mp"),
            P(None, "mp"),
            P(),
            P(),
            P(None, "mp"),
            P(None, "mp"),
            P(None, "mp"),
        ),
        out_specs=(P("graph", "mp"), P("graph", "mp")),
        check_vma=False,
    )
```

profile of v0, /device:TPU:0, one launch (start us, length us, event | category | flops | bytes accessed | tf_op | source)
XLA Modules:
  0.0 235.3 jit_solution(17766612996900487888)
XLA Ops:
  7.9 1.3 add_select_fusion.1
  9.2 5.2 %all-to-all-start = ((s32[8,256,1]{1,2,0:T(1,128)}), s32[8,256,1]{1,2,0:T(1,128)S(1)}, u32[]{:S(2)}, u32[]{:S(2)}) async-start(s32[8,256,1]{1,2,0:T(1,128)} %bitcast.7), calls=%async_computation | async-start | bytes 16384 | tf_op jit(solution)/shard_map/all_to_all | solution.py:68
  14.4 0.9 fusion.18
  16.1 1.2 copy.24
  17.4 0.8 convert_bitcast_fusion
  18.3 4.2 %copy.28 = bf16[2048,8,16]{2,1,0:T(8,128)(2,1)} copy(bf16[2048,8,16]{0,2,1:T(8,128)(2,1)S(1)} %broadcast_multiply_fusion) | data formatting | bytes 1048576 | tf_op jit(solution)/shard_map/mul | solution.py:54
  22.5 36.0 %all-gather.4.cloned.1.call-done = bf16[2048,512]{1,0:T(8,128)(2,1)} async-done(((bf16[2048,128]{1,0:T(8,128)(2,1)}), bf16[2048,512]{1,0:T(8,128)(2,1)}) %all-gather.4.cloned.1.call-update) | async-done | bytes 2097168 | tf_op jit(solution)/shard_map/all_gather | solution.py:34
  58.5 2.3 convolution_convert_fusion.1
  60.9 4.4 %fusion.12 = bf16[8,2048,64]{1,2,0:T(8,128)(2,1)S(1)} fusion(s32[8,2048]{1,0:T(8,128)S(1)} %eq.39, bf16[8,8,8,256]{3,2,1,0:T(8,128)(2,1)S(1)} %bitcast.52), kind=kOutput, calls=%fused_computation.13 | convolution fusion | flops 542113792 | bytes 2424832 | tf_op jit(solution)/shard_map/while/body/eval_jaxpr/gqc,gca->gqa/dot_general | solution.py:48
  65.3 3.2 %copy.27 = bf16[8,2048,64]{2,1,0:T(8,128)(2,1)} copy(bf16[8,2048,64]{1,2,0:T(8,128)(2,1)S(1)} %fusion.12) | data formatting | bytes 4194304 | tf_op jit(solution)/shard_map/while/body/eval_jaxpr/convert_element_type | solution.py:48
  68.5 9.3 %convolution_convert_fusion = bf16[2048,16,64]{2,1,0:T(8,128)(2,1)} fusion(bf16[2048,8,16]{2,1,0:T(8,128)(2,1)} %copy.28, bf16[2048,8,64]{2,1,0:T(8,128)(2,1)} %bitcast.48), kind=kOutput, calls=%fused_computation.12 | convolution fusion | flops 35651584 | bytes 6815744 | tf_op jit(solution)/shard_map/esb,esa->eba/dot_general | solution.py:57
  77.8 9.9 %copy.29 = bf16[2048,16,64]{0,2,1:T(8,128)(2,1)} copy(bf16[2048,16,64]{2,1,0:T(8,128)(2,1)} %convolution_convert_fusion) | data formatting | bytes 8388608 | tf_op jit(solution)/shard_map/convert_element_type | solution.py:57
  87.8 0.7 fusion.22
  88.5 4.6 %multiply_convert_fusion = (bf16[2048,128]{1,0:T(8,128)(2,1)}, f32[2048,128]{1,0:T(8,128)}) fusion(f32[2048]{0:T(1024)S(1)} %convert_element_type.66, bf16[64,128]{1,0:T(8,128)(2,1)S(1)} %copy-done.10, bf16[1024,64]{0,1:T(8,128)(2,1)S(1)} %copy-done, bf16[2048,1024]{0,1:T(8,128)(2,1)} %bitcast.49, f32[2048,128]{1,0:T(8,128)S(1)} %fusion.22, ...), kind=kOutput, calls=%fused_computation.23 | convolution fusion | flops 304480256 | bytes 7495680 | tf_op jit(solution)/shard_map/dot_general | solution.py:63
  93.1 3.7 %all-to-all-start.1 = ((bf16[8,256,128]{2,1,0:T(8,128)(2,1)}), bf16[8,256,128]{2,1,0:T(8,128)(2,1)S(1)}, u32[]{:S(2)}, u32[]{:S(2)}) async-start(bf16[8,256,128]{2,1,0:T(8,128)(2,1)} %bitcast.9), calls=%async_computation.1 | async-start | bytes 1048576 | tf_op jit(solution)/shard_map/all_to_all | solution.py:67
  96.9 9.7 %all-to-all-done.1 = bf16[8,256,128]{2,1,0:T(8,128)(2,1)S(1)} async-done(((bf16[8,256,128]{2,1,0:T(8,128)(2,1)}), bf16[8,256,128]{2,1,0:T(8,128)(2,1)S(1)}, u32[]{:S(2)}, u32[]{:S(2)}) %all-to-all-start.1) | async-done | bytes 524320 | tf_op jit(solution)/shard_map/all_to_all | solution.py:67
  106.6 8.1 %while.2 = (s32[]{:T(128)}, f32[4,512,128]{2,1,0:T(8,128)S(1)}, s32[4]{0:T(128)S(1)}, s32[2048]{0:T(1024)S(1)}, bf16[2048,128]{1,0:T(8,128)(2,1)S(1)}, /*index=5*/s32[]{:T(128)}, s32[1]{0:T(128)}) while((s32[]{:T(128)}, f32[4,512,128]{2,1,0:T(8,128)S(1)}, s32[4]{0:T(128)S(1)}, s32[2048]{0:T(1024)S(1)}, bf16[2048,128]{1,0:T(8,128)(2,1)S(1)}, ...), condition=%wide.region_1.2_spmd, body=%wide.region_0.1_spmd.sunk | while | flops 269484544 | bytes 798829 | solution.py:77
  107.8 0.8 fusion.42
  109.8 0.8 fusion.42
  111.9 0.8 fusion.42
  113.9 0.8 fusion.42
  114.7 0.9 fusion.14
  115.6 42.7 %all-gather.6.cloned.1.call-done = bf16[2048,512]{1,0:T(8,128)(2,1)} async-done(((bf16[2048,128]{1,0:T(8,128)(2,1)}), bf16[2048,512]{1,0:T(8,128)(2,1)}) %all-gather.6.cloned.1.call-update) | async-done | bytes 2097168 | tf_op jit(solution)/shard_map/all_gather | solution.py:82
  158.4 2.4 %add_convert_fusion.1 = bf16[2048,128]{1,0:T(8,128)(2,1)S(1)} fusion(bf16[2048,128]{1,0:T(8,128)(2,1)} %fusion.14, bf16[2048,512]{1,0:T(8,128)(2,1)} %all-gather.6.cloned.1.call-done, bf16[512,128]{1,0:T(8,128)(2,1)S(1)} %copy-done.8), kind=kOutput, calls=%fused_computation.22 | convolution fusion | flops 270270464 | bytes 3276800 | tf_op jit(solution)/shard_map/dot_general | solution.py:81
  160.8 6.2 %gather_fusion.1 = bf16[2048,128]{1,0:T(8,128)(2,1)S(1)} fusion(bf16[2048,128]{1,0:T(8,128)(2,1)S(1)} %add_convert_fusion.1, s32[2048]{0:T(1024)S(1)} %fusion.20), kind=kCustom, calls=%fused_computation.1.clone | custom fusion | bytes 1056768 | tf_op jit(solution)/shard_map/jit(_take)/gather | solution.py:88
  167.0 1.1 broadcast_select_fusion
  168.1 3.8 %all-to-all-start.2 = ((bf16[8,256,128]{2,1,0:T(8,128)(2,1)}), bf16[8,256,128]{2,1,0:T(8,128)(2,1)S(1)}, u32[]{:S(2)}, u32[]{:S(2)}) async-start(bf16[8,256,128]{2,1,0:T(8,128)(2,1)} %bitcast.12), calls=%async_computation.2 | async-start | bytes 1048576 | tf_op jit(solution)/shard_map/all_to_all | solution.py:89
  172.0 6.2 %gather_fusion = bf16[2048,128]{1,0:T(8,128)(2,1)S(1)} fusion(bf16[2048,128]{1,0:T(8,128)(2,1)S(1)} %add_convert_fusion.1, s32[2048]{0:T(1024)S(1)} %fusion.21), kind=kCustom, calls=%fused_computation.clone | custom fusion | bytes 1056768 | tf_op jit(solution)/shard_map/jit(_take)/gather | solution.py:87
  178.2 3.5 %all-to-all-done.2 = bf16[8,256,128]{2,1,0:T(8,128)(2,1)S(1)} async-done(((bf16[8,256,128]{2,1,0:T(8,128)(2,1)}), bf16[8,256,128]{2,1,0:T(8,128)(2,1)S(1)}, u32[]{:S(2)}, u32[]{:S(2)}) %all-to-all-start.2) | async-done | bytes 524320 | tf_op jit(solution)/shard_map/all_to_all | solution.py:89
  181.7 1.1 fusion.13
  182.8 42.8 %all-gather.8.cloned.1.call-done = bf16[2048,512]{1,0:T(8,128)(2,1)} async-done(((bf16[2048,128]{1,0:T(8,128)(2,1)}), bf16[2048,512]{1,0:T(8,128)(2,1)}) %all-gather.8.cloned.1.call-update) | async-done | bytes 2097168 | tf_op jit(solution)/shard_map/all_gather | solution.py:92
  225.6 3.1 %add_convert_fusion = bf16[2048,128]{1,0:T(8,128)(2,1)} fusion(f32[2048,128]{1,0:T(8,128)S(1)} %copy-done.11, bf16[2048,512]{1,0:T(8,128)(2,1)} %all-gather.8.cloned.1.call-done, bf16[512,128]{1,0:T(8,128)(2,1)S(1)} %copy-done.9), kind=kOutput, calls=%fused_computation.21 | convolution fusion | flops 270008320 | bytes 3801088 | tf_op jit(solution)/shard_map/dot_general | solution.py:91
  (49 shorter events, 4.2 us)
Async XLA Ops:
  7.2 81.3 %copy-start = (bf16[1024,64]{0,1:T(8,128)(2,1)S(1)}, bf16[1024,64]{0,1:T(8,128)(2,1)}, u32[]{:S(2)}) copy-start(bf16[1024,64]{0,1:T(8,128)(2,1)} %param.28) | copy-start | bytes 393220
  7.2 51.4 %all-gather.4.cloned.1.call-start = ((), (), s32[]{:S(2)}) async-start(), calls=%async_computation.3 | async-start | bytes 2621440 | tf_op jit(solution)/shard_map/all_gather | solution.py:34
  9.2 83.9 %all-to-all-start = ((s32[8,256,1]{1,2,0:T(1,128)}), s32[8,256,1]{1,2,0:T(1,128)S(1)}, u32[]{:S(2)}, u32[]{:S(2)}) async-start(s32[8,256,1]{1,2,0:T(1,128)} %bitcast.7), calls=%async_computation | async-start | bytes 16384 | tf_op jit(solution)/shard_map/all_to_all | solution.py:68
  15.6 6.9 %copy-start.7 = (s32[2048]{0:T(1024)S(1)}, s32[2048]{0:T(1024)}, u32[]{:S(2)}) copy-start(s32[2048]{0:T(1024)} %param.21) | copy-start | bytes 24580
  15.6 42.9 %copy-start.5 = (bf16[512,64]{0,1:T(8,128)(2,1)S(1)}, bf16[512,64]{0,1:T(8,128)(2,1)}, u32[]{:S(2)}) copy-start(bf16[512,64]{0,1:T(8,128)(2,1)} %param.27) | copy-start | bytes 196612
  77.8 10.0 %copy-start.2 = (bf16[2048,512]{1,0:T(8,128)(2,1)S(1)}, bf16[2048,512]{1,0:T(8,128)(2,1)}, u32[]{:S(2)}) copy-start(bf16[2048,512]{1,0:T(8,128)(2,1)} %all-gather.4.cloned.1.call-done) | copy-start | bytes 6291460
  77.8 10.0 %copy-start.4 = (bf16[512,128]{1,0:T(8,128)(2,1)S(1)}, bf16[512,128]{1,0:T(8,128)(2,1)}, u32[]{:S(2)}) copy-start(bf16[512,128]{1,0:T(8,128)(2,1)} %param.26) | copy-start | bytes 393220
  77.8 10.7 %copy-start.10 = (bf16[64,128]{1,0:T(8,128)(2,1)S(1)}, bf16[64,128]{1,0:T(8,128)(2,1)}, u32[]{:S(2)}) copy-start(bf16[64,128]{1,0:T(8,128)(2,1)} %param.29) | copy-start | bytes 49156
  93.1 13.4 %all-to-all-start.1 = ((bf16[8,256,128]{2,1,0:T(8,128)(2,1)}), bf16[8,256,128]{2,1,0:T(8,128)(2,1)S(1)}, u32[]{:S(2)}, u32[]{:S(2)}) async-start(bf16[8,256,128]{2,1,0:T(8,128)(2,1)} %bitcast.9), calls=%async_computation.1 | async-start | bytes 1048576 | tf_op jit(solution)/shard_map/all_to_all | solution.py:67
  96.8 61.6 %all-gather.6.cloned.1.call-start = ((), (), s32[]{:S(2)}) async-start(), calls=%async_computation.4 | async-start | bytes 2621440 | tf_op jit(solution)/shard_map/all_gather | solution.py:82
  106.5 8.1 %copy-start.3 = (bf16[2048,128]{1,0:T(8,128)(2,1)S(1)}, bf16[2048,128]{1,0:T(8,128)(2,1)}, u32[]{:S(2)}) copy-start(bf16[2048,128]{1,0:T(8,128)(2,1)} %param.25) | copy-start | bytes 1572868
  106.6 51.8 %copy-start.8 = (bf16[512,128]{1,0:T(8,128)(2,1)S(1)}, bf16[512,128]{1,0:T(8,128)(2,1)}, u32[]{:S(2)}) copy-start(bf16[512,128]{1,0:T(8,128)(2,1)} %param.30) | copy-start | bytes 393220
  160.8 17.5 %copy-start.1 = (bf16[2048,128]{1,0:T(8,128)(2,1)}, bf16[2048,128]{1,0:T(8,128)(2,1)S(1)}, u32[]{:S(2)}) copy-start(bf16[2048,128]{1,0:T(8,128)(2,1)S(1)} %add_convert_fusion.1) | copy-start | bytes 1572868
  160.8 11.2 %copy-start.6 = (s32[2048]{0:T(1024)S(1)}, s32[2048]{0:T(1024)}, u32[]{:S(2)}) copy-start(s32[2048]{0:T(1024)} %param.19) | copy-start | bytes 24580
  168.1 57.5 %copy-start.9 = (bf16[512,128]{1,0:T(8,128)(2,1)S(1)}, bf16[512,128]{1,0:T(8,128)(2,1)}, u32[]{:S(2)}) copy-start(bf16[512,128]{1,0:T(8,128)(2,1)} %param.31) | copy-start | bytes 393220
  168.1 57.5 %copy-start.11 = (f32[2048,128]{1,0:T(8,128)S(1)}, f32[2048,128]{1,0:T(8,128)}, u32[]{:S(2)}) copy-start(f32[2048,128]{1,0:T(8,128)} %get-tuple-element.57) | copy-start | bytes 3145732
  168.1 13.6 %all-to-all-start.2 = ((bf16[8,256,128]{2,1,0:T(8,128)(2,1)}), bf16[8,256,128]{2,1,0:T(8,128)(2,1)S(1)}, u32[]{:S(2)}, u32[]{:S(2)}) async-start(bf16[8,256,128]{2,1,0:T(8,128)(2,1)} %bitcast.12), calls=%async_computation.2 | async-start | bytes 1048576 | tf_op jit(solution)/shard_map/all_to_all | solution.py:89
  171.9 53.7 %all-gather.8.cloned.1.call-start = ((), (), s32[]{:S(2)}) async-start(), calls=%async_computation.5 | async-start | bytes 2621440 | tf_op jit(solution)/shard_map/all_gather | solution.py:92
Sparse Core Ops, SparseCore 0:
  9.6 48.9 all-gather.3
  115.7 42.5 all-gather.5
  183.0 42.6 all-gather.7
where the time goes:
time: 236 us; the launch traced here: 235 us
  waiting for transfers between devices  135 us (57%)
  local copies, waits for them, and re-layouts  34.2 us (14%)
  matrix products  29.9 us (13%)
  between operations  13.9 us (6%)
  starting transfers between devices  12.8 us (5%)
  other arithmetic  6.28 us (3%)
  loops' own time  2.7 us (1%)
    all_gather x1, waiting for transfers between devices, local(): lax.all_gather(pair, 'mp', axis=1, tiled=True)  42.8 us
    all_gather x1, waiting for transfers between devices, local(): lax.all_gather(atom_mid, 'mp', axis=1, tiled=True)  42.7 us
    all_gather x1, waiting for transfers between devices, local(): piece = lax.all_gather(edge_feats, 'mp', axis=1, tiled=True)  36 us
    convert_element_type x1, local copies, waits for them, and re-layouts, local(): jnp.einsum('esb,esa->eba', weights, picked, preferred_element_type=jnp.fl...  9.94 us
    all_to_all x1, waiting for transfers between devices, local(): lax.all_to_all(outgoing, 'graph', split_axis=0, concat_axis=0, tiled=True)  9.69 us
    dot_general x1, matrix products, local(): jnp.einsum('esb,esa->eba', weights, picked, preferred_element_type=jnp.fl...  9.28 us
    gather x1, local copies, waits for them, and re-layouts, local(): source_rows = jnp.take(atom_out, edge_source - shard * atoms_local, axis=0)  6.18 us
    gather x1, local copies, waits for them, and re-layouts, local(): named = jnp.take(atom_out, in_ids, axis=0)  6.18 us
  transfers between devices with their start and end apart: 6, of which 5 were waited for; matrix products, arithmetic and copies ran while one was open for 21% of the time, Pallas kernels for 0%

commit v1 on v0

v1 whole, which is shorter than its diff:
```python
import functools

import jax
import jax.numpy as jnp
from jax import lax
from jax.experimental import pallas as pl
from jax.experimental.pallas import tpu as pltpu
from jax.sharding import PartitionSpec as P

NB = 16
SLOTS = 8
CAP = 256
BF = jnp.bfloat16
F32 = jnp.float32
VMEM_LIMIT = 40 * 1024 * 1024


def shard_at(plane, slot, n_graph, n_mp):
    half = n_mp // 2
    odd = (slot % 2) ^ (plane // half)
    chip = (slot // 2) * n_mp + (plane + half * odd) % n_mp
    return 2 * chip + odd


def silu(v):
    return v / (1.0 + jnp.exp(-v))


def dot(a, b):
    return jnp.dot(a, b, preferred_element_type=F32)


def dot_t(a, b):
    return lax.dot_general(a, b, (((1,), (1,)), ((), ())), preferred_element_type=F32)


def call(kernel, out_shapes, info, args, scratch=(), grid=(1,), in_specs=None, out_specs=None, flops=0, moved=0):
    whole = lambda s: pl.BlockSpec(s.shape, functools.partial(lambda n, *_: (0,) * n, len(s.shape)))
    in_specs = [whole(a) if in_specs is None or in_specs[i] is None else in_specs[i] for i, a in enumerate(args)]
    out_specs = [
        whole(o) if out_specs is None or out_specs[i] is None else out_specs[i] for i, o in enumerate(out_shapes)
    ]
    return pl.pallas_call(
        kernel,
        out_shape=list(out_shapes),
        grid_spec=pltpu.PrefetchScalarGridSpec(
            num_scalar_prefetch=1, grid=grid, in_specs=in_specs, out_specs=out_specs, scratch_shapes=list(scratch)
        ),
        compiler_params=pltpu.CompilerParams(vmem_limit_bytes=VMEM_LIMIT),
        cost_estimate=pl.CostEstimate(flops=flops, bytes_accessed=moved, transcendentals=0),
    )(info, *args)


def sds(shape, dtype=BF):
    return jax.ShapeDtypeStruct(tuple(shape), dtype)


def block_rows(i):
    return pl.ds(pl.multiple_of(i * CAP, CAP), CAP)


def lanes(i, width):
    return pl.ds(pl.multiple_of(i * width, width), width)


def column(row):
    wide = jnp.broadcast_to(row.astype(F32), (8, row.shape[1]))
    return jnp.transpose(wide)[:, :1].astype(jnp.int32)


def solution(mesh):
    G = mesh.shape["graph"]
    M = mesh.shape["mp"]
    per = G // M
    at = functools.partial(shard_at, n_graph=G, n_mp=M)
    both = ("graph", "mp")

    def over_mp(x, k):
        return lax.ppermute(x, "mp", [(i, i ^ k) for i in range(M)])

    def over_plane(x, k):
        return lax.ppermute(x, "graph", [(i, i ^ k) for i in range(G)])

    home_to_plane = [
        (at(z, s) * M + f, (s * M + f) * M + z) for z in range(M) for s in range(per) for f in range(M)
    ]
    plane_to_home = [(b, a) for a, b in home_to_plane]

    def source_route(r):
        return [
            ((s * M + f) * M + z, at(z, s) * M + (f ^ r)) for z in range(M) for s in range(per) for f in range(M)
        ]

    def prepare(info, ef, tgt, src, wm, wu, wa, we, *outs):
        g, m = info[0], info[1]
        chunks, (ids, w1, w2) = outs[:M], outs[M:]
        for k in range(M):
            for s in range(per):
                chunks[k][s * CAP : (s + 1) * CAP, :] = ef[block_rows(at(m ^ k, s)), :]
        core = g % 2
        half, uhalf = w1.shape[0] - wu.shape[0] // 2, wu.shape[0] // 2
        w1[:half, :] = wm[pl.ds(pl.multiple_of(core * half, half), half), :]
        w1[half:, :] = wu[pl.ds(pl.multiple_of(core * uhalf, uhalf), uhalf), :]
        w2[:half, :] = wa[pl.ds(pl.multiple_of(core * half, half), half), :]
        w2[half:, :] = we[pl.ds(pl.multiple_of(core * half, half), half), :]
        atoms = info[2]
        for d in range(G):
            ids[d, 0:1, :] = lax.rem(tgt[pl.ds(at(m, d // M), 1), :], atoms)
            ids[d, 1:, :] = lax.rem(src[...], atoms)

    def triplets(info, *refs):
        m = info[1]
        xs, (partner, mask, basis, wdt, wbt, x_out, bil_out, mixed) = refs[:M], refs[M:]
        w = xs[0].shape[1]
        for k in range(M):
            x_out[:, lanes(m ^ k, w)] = xs[k][...]
        downt = dot_t(wdt[...], x_out[...]).astype(BF)
        dt = downt.shape[0]
        ids = lax.rem(partner[...], CAP)
        rows = lax.broadcasted_iota(jnp.int32, (CAP, CAP), 0)
        picked = []
        for s in range(SLOTS):
            onehot = (rows == ids[s : s + 1, :]).astype(F32).astype(BF)
            picked.append(dot(downt, onehot))
        basist = jnp.transpose(basis[...].astype(F32))
        maskf = mask[...].astype(F32)
        weight = [basist[s * NB : (s + 1) * NB, :] * maskf[s : s + 1, :] for s in range(SLOTS)]
        for b in range(NB):
            acc = weight[0][b : b + 1, :] * picked[0]
            for s in range(1, SLOTS):
                acc = acc + weight[s][b : b + 1, :] * picked[s]
            mixed[b * dt : (b + 1) * dt, :] = acc.astype(BF)
        bilt = dot(wbt[...], mixed[...])
        bil_out[...] = jnp.transpose(bilt).astype(BF)

    def put_weights(m, mine, other, dst, core, half, upto, width):
        start = upto
        for k in range(M):
            cols = lanes(m ^ k, width)
            dst[pl.ds(pl.multiple_of(core * half, half), half), cols] = mine[k][start : start + half, :]
            dst[pl.ds(pl.multiple_of((1 - core) * half, half), half), cols] = other[k][start : start + half, :]

    def messages(info, *refs):
        g, m = info[0], info[1]
        mine, other = refs[:M], refs[M : 2 * M]
        x, bil, live, total_out, out, wm, wu = refs[2 * M :]
        width = out.shape[3]
        half = wm.shape[0] // 2

        @pl.when(pl.program_id(0) == 0)
        def _():
            put_weights(m, mine, other, wm, g % 2, half, 0, width)
            put_weights(m, mine, other, wu, g % 2, wu.shape[0] // 2, half, width)

        hid = dot(x[...], wm[...])
        total = x[...].astype(F32) + silu(hid) + dot(bil[...], wu[...])
        total_out[...] = total
        alive = column(live[pl.ds(at(m, pl.program_id(0)), 1), :]).astype(F32)
        sent = (total * alive).astype(BF)
        for f in range(M):
            out[0, f] = sent[:, f * width : (f + 1) * width]

    def aggregate(info, incoming, ids, af, *outs):
        f = info[0] % M
        part = outs[0].shape[0]
        for r in range(M):
            q = f ^ r
            rows = lax.broadcasted_iota(jnp.int32, (part, CAP), 0) + q * part

            def add(g, acc):
                onehot = (rows == ids[g, 0:1, :]).astype(F32).astype(BF)
                return acc + dot(onehot, incoming[g])

            acc = lax.fori_loop(0, G, add, jnp.zeros(outs[0].shape, F32), unroll=G <= 8)
            base = af[pl.ds(pl.multiple_of(q * part, part), part), :].astype(F32)
            outs[r][...] = (base + acc).astype(BF)

    def atom_layer(info, *refs):
        g, m = info[0], info[1]
        f = g % M
        xs, mine, other = refs[:M], refs[M : 2 * M], refs[2 * M : 3 * M]
        outs, (x, wa) = refs[3 * M : 4 * M], refs[4 * M :]
        width = xs[0].shape[1]
        for r in range(M):
            x[:, lanes(f ^ r, width)] = xs[r][...]
        put_weights(m, mine, other, wa, g % 2, wa.shape[0] // 2, 0, width)
        ahid = dot(x[...], wa[...])
        x[...] = (x[...].astype(F32) + silu(ahid)).astype(BF)
        for r in range(M):
            outs[r][...] = x[:, lanes(f ^ r, width)]

    def pick_rows(row, table):
        atoms = table.shape[0]
        onehot = lax.broadcasted_iota(jnp.int32, (CAP, atoms), 1) == column(row)
        return dot(onehot.astype(F32).astype(BF), table[...]).astype(BF)

    def sources(info, *refs):
        g, m = info[0], info[1]
        f, slot = g % M, g // M
        parts, ids, outs, table = refs[:M], refs[M], refs[M + 1 : 2 * M + 1], refs[2 * M + 1]
        part = parts[0].shape[0]
        for r in range(M):
            table[pl.ds(pl.multiple_of((f ^ r) * part, part), part), :] = parts[r][...]
        mine = at(m, slot)
        for r in range(M):
            for s in range(per):
                row = ids[mine, pl.ds(1 + at(f ^ r, s), 1), :]
                outs[r][s * CAP : (s + 1) * CAP, :] = pick_rows(row, table)

    def targets(info, table, ids, out):
        def one(g, _):
            out[g] = pick_rows(ids[g, 0:1, :], table)
            return 0

        lax.fori_loop(0, G, one, 0, unroll=G <= 8)

    def edges(info, *refs):
        g, m = info[0], info[1]
        srcs, mine, other = refs[:M], refs[M : 2 * M], refs[2 * M : 3 * M]
        tgt, total = refs[3 * M : 3 * M + 2]
        outs, (x, we) = refs[3 * M + 2 : 4 * M + 2], refs[4 * M + 2 :]
        width = srcs[0].shape[1]

        @pl.when(pl.program_id(0) == 0)
        def _():
            put_weights(m, mine, other, we, g % 2, we.shape[0] // 2, we.shape[0] // 2, width)

        for r in range(M):
            f = m ^ r
            x[:, lanes(f, width)] = (srcs[r][...].astype(F32) * tgt[0, f].astype(F32)).astype(BF)
        ehid = dot(x[...], we[...])
        x[...] = (total[...] + silu(ehid)).astype(BF)
        for k in range(M):
            outs[k][...] = x[:, lanes(m ^ k, width)]

    def assemble(info, *refs):
        m = info[1]
        parts, out = refs[:M], refs[M]
        for k in range(M):
            for s in range(per):
                out[block_rows(at(m ^ k, s)), :] = parts[k][s * CAP : (s + 1) * CAP, :]

    def local(ef, esrc, etgt, live, partner, mask, basis, af, w_msg, w_down, w_bil, w_up, w_atom, w_edge):
        rows, width = ef.shape
        atoms = af.shape[0]
        depth = w_msg.shape[0]
        dt = w_down.shape[1]
        chunk = per * CAP
        part = atoms // M
        g = lax.axis_index("graph")
        m = lax.axis_index("mp")
        info = jnp.stack([g, m, jnp.int32(atoms)]).astype(jnp.int32)
        w1_rows = depth // 2 + dt // 2
        *chunks, ids, w1, w2 = call(
            prepare,
            [sds((chunk, width))] * M + [sds((G, 1 + G, CAP), jnp.int32), sds((w1_rows, width)), sds((depth, width))],
            info,
            [ef, etgt.reshape(G, CAP), esrc.reshape(G, CAP), w_msg, w_up, w_atom, w_edge],
        )
        xs = [chunks[0]] + [over_mp(chunks[k], k) for k in range(1, M)]
        w1s = [w1] + [over_mp(w1, k) for k in range(1, M)]
        ids = lax.all_to_all(ids, "graph", split_axis=0, concat_axis=0, tiled=True)

        blk = lambda i, info: at(info[1], i)
        x, bil = call(
            triplets,
            [sds((chunk, depth)), sds((chunk, dt))],
            info,
            xs + [partner, mask, basis, w_down.T, w_bil.T],
            scratch=[pltpu.VMEM((NB * dt, CAP), BF)],
            grid=(per,),
            in_specs=[pl.BlockSpec((CAP, width), lambda i, info: (i, 0))] * M
            + [pl.BlockSpec((SLOTS, CAP), lambda i, info: (0, blk(i, info)))] * 2
            + [pl.BlockSpec((CAP, SLOTS * NB), lambda i, info: (blk(i, info), 0)), None, None],
            out_specs=[
                pl.BlockSpec((CAP, depth), lambda i, info: (i, 0)),
                pl.BlockSpec((CAP, dt), lambda i, info: (i, 0)),
            ],
        )
        w1o = [over_plane(w, 1) for w in w1s]
        total, outgoing = call(
            messages,
            [sds((chunk, depth), F32), sds((per, M, CAP, width))],
            info,
            w1s + w1o + [x, bil, live.reshape(G, CAP)],
            scratch=[pltpu.VMEM((depth, depth), BF), pltpu.VMEM((dt, depth), BF)],
            grid=(per,),
            in_specs=[None] * (2 * M)
            + [
                pl.BlockSpec((CAP, depth), lambda i, info: (i, 0)),
                pl.BlockSpec((CAP, dt), lambda i, info: (i, 0)),
                None,
            ],
            out_specs=[
                pl.BlockSpec((CAP, depth), lambda i, info: (i, 0)),
                pl.BlockSpec((1, M, CAP, width), lambda i, info: (i, 0, 0, 0)),
            ],
        )
        incoming = lax.all_to_all(outgoing.reshape(G, CAP, width), "graph", split_axis=0, concat_axis=0, tiled=True)
        af_later, w2_later, _ = lax.optimization_barrier((af, w2, xs[1]))
        af_plane = lax.ppermute(af_later, both, home_to_plane)
        w2s = [w2_later] + [over_mp(w2_later, k) for k in range(1, M)]
        w2o = [over_plane(w, 1) for w in w2s]

        mids = call(aggregate, [sds((part, width))] * M, info, [incoming, ids, af_plane])
        mids = [mids[0]] + [over_plane(mids[r], r) for r in range(1, M)]
        outs = call(
            atom_layer,
            [sds((part, width))] * M,
            info,
            mids + w2s + w2o,
            scratch=[pltpu.VMEM((part, depth), BF), pltpu.VMEM((depth, depth), BF)],
        )
        outs = [outs[0]] + [over_plane(outs[r], r) for r in range(1, M)]
        *srcs, table = call(sources, [sds((chunk, width))] * M + [sds((atoms, width))], info, list(outs) + [ids])
        srcs = [lax.ppermute(srcs[r], both, source_route(r)) for r in range(M)]
        (named,) = call(targets, [sds((G, CAP, width))], info, [table, ids])
        tgt = lax.all_to_all(named, "graph", split_axis=0, concat_axis=0, tiled=True)
        atom_out = lax.ppermute(table, both, plane_to_home)
        outs = call(
            edges,
            [sds((chunk, width))] * M,
            info,
            srcs + w2s + w2o + [tgt.reshape(per, M, CAP, width), total],
            scratch=[pltpu.VMEM((CAP, depth), BF), pltpu.VMEM((depth, depth), BF)],
            grid=(per,),
            in_specs=[pl.BlockSpec((CAP, width), lambda i, info: (i, 0))] * M
            + [None] * (2 * M)
            + [
                pl.BlockSpec((1, M, CAP, width), lambda i, info: (i, 0, 0, 0)),
                pl.BlockSpec((CAP, depth), lambda i, info: (i, 0)),
            ],
            out_specs=[pl.BlockSpec((CAP, width), lambda i, info: (i, 0))] * M,
        )
        outs = [outs[0]] + [over_mp(outs[k], k) for k in range(1, M)]
        (edge_out,) = call(assemble, [sds((rows, width))], info, list(outs))
        return (edge_out, atom_out)

    return jax.shard_map(
        local,
        mesh=mesh,
        in_specs=(
            P("graph", "mp"),
            P("graph"),
            P("graph"),
            P("graph"),
            P(None, "graph"),
            P(None, "graph"),
            P("graph", None),
            P("graph", "mp"),
            P(None, "mp"),
            P(),
            P(),
            P(None, "mp"),
            P(None, "mp"),
            P(None, "mp"),
        ),
        out_specs=(P("graph", "mp"), P("graph", "mp")),
        check_vma=False,
    )
```

time: 236 us -> 162 us (0.69)
  waiting for transfers between devices: 135 us -> 54.3 us
  starting transfers between devices: 12.8 us -> 70.6 us
  matrix products: 29.9 us -> 0 us
  Pallas kernels: 0 us -> 24.5 us
  local copies, waits for them, and re-layouts: 34.2 us -> 9.8 us
  between operations: 13.9 us -> 0.86 us
  other arithmetic: 6.28 us -> 0.08 us
  loops' own time: 2.7 us -> 0 us
    all_gather x3 -> x0, waiting for transfers between devices: 122 us -> none  [the longest x1 42.8 us: local(): lax.all_gather(pair, 'mp', axis=1, tiled=True)]
    ppermute x0 -> x32, starting transfers between devices: none -> 55.5 us  [the longest x12 31.6 us: over_mp(): return lax.ppermute(x, 'mp', [(i, i ^ k) for i in range(M)])]
    ppermute x0 -> x32, waiting for transfers between devices: none -> 46.7 us  [the longest x12 30.2 us: over_mp(): return lax.ppermute(x, 'mp', [(i, i ^ k) for i in range(M)])]
    dot_general x11 -> x0, matrix products: 29.9 us -> none  [the longest x1 9.28 us: local(): jnp.einsum('esb,esa->eba', weights, picked, preferred_element_type=jnp.fl...]
    pallas_call x0 -> x9, Pallas kernels: none -> 24.5 us  [call(): pl.pallas_call(kernel, out_shape=list(out_shapes), grid_spec=pltpu.Prefet...]
    convert_element_type x2 -> x0, local copies, waits for them, and re-layouts: 13.1 us -> none  [the longest x1 9.94 us: local(): jnp.einsum('esb,esa->eba', weights, picked, preferred_element_type=jnp.fl...]
    gather x2 -> x0, local copies, waits for them, and re-layouts: 12.4 us -> none  [the longest x1 6.18 us: local(): source_rows = jnp.take(atom_out, edge_source - shard * atoms_local, axis=0)]
    unnamed x25 -> x35, local copies, waits for them, and re-layouts: 1.3 us -> 9.79 us
  transfers between devices with their start and end apart: 6 -> 35, of which waited for: 5 -> 12; matrix products, arithmetic and copies ran while one was open for 21% -> 0% of each run, Pallas kernels for 0% -> 6%
where the time goes in v1:
time: 162 us; the launch traced here: 160 us
  starting transfers between devices  70.6 us (44%)
  waiting for transfers between devices  54.3 us (34%)
  Pallas kernels  24.5 us (15%)
  local copies, waits for them, and re-layouts  9.8 us (6%)
    ppermute x12, starting transfers between devices, over_mp(): return lax.ppermute(x, 'mp', [(i, i ^ k) for i in range(M)])  31.6 us
    ppermute x12, waiting for transfers between devices, over_mp(): return lax.ppermute(x, 'mp', [(i, i ^ k) for i in range(M)])  30.2 us
    pallas_call x9, Pallas kernels, call(): pl.pallas_call(kernel, out_shape=list(out_shapes), grid_spec=pltpu.Prefet...  24.5 us
    ppermute x4, starting transfers between devices, local(): srcs = [lax.ppermute(srcs[r], both, source_route(r)) for r in range(M)]  15.2 us
    ppermute x14, waiting for transfers between devices, over_plane(): return lax.ppermute(x, 'graph', [(i, i ^ k) for i in range(G)])  12.5 us
    unnamed x35, local copies, waits for them, and re-layouts  9.79 us
    all_to_all x1, starting transfers between devices, local(): ids = lax.all_to_all(ids, 'graph', split_axis=0, concat_axis=0, tiled=True)  6.78 us
    ppermute x14, starting transfers between devices, over_plane(): return lax.ppermute(x, 'graph', [(i, i ^ k) for i in range(G)])  5.49 us
  transfers between devices with their start and end apart: 35, of which 12 were waited for; matrix products, arithmetic and copies ran while one was open for 0% of the time, Pallas kernels for 6%

profile of v1, /device:TPU:0, one launch (start us, length us, event | category | flops | bytes accessed | tf_op | source)
XLA Modules:
  0.0 160.0 jit_solution(3960290349692573184)
XLA Ops:
  5.8 2.2 %shard_map.149 = (bf16[512,128]{1,0:T(8,128)(2,1)S(1)}, bf16[512,128]{1,0:T(8,128)(2,1)S(1)}, bf16[512,128]{1,0:T(8,128)(2,1)S(1)}, bf16[512,128]{1,0:T(8,128)(2...) custom-call(s32[3]{0:T(128)S(1)} %pad_add_fusion.info, ...), custom_call_target="tpu_custom_call" | custom-call | tf_op jit(solution)/shard_map/pallas_call | solution.py:43
  8.0 5.0 %collective-permute-start.2 = (bf16[288,128]{1,0:T(8,128)(2,1)S(1)}, bf16[288,128]{1,0:T(8,128)(2,1)S(1)}, u32[]{:S(2)}, u32[]{:S(2)}) collective-permute-start(bf16[288,128]{1,0:T(8,128)(2,1)S(1)} %get-tuple-element.32.refs_0_), channel_id=1, source_target_pairs={{0,3},{1,2},{2,1},{3,0},{4,7},{5,6},{6,5},{7,4},{8,11},{9,10},{10,... | collective-permute-start | bytes 221192 | tf_op jit(solution)/shard_map/ppermute | solution.py:79
  13.6 3.8 %collective-permute-start.9 = (bf16[512,128]{1,0:T(8,128)(2,1)S(1)}, bf16[512,128]{1,0:T(8,128)(2,1)S(1)}, u32[]{:S(2)}, u32[]{:S(2)}) collective-permute-start(bf16[512,128]{1,0:T(8,128)(2,1)S(1)} %get-tuple-element.36), channel_id=1, source_target_pairs={{0,3},{1,2},{2,1},{3,0},{4,7},{5,6},{6,5},{7,4},{8,11},{9,10},{10,... | collective-permute-start | bytes 393224 | tf_op jit(solution)/shard_map/ppermute | solution.py:79
  18.0 12.6 %collective-permute-done.1.refs_2_ = bf16[288,128]{1,0:T(8,128)(2,1)S(1)} collective-permute-done((bf16[288,128]{1,0:T(8,128)(2,1)S(1)}, bf16[288,128]{1,0:T(8,128)(2,1)S(1)}, u32[]{:S(2)}, u32[]{:S(2)}) %collective-permute-start.1) | collective-permute-done | bytes 73760 | tf_op jit(solution)/shard_map/ppermute | solution.py:79
  31.6 1.7 %collective-permute-start.10 = (bf16[2048,128]{1,0:T(8,128)(2,1)}, bf16[2048,128]{1,0:T(8,128)(2,1)S(1)}, u32[]{:S(2)}, u32[]{:S(2)}) collective-permute-start(bf16[2048,128]{1,0:T(8,128)(2,1)} %param.21), channel_id=1, source_target_pairs={{0,0},{1,4},{2,8},{3,12},{20,16},{21,20},{22,24},{23,28},{8,1},{9,... | collective-permute-start | bytes 1572872 | tf_op jit(solution)/shard_map/ppermute | solution.py:301
  33.3 6.8 %all-to-all-start.1 = ((s32[8,9,256]{2,1,0:T(8,128)}), s32[8,9,256]{2,1,0:T(8,128)S(1)}, u32[]{:S(2)}, u32[]{:S(2)}) async-start(s32[8,9,256]{2,1,0:T(8,128)} %get-tuple-element.40), calls=%async_computation.1 | async-start | bytes 262144 | tf_op jit(solution)/shard_map/all_to_all | solution.py:262
  40.2 3.1 %shard_map.150 = (bf16[512,512]{1,0:T(8,128)(2,1)S(1)}, bf16[512,64]{1,0:T(8,128)(2,1)S(1)}) custom-call(s32[3]{0:T(128)S(1)} %pad_add_fusion.info, bf16[512,128]{1,0:T(8,128)(2,1)S(1)} %get-tuple-element.33.refs_0_, bf16[512,128]{1,0:T(8,128)(2,1)S(1)} %collective-permute-done.7.refs_1_, bf16[512,128]{1,0:T(8,128)(2,1)S(1)} %collective-permute-done.8.refs_2_, ...), custom_call_target="tpu_custom_call" | custom-call | tf_op jit(solution)/shard_map/pallas_call | solution.py:43
  43.3 2.4 %shard_map.151 = (f32[512,512]{1,0:T(8,128)S(1)}, bf16[2,4,256,128]{3,2,1,0:T(8,128)(2,1)}) custom-call(s32[3]{0:T(128)S(1)} %pad_add_fusion.info, bf16[288,128]{1,0:T(8,128)(2,1)S(1)} %get-tuple-element.32.refs_0_, bf16[288,128]{1,0:T(8,128)(2,1)S(1)} %collective-permute-done.refs_1_, bf16[288,128]{1,0:T(8,128)(2,1)S(1)} %collective-permute-done.1.refs_2_, ...), custom_call_target="tpu_custom_call" | custom-call | tf_op jit(solution)/shard_map/pallas_call | solution.py:43
  45.7 5.2 %all-to-all-done.1.ids.refs_4_ = s32[8,9,256]{2,1,0:T(8,128)S(1)} async-done(((s32[8,9,256]{2,1,0:T(8,128)}), s32[8,9,256]{2,1,0:T(8,128)S(1)}, u32[]{:S(2)}, u32[]{:S(2)}) %all-to-all-start.1) | async-done | bytes 73760 | tf_op jit(solution)/shard_map/all_to_all | solution.py:262
  51.0 4.3 %all-to-all-start = ((bf16[8,256,128]{2,1,0:T(8,128)(2,1)}), bf16[8,256,128]{2,1,0:T(8,128)(2,1)S(1)}, u32[]{:S(2)}, u32[]{:S(2)}) async-start(bf16[8,256,128]{2,1,0:T(8,128)(2,1)} %bitcast.4), calls=%async_computation | async-start | bytes 1048576 | tf_op jit(solution)/shard_map/all_to_all | solution.py:299
  55.3 3.6 %collective-permute-start.16 = (bf16[512,128]{1,0:T(8,128)(2,1)S(1)}, bf16[512,128]{1,0:T(8,128)(2,1)S(1)}, u32[]{:S(2)}, u32[]{:S(2)}) collective-permute-start(bf16[512,128]{1,0:T(8,128)(2,1)S(1)} %get-tuple-element.47.refs_4_), channel_id=1, source_target_pairs={{0,3},{1,2},{2,1},{3,0},{4,7},{5,6},{6,5},{7,4},{8,11},{9,10},{10,... | collective-permute-start | bytes 393224 | tf_op jit(solution)/shard_map/ppermute | solution.py:79
  59.7 3.8 %collective-permute-done.16.refs_7_ = bf16[512,128]{1,0:T(8,128)(2,1)S(1)} collective-permute-done((bf16[512,128]{1,0:T(8,128)(2,1)S(1)}, bf16[512,128]{1,0:T(8,128)(2,1)S(1)}, u32[]{:S(2)}, u32[]{:S(2)}) %collective-permute-start.16) | collective-permute-done | bytes 131104 | tf_op jit(solution)/shard_map/ppermute | solution.py:79
  63.5 5.1 %collective-permute-done.15.refs_6_ = bf16[512,128]{1,0:T(8,128)(2,1)S(1)} collective-permute-done((bf16[512,128]{1,0:T(8,128)(2,1)S(1)}, bf16[512,128]{1,0:T(8,128)(2,1)S(1)}, u32[]{:S(2)}, u32[]{:S(2)}) %collective-permute-start.15) | collective-permute-done | bytes 131104 | tf_op jit(solution)/shard_map/ppermute | solution.py:79
  69.1 2.9 %shard_map.152 = (bf16[512,128]{1,0:T(8,128)(2,1)S(1)}, bf16[512,128]{1,0:T(8,128)(2,1)S(1)}, bf16[512,128]{1,0:T(8,128)(2,1)S(1)}, bf16[512,128]{1,0:T(8,128)(2,1)S(1)}) custom-call(s32[3]{0:T(128)S(1)} %pad_add_fusion.info, bf16[8,256,128]{2,1,0:T(8,128)(2,1)S(1)} %all-to-all-done.incoming, s32[8,9,256]{2,1,0:T(8,128)S(1)} %all-to-all-done.1.ids.refs_4_, ...), custom_call_target="tpu_custom_call" | custom-call | tf_op jit(solution)/shard_map/pallas_call | solution.py:43
  72.1 1.7 %collective-permute-start.12 = (bf16[512,128]{1,0:T(8,128)(2,1)S(1)}, bf16[512,128]{1,0:T(8,128)(2,1)S(1)}, u32[]{:S(2)}, u32[]{:S(2)}) collective-permute-start(bf16[512,128]{1,0:T(8,128)(2,1)S(1)} %get-tuple-element.45), channel_id=1, source_target_pairs={{0,8},{4,12},{8,0},{12,4},{16,24},{20,28},{24,16},{28,20},{1,9},{5... | collective-permute-start | bytes 393224 | tf_op jit(solution)/shard_map/ppermute | solution.py:82
  74.0 4.5 %collective-permute-done.12.refs_2_ = bf16[512,128]{1,0:T(8,128)(2,1)S(1)} collective-permute-done((bf16[512,128]{1,0:T(8,128)(2,1)S(1)}, bf16[512,128]{1,0:T(8,128)(2,1)S(1)}, u32[]{:S(2)}, u32[]{:S(2)}) %collective-permute-start.12) | collective-permute-done | bytes 131104 | tf_op jit(solution)/shard_map/ppermute | solution.py:82
  78.5 1.9 %collective-permute-done.13.refs_3_ = bf16[512,128]{1,0:T(8,128)(2,1)S(1)} collective-permute-done((bf16[512,128]{1,0:T(8,128)(2,1)S(1)}, bf16[512,128]{1,0:T(8,128)(2,1)S(1)}, u32[]{:S(2)}, u32[]{:S(2)}) %collective-permute-start.13) | collective-permute-done | bytes 131104 | tf_op jit(solution)/shard_map/ppermute | solution.py:82
  83.8 4.7 %collective-permute-done.22.refs_2_ = bf16[512,128]{1,0:T(8,128)(2,1)S(1)} collective-permute-done((bf16[512,128]{1,0:T(8,128)(2,1)S(1)}, bf16[512,128]{1,0:T(8,128)(2,1)S(1)}, u32[]{:S(2)}, u32[]{:S(2)}) %collective-permute-start.22) | collective-permute-done | bytes 131104 | tf_op jit(solution)/shard_map/ppermute | solution.py:82
  89.8 4.5 %shard_map.154 = (bf16[512,128]{1,0:T(8,128)(2,1)}, bf16[512,128]{1,0:T(8,128)(2,1)}, bf16[512,128]{1,0:T(8,128)(2,1)S(1)}, bf16[512,128]{1,0:T(8,128)(2,1)S(1)}, bf16[2048,128]{1,0:T(8,128)(2,1)S(1)}) custom-call(s32[3]{0:T(128)S(1)} %pad_add_fusion.info, bf16[512,128]{1,0:T(8,128)(2,1)S(1)} %get-tuple-element.48.refs_0_, ...), custom_call_target="tpu_custom_call" | custom-call | tf_op jit(solution)/shard_map/pallas_call | solution.py:43
  95.7 4.8 %shard_map.155 = bf16[8,256,128]{2,1,0:T(8,128)(2,1)} custom-call(s32[3]{0:T(128)S(1)} %pad_add_fusion.info, bf16[2048,128]{1,0:T(8,128)(2,1)S(1)} %get-tuple-element.56.table, s32[8,9,256]{2,1,0:T(8,128)S(1)} %all-to-all-done.1.ids.refs_4_), custom_call_target="tpu_custom_call" | custom-call | tf_op jit(solution)/shard_map/pallas_call | solution.py:43
  100.5 4.0 %all-to-all-start.2 = ((bf16[8,256,128]{2,1,0:T(8,128)(2,1)}), bf16[8,256,128]{2,1,0:T(8,128)(2,1)S(1)}, u32[]{:S(2)}, u32[]{:S(2)}) async-start(bf16[8,256,128]{2,1,0:T(8,128)(2,1)} %shard_map.155), calls=%async_computation.2 | async-start | bytes 1048576 | tf_op jit(solution)/shard_map/all_to_all | solution.py:318
  107.5 6.2 %collective-permute-start.25 = (bf16[512,128]{1,0:T(8,128)(2,1)}, bf16[512,128]{1,0:T(8,128)(2,1)S(1)}, u32[]{:S(2)}, u32[]{:S(2)}) collective-permute-start(bf16[512,128]{1,0:T(8,128)(2,1)} %get-tuple-element.53), channel_id=1, source_target_pairs={{0,1},{4,0},{8,3},{12,2},{16,21},{20,20},{24,23},{28,22},{1,9},{5,... | collective-permute-start | bytes 393224 | tf_op jit(solution)/shard_map/ppermute | solution.py:316
  113.7 2.6 %collective-permute-start.26 = (bf16[512,128]{1,0:T(8,128)(2,1)}, bf16[512,128]{1,0:T(8,128)(2,1)S(1)}, u32[]{:S(2)}, u32[]{:S(2)}) collective-permute-start(bf16[512,128]{1,0:T(8,128)(2,1)} %copy-done.13), channel_id=1, source_target_pairs={{0,2},{4,3},{8,0},{12,1},{16,22},{20,23},{24,20},{28,21},{1,10},{5... | collective-permute-start | bytes 393224 | tf_op jit(solution)/shard_map/ppermute | solution.py:316
  116.4 4.8 %collective-permute-start.27 = (bf16[512,128]{1,0:T(8,128)(2,1)}, bf16[512,128]{1,0:T(8,128)(2,1)S(1)}, u32[]{:S(2)}, u32[]{:S(2)}) collective-permute-start(bf16[512,128]{1,0:T(8,128)(2,1)} %copy-done.12), channel_id=1, source_target_pairs={{0,3},{4,2},{8,1},{12,0},{16,23},{20,22},{24,21},{28,20},{1,11},{5... | collective-permute-start | bytes 393224 | tf_op jit(solution)/shard_map/ppermute | solution.py:316
  121.2 4.1 %collective-permute-done.26.refs_2_ = bf16[512,128]{1,0:T(8,128)(2,1)S(1)} collective-permute-done((bf16[512,128]{1,0:T(8,128)(2,1)}, bf16[512,128]{1,0:T(8,128)(2,1)S(1)}, u32[]{:S(2)}, u32[]{:S(2)}) %collective-permute-start.26) | collective-permute-done | bytes 131104 | tf_op jit(solution)/shard_map/ppermute | solution.py:316
  126.0 2.3 %all-to-all-done.2 = bf16[8,256,128]{2,1,0:T(8,128)(2,1)S(1)} async-done(((bf16[8,256,128]{2,1,0:T(8,128)(2,1)}), bf16[8,256,128]{2,1,0:T(8,128)(2,1)S(1)}, u32[]{:S(2)}, u32[]{:S(2)}) %all-to-all-start.2) | async-done | bytes 524320 | tf_op jit(solution)/shard_map/all_to_all | solution.py:318
  129.2 1.7 %shard_map.156 = (bf16[512,128]{1,0:T(8,128)(2,1)S(1)}, bf16[512,128]{1,0:T(8,128)(2,1)S(1)}, bf16[512,128]{1,0:T(8,128)(2,1)S(1)}, bf16[512,128]{1,0:T(8,128)(2,1)S(1)}) custom-call(s32[3]{0:T(128)S(1)} %pad_add_fusion.info, bf16[512,128]{1,0:T(8,128)(2,1)S(1)} %collective-permute-done.24.refs_0_, bf16[512,128]{1,0:T(8,128)(2,1)S(1)} %collective-permute-done.25.refs_1_, ...), custom_call_target="tpu_custom_call" | custom-call | tf_op jit(solution)/shard_map/pallas_call | solution.py:43
  130.9 4.6 %collective-permute-start.28 = (bf16[512,128]{1,0:T(8,128)(2,1)S(1)}, bf16[512,128]{1,0:T(8,128)(2,1)S(1)}, u32[]{:S(2)}, u32[]{:S(2)}) collective-permute-start(bf16[512,128]{1,0:T(8,128)(2,1)S(1)} %get-tuple-element.59), channel_id=1, source_target_pairs={{0,1},{1,0},{2,3},{3,2},{4,5},{5,4},{6,7},{7,6},{8,9},{9,8},{10,11... | collective-permute-start | bytes 393224 | tf_op jit(solution)/shard_map/ppermute | solution.py:79
  135.5 11.2 %collective-permute-start.29 = (bf16[512,128]{1,0:T(8,128)(2,1)S(1)}, bf16[512,128]{1,0:T(8,128)(2,1)S(1)}, u32[]{:S(2)}, u32[]{:S(2)}) collective-permute-start(bf16[512,128]{1,0:T(8,128)(2,1)S(1)} %get-tuple-element.60), channel_id=1, source_target_pairs={{0,2},{1,3},{2,0},{3,1},{4,6},{5,7},{6,4},{7,5},{8,10},{9,11},{10,... | collective-permute-start | bytes 393224 | tf_op jit(solution)/shard_map/ppermute | solution.py:79
  148.1 2.5 %collective-permute-done.29.refs_2_ = bf16[512,128]{1,0:T(8,128)(2,1)S(1)} collective-permute-done((bf16[512,128]{1,0:T(8,128)(2,1)S(1)}, bf16[512,128]{1,0:T(8,128)(2,1)S(1)}, u32[]{:S(2)}, u32[]{:S(2)}) %collective-permute-start.29) | collective-permute-done | bytes 131104 | tf_op jit(solution)/shard_map/ppermute | solution.py:79
  150.6 6.2 %collective-permute-done.30.refs_3_ = bf16[512,128]{1,0:T(8,128)(2,1)S(1)} collective-permute-done((bf16[512,128]{1,0:T(8,128)(2,1)S(1)}, bf16[512,128]{1,0:T(8,128)(2,1)S(1)}, u32[]{:S(2)}, u32[]{:S(2)}) %collective-permute-start.30) | collective-permute-done | bytes 131104 | tf_op jit(solution)/shard_map/ppermute | solution.py:79
  158.2 1.9 %copy.17 = bf16[2048,128]{1,0:T(8,128)(2,1)} copy(bf16[2048,128]{1,0:T(8,128)(2,1)} %collective-permute-done.31) | data formatting | bytes 1048576
  (86 shorter events, 22.3 us)
Async XLA Ops:
  8.0 9.4 %collective-permute-start.2 = (bf16[288,128]{1,0:T(8,128)(2,1)S(1)}, bf16[288,128]{1,0:T(8,128)(2,1)S(1)}, u32[]{:S(2)}, u32[]{:S(2)}) collective-permute-start(bf16[288,128]{1,0:T(8,128)(2,1)S(1)} %get-tuple-element.32.refs_0_), channel_id=1, source_target_pairs={{0,3},{1,2},{2,1},{3,0},{4,7},{5,6},{6,5},{7,4},{8,11},{9,10},{10,... | collective-permute-start | bytes 221192 | tf_op jit(solution)/shard_map/ppermute | solution.py:79
  13.0 18.1 %collective-permute-start.7 = (bf16[512,128]{1,0:T(8,128)(2,1)S(1)}, bf16[512,128]{1,0:T(8,128)(2,1)S(1)}, u32[]{:S(2)}, u32[]{:S(2)}) collective-permute-start(bf16[512,128]{1,0:T(8,128)(2,1)S(1)} %get-tuple-element.34), channel_id=1, source_target_pairs={{0,1},{1,0},{2,3},{3,2},{4,5},{5,4},{6,7},{7,6},{8,9},{9,8},{10,11... | collective-permute-start | bytes 393224 | tf_op jit(solution)/shard_map/ppermute | solution.py:79
  13.0 18.1 %collective-permute-start.8 = (bf16[512,128]{1,0:T(8,128)(2,1)S(1)}, bf16[512,128]{1,0:T(8,128)(2,1)S(1)}, u32[]{:S(2)}, u32[]{:S(2)}) collective-permute-start(bf16[512,128]{1,0:T(8,128)(2,1)S(1)} %get-tuple-element.35), channel_id=1, source_target_pairs={{0,2},{1,3},{2,0},{3,1},{4,6},{5,7},{6,4},{7,5},{8,10},{9,11},{10,... | collective-permute-start | bytes 393224 | tf_op jit(solution)/shard_map/ppermute | solution.py:79
  13.6 18.0 %collective-permute-start.9 = (bf16[512,128]{1,0:T(8,128)(2,1)S(1)}, bf16[512,128]{1,0:T(8,128)(2,1)S(1)}, u32[]{:S(2)}, u32[]{:S(2)}) collective-permute-start(bf16[512,128]{1,0:T(8,128)(2,1)S(1)} %get-tuple-element.36), channel_id=1, source_target_pairs={{0,3},{1,2},{2,1},{3,0},{4,7},{5,6},{6,5},{7,4},{8,11},{9,10},{10,... | collective-permute-start | bytes 393224 | tf_op jit(solution)/shard_map/ppermute | solution.py:79
  17.4 13.2 %collective-permute-start.1 = (bf16[288,128]{1,0:T(8,128)(2,1)S(1)}, bf16[288,128]{1,0:T(8,128)(2,1)S(1)}, u32[]{:S(2)}, u32[]{:S(2)}) collective-permute-start(bf16[288,128]{1,0:T(8,128)(2,1)S(1)} %get-tuple-element.32.refs_0_), channel_id=1, source_target_pairs={{0,2},{1,3},{2,0},{3,1},{4,6},{5,7},{6,4},{7,5},{8,10},{9,11},{10,... | collective-permute-start | bytes 221192 | tf_op jit(solution)/shard_map/ppermute | solution.py:79
  17.4 13.2 %collective-permute-start = (bf16[288,128]{1,0:T(8,128)(2,1)S(1)}, bf16[288,128]{1,0:T(8,128)(2,1)S(1)}, u32[]{:S(2)}, u32[]{:S(2)}) collective-permute-start(bf16[288,128]{1,0:T(8,128)(2,1)S(1)} %get-tuple-element.32.refs_0_), channel_id=1, source_target_pairs={{0,1},{1,0},{2,3},{3,2},{4,5},{5,4},{6,7},{7,6},{8,9},{9,8},{10,11... | collective-permute-start | bytes 221192 | tf_op jit(solution)/shard_map/ppermute | solution.py:79
  30.6 12.7 %collective-permute-start.3 = (bf16[288,128]{1,0:T(8,128)(2,1)S(1)}, bf16[288,128]{1,0:T(8,128)(2,1)S(1)}, u32[]{:S(2)}, u32[]{:S(2)}) collective-permute-start(bf16[288,128]{1,0:T(8,128)(2,1)S(1)} %get-tuple-element.32.refs_0_), channel_id=1, source_target_pairs={{0,4},{4,0},{8,12},{12,8},{16,20},{20,16},{24,28},{28,24},{1,5},{5... | collective-permute-start | bytes 221192 | tf_op jit(solution)/shard_map/ppermute | solution.py:82
  30.6 12.7 %collective-permute-start.6 = (bf16[288,128]{1,0:T(8,128)(2,1)S(1)}, bf16[288,128]{1,0:T(8,128)(2,1)S(1)}, u32[]{:S(2)}, u32[]{:S(2)}) collective-permute-start(bf16[288,128]{1,0:T(8,128)(2,1)S(1)} %collective-permute-done.2.refs_3_), channel_id=1, source_target_pairs={{0,4},{4,0},{8,12},{12,8},{16,20},{20,16},{24,28},{28,24},{1,5},{5... | collective-permute-start | bytes 221192 | tf_op jit(solution)/shard_map/ppermute | solution.py:82
  31.1 12.2 %collective-permute-start.5 = (bf16[288,128]{1,0:T(8,128)(2,1)S(1)}, bf16[288,128]{1,0:T(8,128)(2,1)S(1)}, u32[]{:S(2)}, u32[]{:S(2)}) collective-permute-start(bf16[288,128]{1,0:T(8,128)(2,1)S(1)} %collective-permute-done.1.refs_2_), channel_id=1, source_target_pairs={{0,4},{4,0},{8,12},{12,8},{16,20},{20,16},{24,28},{28,24},{1,5},{5... | collective-permute-start | bytes 221192 | tf_op jit(solution)/shard_map/ppermute | solution.py:82
  31.2 12.1 %collective-permute-start.4 = (bf16[288,128]{1,0:T(8,128)(2,1)S(1)}, bf16[288,128]{1,0:T(8,128)(2,1)S(1)}, u32[]{:S(2)}, u32[]{:S(2)}) collective-permute-start(bf16[288,128]{1,0:T(8,128)(2,1)S(1)} %collective-permute-done.refs_1_), channel_id=1, source_target_pairs={{0,4},{4,0},{8,12},{12,8},{16,20},{20,16},{24,28},{28,24},{1,5},{5... | collective-permute-start | bytes 221192 | tf_op jit(solution)/shard_map/ppermute | solution.py:82
  31.6 37.5 %collective-permute-start.10 = (bf16[2048,128]{1,0:T(8,128)(2,1)}, bf16[2048,128]{1,0:T(8,128)(2,1)S(1)}, u32[]{:S(2)}, u32[]{:S(2)}) collective-permute-start(bf16[2048,128]{1,0:T(8,128)(2,1)} %param.21), channel_id=1, source_target_pairs={{0,0},{1,4},{2,8},{3,12},{20,16},{21,20},{22,24},{23,28},{8,1},{9,... | collective-permute-start | bytes 1572872 | tf_op jit(solution)/shard_map/ppermute | solution.py:301
  33.3 17.7 %all-to-all-start.1 = ((s32[8,9,256]{2,1,0:T(8,128)}), s32[8,9,256]{2,1,0:T(8,128)S(1)}, u32[]{:S(2)}, u32[]{:S(2)}) async-start(s32[8,9,256]{2,1,0:T(8,128)} %get-tuple-element.40), calls=%async_computation.1 | async-start | bytes 262144 | tf_op jit(solution)/shard_map/all_to_all | solution.py:262
  51.0 18.1 %all-to-all-start = ((bf16[8,256,128]{2,1,0:T(8,128)(2,1)}), bf16[8,256,128]{2,1,0:T(8,128)(2,1)S(1)}, u32[]{:S(2)}, u32[]{:S(2)}) async-start(bf16[8,256,128]{2,1,0:T(8,128)(2,1)} %bitcast.4), calls=%async_computation | async-start | bytes 1048576 | tf_op jit(solution)/shard_map/all_to_all | solution.py:299
  55.3 8.2 %collective-permute-start.16 = (bf16[512,128]{1,0:T(8,128)(2,1)S(1)}, bf16[512,128]{1,0:T(8,128)(2,1)S(1)}, u32[]{:S(2)}, u32[]{:S(2)}) collective-permute-start(bf16[512,128]{1,0:T(8,128)(2,1)S(1)} %get-tuple-element.47.refs_4_), channel_id=1, source_target_pairs={{0,3},{1,2},{2,1},{3,0},{4,7},{5,6},{6,5},{7,4},{8,11},{9,10},{10,... | collective-permute-start | bytes 393224 | tf_op jit(solution)/shard_map/ppermute | solution.py:79
  58.9 9.7 %collective-permute-start.15 = (bf16[512,128]{1,0:T(8,128)(2,1)S(1)}, bf16[512,128]{1,0:T(8,128)(2,1)S(1)}, u32[]{:S(2)}, u32[]{:S(2)}) collective-permute-start(bf16[512,128]{1,0:T(8,128)(2,1)S(1)} %get-tuple-element.47.refs_4_), channel_id=1, source_target_pairs={{0,2},{1,3},{2,0},{3,1},{4,6},{5,7},{6,4},{7,5},{8,10},{9,11},{10,... | collective-permute-start | bytes 393224 | tf_op jit(solution)/shard_map/ppermute | solution.py:79
  58.9 9.7 %collective-permute-start.14 = (bf16[512,128]{1,0:T(8,128)(2,1)S(1)}, bf16[512,128]{1,0:T(8,128)(2,1)S(1)}, u32[]{:S(2)}, u32[]{:S(2)}) collective-permute-start(bf16[512,128]{1,0:T(8,128)(2,1)S(1)} %get-tuple-element.47.refs_4_), channel_id=1, source_target_pairs={{0,1},{1,0},{2,3},{3,2},{4,5},{5,4},{6,7},{7,6},{8,9},{9,8},{10,11... | collective-permute-start | bytes 393224 | tf_op jit(solution)/shard_map/ppermute | solution.py:79
  59.7 12.4 %collective-permute-start.17 = (bf16[512,128]{1,0:T(8,128)(2,1)S(1)}, bf16[512,128]{1,0:T(8,128)(2,1)S(1)}, u32[]{:S(2)}, u32[]{:S(2)}) collective-permute-start(bf16[512,128]{1,0:T(8,128)(2,1)S(1)} %get-tuple-element.47.refs_4_), channel_id=1, source_target_pairs={{0,4},{4,0},{8,12},{12,8},{16,20},{20,16},{24,28},{28,24},{1,5},{5... | collective-permute-start | bytes 393224 | tf_op jit(solution)/shard_map/ppermute | solution.py:82
  63.5 10.4 %collective-permute-start.20 = (bf16[512,128]{1,0:T(8,128)(2,1)S(1)}, bf16[512,128]{1,0:T(8,128)(2,1)S(1)}, u32[]{:S(2)}, u32[]{:S(2)}) collective-permute-start(bf16[512,128]{1,0:T(8,128)(2,1)S(1)} %collective-permute-done.16.refs_7_), channel_id=1, source_target_pairs={{0,4},{4,0},{8,12},{12,8},{16,20},{20,16},{24,28},{28,24},{1,5},{5... | collective-permute-start | bytes 393224 | tf_op jit(solution)/shard_map/ppermute | solution.py:82
  68.6 5.4 %collective-permute-start.19 = (bf16[512,128]{1,0:T(8,128)(2,1)S(1)}, bf16[512,128]{1,0:T(8,128)(2,1)S(1)}, u32[]{:S(2)}, u32[]{:S(2)}) collective-permute-start(bf16[512,128]{1,0:T(8,128)(2,1)S(1)} %collective-permute-done.15.refs_6_), channel_id=1, source_target_pairs={{0,4},{4,0},{8,12},{12,8},{16,20},{20,16},{24,28},{28,24},{1,5},{5... | collective-permute-start | bytes 393224 | tf_op jit(solution)/shard_map/ppermute | solution.py:82
  72.1 6.4 %collective-permute-start.12 = (bf16[512,128]{1,0:T(8,128)(2,1)S(1)}, bf16[512,128]{1,0:T(8,128)(2,1)S(1)}, u32[]{:S(2)}, u32[]{:S(2)}) collective-permute-start(bf16[512,128]{1,0:T(8,128)(2,1)S(1)} %get-tuple-element.45), channel_id=1, source_target_pairs={{0,8},{4,12},{8,0},{12,4},{16,24},{20,28},{24,16},{28,20},{1,9},{5... | collective-permute-start | bytes 393224 | tf_op jit(solution)/shard_map/ppermute | solution.py:82
  73.8 6.5 %collective-permute-start.13 = (bf16[512,128]{1,0:T(8,128)(2,1)S(1)}, bf16[512,128]{1,0:T(8,128)(2,1)S(1)}, u32[]{:S(2)}, u32[]{:S(2)}) collective-permute-start(bf16[512,128]{1,0:T(8,128)(2,1)S(1)} %get-tuple-element.46), channel_id=1, source_target_pairs={{0,12},{4,8},{8,4},{12,0},{16,28},{20,24},{24,20},{28,16},{1,13},{... | collective-permute-start | bytes 393224 | tf_op jit(solution)/shard_map/ppermute | solution.py:82
  82.1 6.3 %collective-permute-start.22 = (bf16[512,128]{1,0:T(8,128)(2,1)S(1)}, bf16[512,128]{1,0:T(8,128)(2,1)S(1)}, u32[]{:S(2)}, u32[]{:S(2)}) collective-permute-start(bf16[512,128]{1,0:T(8,128)(2,1)S(1)} %get-tuple-element.50), channel_id=1, source_target_pairs={{0,8},{4,12},{8,0},{12,4},{16,24},{20,28},{24,16},{28,20},{1,9},{5... | collective-permute-start | bytes 393224 | tf_op jit(solution)/shard_map/ppermute | solution.py:82
  83.8 6.1 %collective-permute-start.23 = (bf16[512,128]{1,0:T(8,128)(2,1)S(1)}, bf16[512,128]{1,0:T(8,128)(2,1)S(1)}, u32[]{:S(2)}, u32[]{:S(2)}) collective-permute-start(bf16[512,128]{1,0:T(8,128)(2,1)S(1)} %get-tuple-element.51), channel_id=1, source_target_pairs={{0,12},{4,8},{8,4},{12,0},{16,28},{20,24},{24,20},{28,16},{1,13},{... | collective-permute-start | bytes 393224 | tf_op jit(solution)/shard_map/ppermute | solution.py:82
  100.5 27.8 %all-to-all-start.2 = ((bf16[8,256,128]{2,1,0:T(8,128)(2,1)}), bf16[8,256,128]{2,1,0:T(8,128)(2,1)S(1)}, u32[]{:S(2)}, u32[]{:S(2)}) async-start(bf16[8,256,128]{2,1,0:T(8,128)(2,1)} %shard_map.155), calls=%async_computation.2 | async-start | bytes 1048576 | tf_op jit(solution)/shard_map/all_to_all | solution.py:318
  104.5 43.6 %collective-permute-start.31 = (bf16[2048,128]{1,0:T(8,128)(2,1)S(1)}, bf16[2048,128]{1,0:T(8,128)(2,1)}, u32[]{:S(2)}, u32[]{:S(2)}) collective-permute-start(bf16[2048,128]{1,0:T(8,128)(2,1)S(1)} %get-tuple-element.56.table), channel_id=1, source_target_pairs={{0,0},{4,1},{8,2},{12,3},{16,20},{20,21},{24,22},{28,23},{1,8},{5,... | collective-permute-start | bytes 1572872 | tf_op jit(solution)/shard_map/ppermute | solution.py:319
  106.0 15.3 %collective-permute-start.24 = (bf16[512,128]{1,0:T(8,128)(2,1)}, bf16[512,128]{1,0:T(8,128)(2,1)S(1)}, u32[]{:S(2)}, u32[]{:S(2)}) collective-permute-start(bf16[512,128]{1,0:T(8,128)(2,1)} %get-tuple-element.52), channel_id=1, source_target_pairs={{0,0},{4,1},{8,2},{12,3},{16,20},{20,21},{24,22},{28,23},{1,8},{5,... | collective-permute-start | bytes 393224 | tf_op jit(solution)/shard_map/ppermute | solution.py:316
  107.5 13.7 %collective-permute-start.25 = (bf16[512,128]{1,0:T(8,128)(2,1)}, bf16[512,128]{1,0:T(8,128)(2,1)S(1)}, u32[]{:S(2)}, u32[]{:S(2)}) collective-permute-start(bf16[512,128]{1,0:T(8,128)(2,1)} %get-tuple-element.53), channel_id=1, source_target_pairs={{0,1},{4,0},{8,3},{12,2},{16,21},{20,20},{24,23},{28,22},{1,9},{5,... | collective-permute-start | bytes 393224 | tf_op jit(solution)/shard_map/ppermute | solution.py:316
  113.7 11.6 %collective-permute-start.26 = (bf16[512,128]{1,0:T(8,128)(2,1)}, bf16[512,128]{1,0:T(8,128)(2,1)S(1)}, u32[]{:S(2)}, u32[]{:S(2)}) collective-permute-start(bf16[512,128]{1,0:T(8,128)(2,1)} %copy-done.13), channel_id=1, source_target_pairs={{0,2},{4,3},{8,0},{12,1},{16,22},{20,23},{24,20},{28,21},{1,10},{5... | collective-permute-start | bytes 393224 | tf_op jit(solution)/shard_map/ppermute | solution.py:316
  116.4 9.0 %collective-permute-start.27 = (bf16[512,128]{1,0:T(8,128)(2,1)}, bf16[512,128]{1,0:T(8,128)(2,1)S(1)}, u32[]{:S(2)}, u32[]{:S(2)}) collective-permute-start(bf16[512,128]{1,0:T(8,128)(2,1)} %copy-done.12), channel_id=1, source_target_pairs={{0,3},{4,2},{8,1},{12,0},{16,23},{20,22},{24,21},{28,20},{1,11},{5... | collective-permute-start | bytes 393224 | tf_op jit(solution)/shard_map/ppermute | solution.py:316
  130.9 17.3 %collective-permute-start.28 = (bf16[512,128]{1,0:T(8,128)(2,1)S(1)}, bf16[512,128]{1,0:T(8,128)(2,1)S(1)}, u32[]{:S(2)}, u32[]{:S(2)}) collective-permute-start(bf16[512,128]{1,0:T(8,128)(2,1)S(1)} %get-tuple-element.59), channel_id=1, source_target_pairs={{0,1},{1,0},{2,3},{3,2},{4,5},{5,4},{6,7},{7,6},{8,9},{9,8},{10,11... | collective-permute-start | bytes 393224 | tf_op jit(solution)/shard_map/ppermute | solution.py:79
  135.5 15.1 %collective-permute-start.29 = (bf16[512,128]{1,0:T(8,128)(2,1)S(1)}, bf16[512,128]{1,0:T(8,128)(2,1)S(1)}, u32[]{:S(2)}, u32[]{:S(2)}) collective-permute-start(bf16[512,128]{1,0:T(8,128)(2,1)S(1)} %get-tuple-element.60), channel_id=1, source_target_pairs={{0,2},{1,3},{2,0},{3,1},{4,6},{5,7},{6,4},{7,5},{8,10},{9,11},{10,... | collective-permute-start | bytes 393224 | tf_op jit(solution)/shard_map/ppermute | solution.py:79
  146.7 10.0 %collective-permute-start.30 = (bf16[512,128]{1,0:T(8,128)(2,1)S(1)}, bf16[512,128]{1,0:T(8,128)(2,1)S(1)}, u32[]{:S(2)}, u32[]{:S(2)}) collective-permute-start(bf16[512,128]{1,0:T(8,128)(2,1)S(1)} %get-tuple-element.61), channel_id=1, source_target_pairs={{0,3},{1,2},{2,1},{3,0},{4,7},{5,6},{6,5},{7,4},{8,11},{9,10},{10,... | collective-permute-start | bytes 393224 | tf_op jit(solution)/shard_map/ppermute | solution.py:79
  (20 other events, 141.5 us)

commit v2 on v1

--- a/solution.py
+++ b/solution.py
@@ -10,6 +10,7 @@
 NB = 16
 SLOTS = 8
 CAP = 256
+LANES = 128
 BF = jnp.bfloat16
 F32 = jnp.float32
 VMEM_LIMIT = 40 * 1024 * 1024
@@ -47,7 +48,7 @@
             num_scalar_prefetch=1, grid=grid, in_specs=in_specs, out_specs=out_specs, scratch_shapes=list(scratch)
         ),
         compiler_params=pltpu.CompilerParams(vmem_limit_bytes=VMEM_LIMIT),
-        cost_estimate=pl.CostEstimate(flops=flops, bytes_accessed=moved, transcendentals=0),
+        cost_estimate=pl.CostEstimate(flops=int(flops), bytes_accessed=moved, transcendentals=0),
     )(info, *args)
 
 
@@ -84,29 +85,46 @@
     home_to_plane = [
         (at(z, s) * M + f, (s * M + f) * M + z) for z in range(M) for s in range(per) for f in range(M)
     ]
-    plane_to_home = [(b, a) for a, b in home_to_plane]
 
     def source_route(r):
         return [
             ((s * M + f) * M + z, at(z, s) * M + (f ^ r)) for z in range(M) for s in range(per) for f in range(M)
         ]
 
-    def prepare(info, ef, tgt, src, wm, wu, wa, we, *outs):
-        g, m = info[0], info[1]
-        chunks, (ids, w1, w2) = outs[:M], outs[M:]
+    def split_rows(info, ef, *refs):
+        m = info[1]
+        outs, sem = refs[:M], refs[M]
+        copies = []
         for k in range(M):
             for s in range(per):
-                chunks[k][s * CAP : (s + 1) * CAP, :] = ef[block_rows(at(m ^ k, s)), :]
+                copies.append(
+                    pltpu.make_async_copy(
+                        ef.at[block_rows(at(m ^ k, s)), :],
+                        outs[k].at[s * CAP : (s + 1) * CAP, :],
+                        sem.at[k * per + s],
+                    )
+                )
+        for c in copies:
+            c.start()
+        for c in copies:
+            c.wait()
+
+    def pack(info, tgt, src, wm, wu, ids, w1):
+        g, m, atoms = info[0], info[1], info[2]
         core = g % 2
-        half, uhalf = w1.shape[0] - wu.shape[0] // 2, wu.shape[0] // 2
+        uhalf = wu.shape[0] // 2
+        half = w1.shape[0] - uhalf
         w1[:half, :] = wm[pl.ds(pl.multiple_of(core * half, half), half), :]
         w1[half:, :] = wu[pl.ds(pl.multiple_of(core * uhalf, uhalf), uhalf), :]
-        w2[:half, :] = wa[pl.ds(pl.multiple_of(core * half, half), half), :]
-        w2[half:, :] = we[pl.ds(pl.multiple_of(core * half, half), half), :]
-        atoms = info[2]
         for d in range(G):
             ids[d, 0:1, :] = lax.rem(tgt[pl.ds(at(m, d // M), 1), :], atoms)
             ids[d, 1:, :] = lax.rem(src[...], atoms)
+
+    def pack_later(info, wa, we, w2):
+        core = info[0] % 2
+        half = w2.shape[0] // 2
+        w2[:half, :] = wa[pl.ds(pl.multiple_of(core * half, half), half), :]
+        w2[half:, :] = we[pl.ds(pl.multiple_of(core * half, half), half), :]
 
     def triplets(info, *refs):
         m = info[1]
@@ -160,18 +178,26 @@
         for f in range(M):
             out[0, f] = sent[:, f * width : (f + 1) * width]
 
-    def aggregate(info, incoming, ids, af, *outs):
+    def aggregate(info, incoming, ids, af, *refs):
         f = info[0] % M
+        outs, onehot = refs[:M], refs[M]
         part = outs[0].shape[0]
+        low = lax.broadcasted_iota(jnp.int32, (LANES, CAP), 0)
         for r in range(M):
             q = f ^ r
-            rows = lax.broadcasted_iota(jnp.int32, (part, CAP), 0) + q * part
-
-            def add(g, acc):
-                onehot = (rows == ids[g, 0:1, :]).astype(F32).astype(BF)
-                return acc + dot(onehot, incoming[g])
-
-            acc = lax.fori_loop(0, G, add, jnp.zeros(outs[0].shape, F32), unroll=G <= 8)
+
+            def fill(g, _):
+                row = ids[g, 0:1, :]
+                near = (low == lax.rem(row, LANES)).astype(F32).astype(BF)
+                far = jnp.broadcast_to(lax.div(row, LANES) - q * (part // LANES), (LANES, CAP)).astype(F32).astype(BF)
+                for h in range(part // LANES):
+                    onehot[h * LANES : (h + 1) * LANES, lanes(g, CAP)] = jnp.where(
+                        far == BF(h), near, jnp.zeros_like(near)
+                    )
+                return 0
+
+            lax.fori_loop(0, G, fill, 0, unroll=G <= 8)
+            acc = dot(onehot[...], incoming[...])
             base = af[pl.ds(pl.multiple_of(q * part, part), part), :].astype(F32)
             outs[r][...] = (base + acc).astype(BF)
 
@@ -189,15 +215,18 @@
         for r in range(M):
             outs[r][...] = x[:, lanes(f ^ r, width)]
 
-    def pick_rows(row, table):
-        atoms = table.shape[0]
-        onehot = lax.broadcasted_iota(jnp.int32, (CAP, atoms), 1) == column(row)
-        return dot(onehot.astype(F32).astype(BF), table[...]).astype(BF)
+    def pick_rows(row, table, onehot):
+        col = column(row)
+        near = (lax.broadcasted_iota(jnp.int32, (CAP, LANES), 1) == lax.rem(col, LANES)).astype(F32).astype(BF)
+        far = jnp.broadcast_to(lax.div(col, LANES), (CAP, LANES)).astype(F32).astype(BF)
+        for h in range(table.shape[0] // LANES):
+            onehot[:, h * LANES : (h + 1) * LANES] = jnp.where(far == BF(h), near, jnp.zeros_like(near))
+        return dot(onehot[...], table[...]).astype(BF)
 
     def sources(info, *refs):
         g, m = info[0], info[1]
         f, slot = g % M, g // M
-        parts, ids, outs, table = refs[:M], refs[M], refs[M + 1 : 2 * M + 1], refs[2 * M + 1]
+        parts, ids, outs, table, onehot = refs[:M], refs[M], refs[M + 1 : 2 * M + 1], refs[2 * M + 1], refs[2 * M + 2]
         part = parts[0].shape[0]
         for r in range(M):
             table[pl.ds(pl.multiple_of((f ^ r) * part, part), part), :] = parts[r][...]
@@ -205,11 +234,11 @@
         for r in range(M):
             for s in range(per):
                 row = ids[mine, pl.ds(1 + at(f ^ r, s), 1), :]
-                outs[r][s * CAP : (s + 1) * CAP, :] = pick_rows(row, table)
-
-    def targets(info, table, ids, out):
+                outs[r][s * CAP : (s + 1) * CAP, :] = pick_rows(row, table, onehot.at[s % 2])
+
+    def targets(info, table, ids, out, onehot):
         def one(g, _):
-            out[g] = pick_rows(ids[g, 0:1, :], table)
+            out[g] = pick_rows(ids[g, 0:1, :], table, onehot.at[g % 2])
             return 0
 
         lax.fori_loop(0, G, one, 0, unroll=G <= 8)
@@ -239,6 +268,13 @@
         for k in range(M):
             for s in range(per):
                 out[block_rows(at(m ^ k, s)), :] = parts[k][s * CAP : (s + 1) * CAP, :]
+
+    def assemble_atoms(info, *refs):
+        m = info[1]
+        parts, out = refs[:M], refs[M]
+        part = parts[0].shape[0]
+        for r in range(M):
+            out[pl.ds(pl.multiple_of((m ^ r) * part, part), part), :] = parts[r][...]
 
     def local(ef, esrc, etgt, live, partner, mask, basis, af, w_msg, w_down, w_bil, w_up, w_atom, w_edge):
         rows, width = ef.shape
@@ -251,15 +287,25 @@
         m = lax.axis_index("mp")
         info = jnp.stack([g, m, jnp.int32(atoms)]).astype(jnp.int32)
         w1_rows = depth // 2 + dt // 2
-        *chunks, ids, w1, w2 = call(
-            prepare,
-            [sds((chunk, width))] * M + [sds((G, 1 + G, CAP), jnp.int32), sds((w1_rows, width)), sds((depth, width))],
-            info,
-            [ef, etgt.reshape(G, CAP), esrc.reshape(G, CAP), w_msg, w_up, w_atom, w_edge],
+        chunks = call(
+            split_rows,
+            [sds((chunk, width))] * M,
+            info,
+            [ef],
+            scratch=[pltpu.SemaphoreType.DMA((M * per,))],
+            in_specs=[pl.BlockSpec(memory_space=pl.ANY)],
+        )
+        ids, w1 = call(
+            pack,
+            [sds((G, 1 + G, CAP), jnp.int32), sds((w1_rows, width))],
+            info,
+            [etgt.reshape(G, CAP), esrc.reshape(G, CAP), w_msg, w_up],
+            flops=1.0e9,
         )
         xs = [chunks[0]] + [over_mp(chunks[k], k) for k in range(1, M)]
         w1s = [w1] + [over_mp(w1, k) for k in range(1, M)]
         ids = lax.all_to_all(ids, "graph", split_axis=0, concat_axis=0, tiled=True)
+        basis, ids = lax.optimization_barrier((basis, ids))
 
         blk = lambda i, info: at(info[1], i)
         x, bil = call(
@@ -297,26 +343,50 @@
             ],
         )
         incoming = lax.all_to_all(outgoing.reshape(G, CAP, width), "graph", split_axis=0, concat_axis=0, tiled=True)
-        af_later, w2_later, _ = lax.optimization_barrier((af, w2, xs[1]))
+        af_later, wa_later, we_later, _ = lax.optimization_barrier((af, w_atom, w_edge, xs[1]))
         af_plane = lax.ppermute(af_later, both, home_to_plane)
-        w2s = [w2_later] + [over_mp(w2_later, k) for k in range(1, M)]
+        (w2,) = call(pack_later, [sds((depth, width))], info, [wa_later, we_later], flops=1.0e9)
+        w2s = [w2] + [over_mp(w2, k) for k in range(1, M)]
+
+        mids = call(
+            aggregate,
+            [sds((part, width))] * M,
+            info,
+            [incoming.reshape(G * CAP, width), ids, af_plane],
+            scratch=[pltpu.VMEM((part, G * CAP), BF)],
+            flops=3.0e9,
+        )
+        *w2s, mid0 = lax.optimization_barrier((*w2s, mids[0]))
         w2o = [over_plane(w, 1) for w in w2s]
-
-        mids = call(aggregate, [sds((part, width))] * M, info, [incoming, ids, af_plane])
-        mids = [mids[0]] + [over_plane(mids[r], r) for r in range(1, M)]
+        mids = [mid0] + [over_plane(mids[r], r) for r in range(1, M)]
         outs = call(
             atom_layer,
             [sds((part, width))] * M,
             info,
             mids + w2s + w2o,
             scratch=[pltpu.VMEM((part, depth), BF), pltpu.VMEM((depth, depth), BF)],
-        )
+            flops=1.5e9,
+        )
+        homeward = [lax.ppermute(outs[r], both, source_route(r)) for r in range(M)]
         outs = [outs[0]] + [over_plane(outs[r], r) for r in range(1, M)]
-        *srcs, table = call(sources, [sds((chunk, width))] * M + [sds((atoms, width))], info, list(outs) + [ids])
+        *srcs, table = call(
+            sources,
+            [sds((chunk, width))] * M + [sds((atoms, width))],
+            info,
+            list(outs) + [ids],
+            scratch=[pltpu.VMEM((2, CAP, atoms), BF)],
+            flops=4.0e9,
+        )
         srcs = [lax.ppermute(srcs[r], both, source_route(r)) for r in range(M)]
-        (named,) = call(targets, [sds((G, CAP, width))], info, [table, ids])
+        (named,) = call(
+            targets,
+            [sds((G, CAP, width))],
+            info,
+            [table, ids],
+            scratch=[pltpu.VMEM((2, CAP, atoms), BF)],
+            flops=4.0e9,
+        )
         tgt = lax.all_to_all(named, "graph", split_axis=0, concat_axis=0, tiled=True)
-        atom_out = lax.ppermute(table, both, plane_to_home)
         outs = call(
             edges,
             [sds((chunk, width))] * M,
@@ -333,7 +403,8 @@
             out_specs=[pl.BlockSpec((CAP, width), lambda i, info: (i, 0))] * M,
         )
         outs = [outs[0]] + [over_mp(outs[k], k) for k in range(1, M)]
-        (edge_out,) = call(assemble, [sds((rows, width))], info, list(outs))
+        (atom_out,) = call(assemble_atoms, [sds((atoms, width))], info, homeward, flops=1.0e9)
+        (edge_out,) = call(assemble, [sds((rows, width))], info, list(outs), flops=1.0e9)
         return (edge_out, atom_out)
 
     return jax.shard_map(

time: 162 us -> 145 us (0.90)
  the two profiles are of different devices: /device:TPU:0 before, /device:TPU:17 now
where the time goes in v2:
time: 145 us; the launch traced here: 144 us
  starting transfers between devices  67.1 us (46%)
  waiting for transfers between devices  44.5 us (31%)
  Pallas kernels  28.8 us (20%)
  local copies, waits for them, and re-layouts  2.92 us (2%)
    pallas_call x12, Pallas kernels, call(): pl.pallas_call(kernel, out_shape=list(out_shapes), grid_spec=pltpu.Prefet...  28.8 us
    ppermute x12, waiting for transfers between devices, over_mp(): return lax.ppermute(x, 'mp', [(i, i ^ k) for i in range(M)])  28.2 us
    ppermute x12, starting transfers between devices, over_mp(): return lax.ppermute(x, 'mp', [(i, i ^ k) for i in range(M)])  14.4 us
    ppermute x4, starting transfers between devices, local(): srcs = [lax.ppermute(srcs[r], both, source_route(r)) for r in range(M)]  13.5 us
    ppermute x14, waiting for transfers between devices, over_plane(): return lax.ppermute(x, 'graph', [(i, i ^ k) for i in range(G)])  12.3 us
    ppermute x4, starting transfers between devices, local(): homeward = [lax.ppermute(outs[r], both, source_route(r)) for r in range(M)]  11.8 us
    ppermute x14, starting transfers between devices, over_plane(): return lax.ppermute(x, 'graph', [(i, i ^ k) for i in range(G)])  9.33 us
    all_to_all x1, starting transfers between devices, local(): lax.all_to_all(outgoing.reshape(G, CAP, width), 'graph', split_axis=0, co...  5.68 us
  transfers between devices with their start and end apart: 38, of which 12 were waited for; matrix products, arithmetic and copies ran while one was open for 0% of the time, Pallas kernels for 10%

profile of v2, /device:TPU:17, one launch (start us, length us, event | category | flops | bytes accessed | tf_op | source)
XLA Modules:
  0.0 144.3 jit_solution(16432426686883537007)
XLA Ops:
  3.0 2.2 %shard_map.151 = (s32[8,9,256]{2,1,0:T(8,128)}, bf16[288,128]{1,0:T(8,128)(2,1)S(1)}) custom-call(s32[3]{0:T(128)S(1)} %pad_add_fusion.info, s32[8,256]{1,0:T(8,128)S(1)} %reshape.22.tgt, s32[8,256]{1,0:T(8,128)S(1)} %reshape.23.src, bf16[512,128]{1,0:T(8,128)(2,1)S(1)} %copy-done.6, bf16[64,128]{1,0:T(8,128)(2,1)S(1)} %copy-done.11), custom_call_target="tpu_custom_call" | custom-call | flops 1000000000 | tf_op jit(solution)/shard_map/pallas_call | solution.py:44
  7.9 2.1 %collective-permute-start.11 = (bf16[512,128]{1,0:T(8,128)(2,1)S(1)}, bf16[512,128]{1,0:T(8,128)(2,1)S(1)}, u32[]{:S(2)}, u32[]{:S(2)}) collective-permute-start(bf16[512,128]{1,0:T(8,128)(2,1)S(1)} %get-tuple-element.44), channel_id=1, source_target_pairs={{0,2},{1,3},{2,0},{3,1},{4,6},{5,7},{6,4},{7,5},{8,10},{9,11},{10,... | collective-permute-start | bytes 393224 | tf_op jit(solution)/shard_map/ppermute | solution.py:80
  10.2 3.3 %collective-permute-start.5 = (bf16[288,128]{1,0:T(8,128)(2,1)S(1)}, bf16[288,128]{1,0:T(8,128)(2,1)S(1)}, u32[]{:S(2)}, u32[]{:S(2)}) collective-permute-start(bf16[288,128]{1,0:T(8,128)(2,1)S(1)} %get-tuple-element.42.refs_0_), channel_id=1, source_target_pairs={{0,2},{1,3},{2,0},{3,1},{4,6},{5,7},{6,4},{7,5},{8,10},{9,11},{10,... | collective-permute-start | bytes 221192 | tf_op jit(solution)/shard_map/ppermute | solution.py:80
  13.5 10.3 %collective-permute-done.5.refs_2_ = bf16[288,128]{1,0:T(8,128)(2,1)S(1)} collective-permute-done((bf16[288,128]{1,0:T(8,128)(2,1)S(1)}, bf16[288,128]{1,0:T(8,128)(2,1)S(1)}, u32[]{:S(2)}, u32[]{:S(2)}) %collective-permute-start.5) | collective-permute-done | bytes 73760 | tf_op jit(solution)/shard_map/ppermute | solution.py:80
  26.0 4.3 %all-to-all-start = ((s32[8,9,256]{2,1,0:T(8,128)}), s32[8,9,256]{2,1,0:T(8,128)S(1)}, u32[]{:S(2)}, u32[]{:S(2)}) async-start(s32[8,9,256]{2,1,0:T(8,128)} %get-tuple-element.46), calls=%async_computation | async-start | bytes 262144 | tf_op jit(solution)/shard_map/all_to_all | solution.py:307
  30.3 3.5 %collective-permute-start.13 = (bf16[2048,128]{1,0:T(8,128)(2,1)S(1)}, bf16[2048,128]{1,0:T(8,128)(2,1)S(1)}, u32[]{:S(2)}, u32[]{:S(2)}) collective-permute-start(bf16[2048,128]{1,0:T(8,128)(2,1)S(1)} %copy-done.15), channel_id=1, source_target_pairs={{0,0},{1,4},{2,8},{3,12},{20,16},{21,20},{22,24},{23,28},{8,1},{9,... | collective-permute-start | bytes 1572872 | tf_op jit(solution)/shard_map/ppermute | solution.py:347
  34.9 3.1 %shard_map.152 = (bf16[512,512]{1,0:T(8,128)(2,1)S(1)}, bf16[512,64]{1,0:T(8,128)(2,1)S(1)}) custom-call(s32[3]{0:T(128)S(1)} %pad_add_fusion.info, bf16[512,128]{1,0:T(8,128)(2,1)S(1)} %get-tuple-element.43.refs_0_, bf16[512,128]{1,0:T(8,128)(2,1)S(1)} %collective-permute-done.refs_1_, bf16[512,128]{1,0:T(8,128)(2,1)S(1)} %collective-permute-done.11.refs_2_, ...), custom_call_target="tpu_custom_call" | custom-call | tf_op jit(solution)/shard_map/pallas_call | solution.py:44
  38.1 2.4 %shard_map.153 = (f32[512,512]{1,0:T(8,128)S(1)}, bf16[2,4,256,128]{3,2,1,0:T(8,128)(2,1)}) custom-call(s32[3]{0:T(128)S(1)} %pad_add_fusion.info, bf16[288,128]{1,0:T(8,128)(2,1)S(1)} %get-tuple-element.42.refs_0_, bf16[288,128]{1,0:T(8,128)(2,1)S(1)} %collective-permute-done.4.refs_1_, bf16[288,128]{1,0:T(8,128)(2,1)S(1)} %collective-permute-done.5.refs_2_, ...), custom_call_target="tpu_custom_call" | custom-call | tf_op jit(solution)/shard_map/pallas_call | solution.py:44
  40.5 5.7 %all-to-all-start.1 = ((bf16[8,256,128]{2,1,0:T(8,128)(2,1)}), bf16[8,256,128]{2,1,0:T(8,128)(2,1)S(1)}, u32[]{:S(2)}, u32[]{:S(2)}) async-start(bf16[8,256,128]{2,1,0:T(8,128)(2,1)} %bitcast.4), calls=%async_computation.1 | async-start | bytes 1048576 | tf_op jit(solution)/shard_map/all_to_all | solution.py:345
  46.9 3.3 %collective-permute-start.2 = (bf16[512,128]{1,0:T(8,128)(2,1)S(1)}, bf16[512,128]{1,0:T(8,128)(2,1)S(1)}, u32[]{:S(2)}, u32[]{:S(2)}) collective-permute-start(bf16[512,128]{1,0:T(8,128)(2,1)S(1)} %shard_map.150.refs_4_), channel_id=1, source_target_pairs={{0,2},{1,3},{2,0},{3,1},{4,6},{5,7},{6,4},{7,5},{8,10},{9,11},{10,... | collective-permute-start | bytes 393224 | tf_op jit(solution)/shard_map/ppermute | solution.py:80
  50.1 2.8 %all-to-all-done.1 = bf16[8,256,128]{2,1,0:T(8,128)(2,1)S(1)} async-done(((bf16[8,256,128]{2,1,0:T(8,128)(2,1)}), bf16[8,256,128]{2,1,0:T(8,128)(2,1)S(1)}, u32[]{:S(2)}, u32[]{:S(2)}) %all-to-all-start.1) | async-done | bytes 524320 | tf_op jit(solution)/shard_map/all_to_all | solution.py:345
  53.0 2.9 %shard_map.154 = (bf16[512,128]{1,0:T(8,128)(2,1)S(1)}, bf16[512,128]{1,0:T(8,128)(2,1)S(1)}, bf16[512,128]{1,0:T(8,128)(2,1)S(1)}, bf16[512,128]{1,0:T(8,128)(2,1)S(1)}) custom-call(s32[3]{0:T(128)S(1)} %pad_add_fusion.info, bf16[2048,128]{1,0:T(8,128)(2,1)S(1)} %bitcast.8, s32[8,9,256]{2,1,0:T(8,128)S(1)} %all-to-all-done.ids.refs_4_, ...), custom_call_target="tpu_custom_call" | custom-call | flops 3000000000 | tf_op jit(solution)/shard_map/pallas_call | solution.py:44
  56.7 1.9 %collective-permute-done.2.refs_6_ = bf16[512,128]{1,0:T(8,128)(2,1)S(1)} collective-permute-done((bf16[512,128]{1,0:T(8,128)(2,1)S(1)}, bf16[512,128]{1,0:T(8,128)(2,1)S(1)}, u32[]{:S(2)}, u32[]{:S(2)}) %collective-permute-start.2) | collective-permute-done | bytes 131104 | tf_op jit(solution)/shard_map/ppermute | solution.py:80
  58.8 1.8 %collective-permute-start.17 = (bf16[512,128]{1,0:T(8,128)(2,1)S(1)}, bf16[512,128]{1,0:T(8,128)(2,1)S(1)}, u32[]{:S(2)}, u32[]{:S(2)}) collective-permute-start(bf16[512,128]{1,0:T(8,128)(2,1)S(1)} %shard_map.150.refs_4_), channel_id=1, source_target_pairs={{0,4},{4,0},{8,12},{12,8},{16,20},{20,16},{24,28},{28,24},{1,5},{5... | collective-permute-start | bytes 393224 | tf_op jit(solution)/shard_map/ppermute | solution.py:83
  61.7 1.7 %collective-permute-start.15 = (bf16[512,128]{1,0:T(8,128)(2,1)S(1)}, bf16[512,128]{1,0:T(8,128)(2,1)S(1)}, u32[]{:S(2)}, u32[]{:S(2)}) collective-permute-start(bf16[512,128]{1,0:T(8,128)(2,1)S(1)} %get-tuple-element.56), channel_id=1, source_target_pairs={{0,8},{4,12},{8,0},{12,4},{16,24},{20,28},{24,16},{28,20},{1,9},{5... | collective-permute-start | bytes 393224 | tf_op jit(solution)/shard_map/ppermute | solution.py:83
  63.8 3.2 %collective-permute-done.15.refs_2_ = bf16[512,128]{1,0:T(8,128)(2,1)S(1)} collective-permute-done((bf16[512,128]{1,0:T(8,128)(2,1)S(1)}, bf16[512,128]{1,0:T(8,128)(2,1)S(1)}, u32[]{:S(2)}, u32[]{:S(2)}) %collective-permute-start.15) | collective-permute-done | bytes 131104 | tf_op jit(solution)/shard_map/ppermute | solution.py:83
  67.0 3.0 %collective-permute-done.16.refs_3_ = bf16[512,128]{1,0:T(8,128)(2,1)S(1)} collective-permute-done((bf16[512,128]{1,0:T(8,128)(2,1)S(1)}, bf16[512,128]{1,0:T(8,128)(2,1)S(1)}, u32[]{:S(2)}, u32[]{:S(2)}) %collective-permute-start.16) | collective-permute-done | bytes 131104 | tf_op jit(solution)/shard_map/ppermute | solution.py:83
  73.6 2.9 %collective-permute-done.22.refs_2_ = bf16[512,128]{1,0:T(8,128)(2,1)S(1)} collective-permute-done((bf16[512,128]{1,0:T(8,128)(2,1)S(1)}, bf16[512,128]{1,0:T(8,128)(2,1)S(1)}, u32[]{:S(2)}, u32[]{:S(2)}) %collective-permute-start.22) | collective-permute-done | bytes 131104 | tf_op jit(solution)/shard_map/ppermute | solution.py:83
  76.5 3.2 %collective-permute-done.23.refs_3_ = bf16[512,128]{1,0:T(8,128)(2,1)S(1)} collective-permute-done((bf16[512,128]{1,0:T(8,128)(2,1)S(1)}, bf16[512,128]{1,0:T(8,128)(2,1)S(1)}, u32[]{:S(2)}, u32[]{:S(2)}) %collective-permute-start.23) | collective-permute-done | bytes 131104 | tf_op jit(solution)/shard_map/ppermute | solution.py:83
  79.7 4.5 %shard_map.156 = (bf16[512,128]{1,0:T(8,128)(2,1)}, bf16[512,128]{1,0:T(8,128)(2,1)}, bf16[512,128]{1,0:T(8,128)(2,1)}, bf16[512,128]{1,0:T(8,128)(2,1)S(1)}, bf16[2048,128]{1,0:T(8,128)(2,1)S(1)}) custom-call(s32[3]{0:T(128)S(1)} %pad_add_fusion.info, bf16[512,128]{1,0:T(8,128)(2,1)S(1)} %get-tuple-element.62.refs_0_, ...), custom_call_target="tpu_custom_call" | custom-call | flops 4000000000 | tf_op jit(solution)/shard_map/pallas_call | solution.py:44
  84.9 4.8 %shard_map.157 = bf16[8,256,128]{2,1,0:T(8,128)(2,1)} custom-call(s32[3]{0:T(128)S(1)} %pad_add_fusion.info, bf16[2048,128]{1,0:T(8,128)(2,1)S(1)} %get-tuple-element.70.table, s32[8,9,256]{2,1,0:T(8,128)S(1)} %all-to-all-done.ids.refs_4_), custom_call_target="tpu_custom_call" | custom-call | flops 4000000000 | tf_op jit(solution)/shard_map/pallas_call | solution.py:44
  89.7 4.5 %all-to-all-start.2 = ((bf16[8,256,128]{2,1,0:T(8,128)(2,1)}), bf16[8,256,128]{2,1,0:T(8,128)(2,1)S(1)}, u32[]{:S(2)}, u32[]{:S(2)}) async-start(bf16[8,256,128]{2,1,0:T(8,128)(2,1)} %shard_map.157), calls=%async_computation.2 | async-start | bytes 1048576 | tf_op jit(solution)/shard_map/all_to_all | solution.py:389
  94.2 2.1 %collective-permute-start.24 = (bf16[512,128]{1,0:T(8,128)(2,1)}, bf16[512,128]{1,0:T(8,128)(2,1)S(1)}, u32[]{:S(2)}, u32[]{:S(2)}) collective-permute-start(bf16[512,128]{1,0:T(8,128)(2,1)} %get-tuple-element.66), channel_id=1, source_target_pairs={{0,0},{4,1},{8,2},{12,3},{16,20},{20,21},{24,22},{28,23},{1,8},{5,... | collective-permute-start | bytes 393224 | tf_op jit(solution)/shard_map/ppermute | solution.py:380
  96.3 3.8 %collective-permute-start.25 = (bf16[512,128]{1,0:T(8,128)(2,1)}, bf16[512,128]{1,0:T(8,128)(2,1)S(1)}, u32[]{:S(2)}, u32[]{:S(2)}) collective-permute-start(bf16[512,128]{1,0:T(8,128)(2,1)} %get-tuple-element.67), channel_id=1, source_target_pairs={{0,1},{4,0},{8,3},{12,2},{16,21},{20,20},{24,23},{28,22},{1,9},{5,... | collective-permute-start | bytes 393224 | tf_op jit(solution)/shard_map/ppermute | solution.py:380
  100.2 6.1 %collective-permute-start.26 = (bf16[512,128]{1,0:T(8,128)(2,1)}, bf16[512,128]{1,0:T(8,128)(2,1)S(1)}, u32[]{:S(2)}, u32[]{:S(2)}) collective-permute-start(bf16[512,128]{1,0:T(8,128)(2,1)} %get-tuple-element.68), channel_id=1, source_target_pairs={{0,2},{4,3},{8,0},{12,1},{16,22},{20,23},{24,20},{28,21},{1,10},{5... | collective-permute-start | bytes 393224 | tf_op jit(solution)/shard_map/ppermute | solution.py:380
  107.8 1.9 %collective-permute-start.31 = (bf16[512,128]{1,0:T(8,128)(2,1)}, bf16[512,128]{1,0:T(8,128)(2,1)}, u32[]{:S(2)}, u32[]{:S(2)}) collective-permute-start(bf16[512,128]{1,0:T(8,128)(2,1)} %copy-done.9), channel_id=1, source_target_pairs={{0,0},{4,1},{8,2},{12,3},{16,20},{20,21},{24,22},{28,23},{1,8},{5,... | collective-permute-start | bytes 393224 | tf_op jit(solution)/shard_map/ppermute | solution.py:370
  109.7 5.8 %collective-permute-start.32 = (bf16[512,128]{1,0:T(8,128)(2,1)S(1)}, bf16[512,128]{1,0:T(8,128)(2,1)}, u32[]{:S(2)}, u32[]{:S(2)}) collective-permute-start(bf16[512,128]{1,0:T(8,128)(2,1)S(1)} %get-tuple-element.63), channel_id=1, source_target_pairs={{0,1},{4,0},{8,3},{12,2},{16,21},{20,20},{24,23},{28,22},{1,9},{5,... | collective-permute-start | bytes 393224 | tf_op jit(solution)/shard_map/ppermute | solution.py:370
  115.5 2.8 %collective-permute-start.33 = (bf16[512,128]{1,0:T(8,128)(2,1)S(1)}, bf16[512,128]{1,0:T(8,128)(2,1)}, u32[]{:S(2)}, u32[]{:S(2)}) collective-permute-start(bf16[512,128]{1,0:T(8,128)(2,1)S(1)} %get-tuple-element.64), channel_id=1, source_target_pairs={{0,2},{4,3},{8,0},{12,1},{16,22},{20,23},{24,20},{28,21},{1,10},{5... | collective-permute-start | bytes 393224 | tf_op jit(solution)/shard_map/ppermute | solution.py:370
  119.6 1.7 %shard_map.158 = (bf16[512,128]{1,0:T(8,128)(2,1)S(1)}, bf16[512,128]{1,0:T(8,128)(2,1)S(1)}, bf16[512,128]{1,0:T(8,128)(2,1)S(1)}, bf16[512,128]{1,0:T(8,128)(2,1)S(1)}) custom-call(s32[3]{0:T(128)S(1)} %pad_add_fusion.info, bf16[512,128]{1,0:T(8,128)(2,1)S(1)} %collective-permute-done.24.refs_0_, bf16[512,128]{1,0:T(8,128)(2,1)S(1)} %collective-permute-done.25.refs_1_, ...), custom_call_target="tpu_custom_call" | custom-call | tf_op jit(solution)/shard_map/pallas_call | solution.py:44
  121.4 2.8 %collective-permute-start.28 = (bf16[512,128]{1,0:T(8,128)(2,1)S(1)}, bf16[512,128]{1,0:T(8,128)(2,1)S(1)}, u32[]{:S(2)}, u32[]{:S(2)}) collective-permute-start(bf16[512,128]{1,0:T(8,128)(2,1)S(1)} %get-tuple-element.73), channel_id=1, source_target_pairs={{0,1},{1,0},{2,3},{3,2},{4,5},{5,4},{6,7},{7,6},{8,9},{9,8},{10,11... | collective-permute-start | bytes 393224 | tf_op jit(solution)/shard_map/ppermute | solution.py:80
  125.4 2.5 %shard_map.160 = bf16[2048,128]{1,0:T(8,128)(2,1)} custom-call(s32[3]{0:T(128)S(1)} %pad_add_fusion.info, bf16[512,128]{1,0:T(8,128)(2,1)} %collective-permute-done.31.refs_0_, bf16[512,128]{1,0:T(8,128)(2,1)} %collective-permute-done.32.refs_1_, bf16[512,128]{1,0:T(8,128)(2,1)} %collective-permute-done.33.refs_2_, ...), custom_call_target="tpu_custom_call" | custom-call | flops 1000000000 | tf_op jit(solution)/shard_map/pallas_call | solution.py:44
  129.3 13.6 %collective-permute-done.30.refs_3_ = bf16[512,128]{1,0:T(8,128)(2,1)S(1)} collective-permute-done((bf16[512,128]{1,0:T(8,128)(2,1)S(1)}, bf16[512,128]{1,0:T(8,128)(2,1)S(1)}, u32[]{:S(2)}, u32[]{:S(2)}) %collective-permute-start.30) | collective-permute-done | bytes 131104 | tf_op jit(solution)/shard_map/ppermute | solution.py:80
  (92 shorter events, 22.9 us)
Async XLA Ops:
  5.1 8.4 %collective-permute-start.6 = (bf16[288,128]{1,0:T(8,128)(2,1)S(1)}, bf16[288,128]{1,0:T(8,128)(2,1)S(1)}, u32[]{:S(2)}, u32[]{:S(2)}) collective-permute-start(bf16[288,128]{1,0:T(8,128)(2,1)S(1)} %get-tuple-element.42.refs_0_), channel_id=1, source_target_pairs={{0,3},{1,2},{2,1},{3,0},{4,7},{5,6},{6,5},{7,4},{8,11},{9,10},{10,... | collective-permute-start | bytes 221192 | tf_op jit(solution)/shard_map/ppermute | solution.py:80
  6.7 18.7 %collective-permute-start = (bf16[512,128]{1,0:T(8,128)(2,1)S(1)}, bf16[512,128]{1,0:T(8,128)(2,1)S(1)}, u32[]{:S(2)}, u32[]{:S(2)}) collective-permute-start(bf16[512,128]{1,0:T(8,128)(2,1)S(1)} %get-tuple-element.39), channel_id=1, source_target_pairs={{0,1},{1,0},{2,3},{3,2},{4,5},{5,4},{6,7},{7,6},{8,9},{9,8},{10,11... | collective-permute-start | bytes 393224 | tf_op jit(solution)/shard_map/ppermute | solution.py:80
  7.9 18.0 %collective-permute-start.11 = (bf16[512,128]{1,0:T(8,128)(2,1)S(1)}, bf16[512,128]{1,0:T(8,128)(2,1)S(1)}, u32[]{:S(2)}, u32[]{:S(2)}) collective-permute-start(bf16[512,128]{1,0:T(8,128)(2,1)S(1)} %get-tuple-element.44), channel_id=1, source_target_pairs={{0,2},{1,3},{2,0},{3,1},{4,6},{5,7},{6,4},{7,5},{8,10},{9,11},{10,... | collective-permute-start | bytes 393224 | tf_op jit(solution)/shard_map/ppermute | solution.py:80
  10.0 20.2 %collective-permute-start.12 = (bf16[512,128]{1,0:T(8,128)(2,1)S(1)}, bf16[512,128]{1,0:T(8,128)(2,1)S(1)}, u32[]{:S(2)}, u32[]{:S(2)}) collective-permute-start(bf16[512,128]{1,0:T(8,128)(2,1)S(1)} %get-tuple-element.45), channel_id=1, source_target_pairs={{0,3},{1,2},{2,1},{3,0},{4,7},{5,6},{6,5},{7,4},{8,11},{9,10},{10,... | collective-permute-start | bytes 393224 | tf_op jit(solution)/shard_map/ppermute | solution.py:80
  10.2 13.5 %collective-permute-start.5 = (bf16[288,128]{1,0:T(8,128)(2,1)S(1)}, bf16[288,128]{1,0:T(8,128)(2,1)S(1)}, u32[]{:S(2)}, u32[]{:S(2)}) collective-permute-start(bf16[288,128]{1,0:T(8,128)(2,1)S(1)} %get-tuple-element.42.refs_0_), channel_id=1, source_target_pairs={{0,2},{1,3},{2,0},{3,1},{4,6},{5,7},{6,4},{7,5},{8,10},{9,11},{10,... | collective-permute-start | bytes 221192 | tf_op jit(solution)/shard_map/ppermute | solution.py:80
  13.5 11.9 %collective-permute-start.4 = (bf16[288,128]{1,0:T(8,128)(2,1)S(1)}, bf16[288,128]{1,0:T(8,128)(2,1)S(1)}, u32[]{:S(2)}, u32[]{:S(2)}) collective-permute-start(bf16[288,128]{1,0:T(8,128)(2,1)S(1)} %get-tuple-element.42.refs_0_), channel_id=1, source_target_pairs={{0,1},{1,0},{2,3},{3,2},{4,5},{5,4},{6,7},{7,6},{8,9},{9,8},{10,11... | collective-permute-start | bytes 221192 | tf_op jit(solution)/shard_map/ppermute | solution.py:80
  23.8 14.3 %collective-permute-start.7 = (bf16[288,128]{1,0:T(8,128)(2,1)S(1)}, bf16[288,128]{1,0:T(8,128)(2,1)S(1)}, u32[]{:S(2)}, u32[]{:S(2)}) collective-permute-start(bf16[288,128]{1,0:T(8,128)(2,1)S(1)} %get-tuple-element.42.refs_0_), channel_id=1, source_target_pairs={{0,4},{4,0},{8,12},{12,8},{16,20},{20,16},{24,28},{28,24},{1,5},{5... | collective-permute-start | bytes 221192 | tf_op jit(solution)/shard_map/ppermute | solution.py:83
  25.4 12.7 %collective-permute-start.10 = (bf16[288,128]{1,0:T(8,128)(2,1)S(1)}, bf16[288,128]{1,0:T(8,128)(2,1)S(1)}, u32[]{:S(2)}, u32[]{:S(2)}) collective-permute-start(bf16[288,128]{1,0:T(8,128)(2,1)S(1)} %collective-permute-done.6.refs_3_), channel_id=1, source_target_pairs={{0,4},{4,0},{8,12},{12,8},{16,20},{20,16},{24,28},{28,24},{1,5},{5... | collective-permute-start | bytes 221192 | tf_op jit(solution)/shard_map/ppermute | solution.py:83
  25.4 12.7 %collective-permute-start.9 = (bf16[288,128]{1,0:T(8,128)(2,1)S(1)}, bf16[288,128]{1,0:T(8,128)(2,1)S(1)}, u32[]{:S(2)}, u32[]{:S(2)}) collective-permute-start(bf16[288,128]{1,0:T(8,128)(2,1)S(1)} %collective-permute-done.5.refs_2_), channel_id=1, source_target_pairs={{0,4},{4,0},{8,12},{12,8},{16,20},{20,16},{24,28},{28,24},{1,5},{5... | collective-permute-start | bytes 221192 | tf_op jit(solution)/shard_map/ppermute | solution.py:83
  25.9 12.2 %collective-permute-start.8 = (bf16[288,128]{1,0:T(8,128)(2,1)S(1)}, bf16[288,128]{1,0:T(8,128)(2,1)S(1)}, u32[]{:S(2)}, u32[]{:S(2)}) collective-permute-start(bf16[288,128]{1,0:T(8,128)(2,1)S(1)} %collective-permute-done.4.refs_1_), channel_id=1, source_target_pairs={{0,4},{4,0},{8,12},{12,8},{16,20},{20,16},{24,28},{28,24},{1,5},{5... | collective-permute-start | bytes 221192 | tf_op jit(solution)/shard_map/ppermute | solution.py:83
  26.0 9.0 %all-to-all-start = ((s32[8,9,256]{2,1,0:T(8,128)}), s32[8,9,256]{2,1,0:T(8,128)S(1)}, u32[]{:S(2)}, u32[]{:S(2)}) async-start(s32[8,9,256]{2,1,0:T(8,128)} %get-tuple-element.46), calls=%async_computation | async-start | bytes 262144 | tf_op jit(solution)/shard_map/all_to_all | solution.py:307
  30.3 22.7 %collective-permute-start.13 = (bf16[2048,128]{1,0:T(8,128)(2,1)S(1)}, bf16[2048,128]{1,0:T(8,128)(2,1)S(1)}, u32[]{:S(2)}, u32[]{:S(2)}) collective-permute-start(bf16[2048,128]{1,0:T(8,128)(2,1)S(1)} %copy-done.15), channel_id=1, source_target_pairs={{0,0},{1,4},{2,8},{3,12},{20,16},{21,20},{22,24},{23,28},{8,1},{9,... | collective-permute-start | bytes 1572872 | tf_op jit(solution)/shard_map/ppermute | solution.py:347
  40.5 12.4 %all-to-all-start.1 = ((bf16[8,256,128]{2,1,0:T(8,128)(2,1)}), bf16[8,256,128]{2,1,0:T(8,128)(2,1)S(1)}, u32[]{:S(2)}, u32[]{:S(2)}) async-start(bf16[8,256,128]{2,1,0:T(8,128)(2,1)} %bitcast.4), calls=%async_computation.1 | async-start | bytes 1048576 | tf_op jit(solution)/shard_map/all_to_all | solution.py:345
  46.8 9.9 %collective-permute-start.3 = (bf16[512,128]{1,0:T(8,128)(2,1)S(1)}, bf16[512,128]{1,0:T(8,128)(2,1)S(1)}, u32[]{:S(2)}, u32[]{:S(2)}) collective-permute-start(bf16[512,128]{1,0:T(8,128)(2,1)S(1)} %shard_map.150.refs_4_), channel_id=1, source_target_pairs={{0,3},{1,2},{2,1},{3,0},{4,7},{5,6},{6,5},{7,4},{8,11},{9,10},{10,... | collective-permute-start | bytes 393224 | tf_op jit(solution)/shard_map/ppermute | solution.py:80
  46.9 11.8 %collective-permute-start.2 = (bf16[512,128]{1,0:T(8,128)(2,1)S(1)}, bf16[512,128]{1,0:T(8,128)(2,1)S(1)}, u32[]{:S(2)}, u32[]{:S(2)}) collective-permute-start(bf16[512,128]{1,0:T(8,128)(2,1)S(1)} %shard_map.150.refs_4_), channel_id=1, source_target_pairs={{0,2},{1,3},{2,0},{3,1},{4,6},{5,7},{6,4},{7,5},{8,10},{9,11},{10,... | collective-permute-start | bytes 393224 | tf_op jit(solution)/shard_map/ppermute | solution.py:80
  50.1 8.7 %collective-permute-start.1 = (bf16[512,128]{1,0:T(8,128)(2,1)S(1)}, bf16[512,128]{1,0:T(8,128)(2,1)S(1)}, u32[]{:S(2)}, u32[]{:S(2)}) collective-permute-start(bf16[512,128]{1,0:T(8,128)(2,1)S(1)} %shard_map.150.refs_4_), channel_id=1, source_target_pairs={{0,1},{1,0},{2,3},{3,2},{4,5},{5,4},{6,7},{7,6},{8,9},{9,8},{10,11... | collective-permute-start | bytes 393224 | tf_op jit(solution)/shard_map/ppermute | solution.py:80
  61.7 5.3 %collective-permute-start.15 = (bf16[512,128]{1,0:T(8,128)(2,1)S(1)}, bf16[512,128]{1,0:T(8,128)(2,1)S(1)}, u32[]{:S(2)}, u32[]{:S(2)}) collective-permute-start(bf16[512,128]{1,0:T(8,128)(2,1)S(1)} %get-tuple-element.56), channel_id=1, source_target_pairs={{0,8},{4,12},{8,0},{12,4},{16,24},{20,28},{24,16},{28,20},{1,9},{5... | collective-permute-start | bytes 393224 | tf_op jit(solution)/shard_map/ppermute | solution.py:83
  63.4 6.6 %collective-permute-start.16 = (bf16[512,128]{1,0:T(8,128)(2,1)S(1)}, bf16[512,128]{1,0:T(8,128)(2,1)S(1)}, u32[]{:S(2)}, u32[]{:S(2)}) collective-permute-start(bf16[512,128]{1,0:T(8,128)(2,1)S(1)} %get-tuple-element.57), channel_id=1, source_target_pairs={{0,12},{4,8},{8,4},{12,0},{16,28},{20,24},{24,20},{28,16},{1,13},{... | collective-permute-start | bytes 393224 | tf_op jit(solution)/shard_map/ppermute | solution.py:83
  71.7 4.8 %collective-permute-start.22 = (bf16[512,128]{1,0:T(8,128)(2,1)S(1)}, bf16[512,128]{1,0:T(8,128)(2,1)S(1)}, u32[]{:S(2)}, u32[]{:S(2)}) collective-permute-start(bf16[512,128]{1,0:T(8,128)(2,1)S(1)} %get-tuple-element.64), channel_id=1, source_target_pairs={{0,8},{4,12},{8,0},{12,4},{16,24},{20,28},{24,16},{28,20},{1,9},{5... | collective-permute-start | bytes 393224 | tf_op jit(solution)/shard_map/ppermute | solution.py:83
  73.0 6.7 %collective-permute-start.23 = (bf16[512,128]{1,0:T(8,128)(2,1)S(1)}, bf16[512,128]{1,0:T(8,128)(2,1)S(1)}, u32[]{:S(2)}, u32[]{:S(2)}) collective-permute-start(bf16[512,128]{1,0:T(8,128)(2,1)S(1)} %get-tuple-element.65), channel_id=1, source_target_pairs={{0,12},{4,8},{8,4},{12,0},{16,28},{20,24},{24,20},{28,16},{1,13},{... | collective-permute-start | bytes 393224 | tf_op jit(solution)/shard_map/ppermute | solution.py:83
  89.7 29.9 %all-to-all-start.2 = ((bf16[8,256,128]{2,1,0:T(8,128)(2,1)}), bf16[8,256,128]{2,1,0:T(8,128)(2,1)S(1)}, u32[]{:S(2)}, u32[]{:S(2)}) async-start(bf16[8,256,128]{2,1,0:T(8,128)(2,1)} %shard_map.157), calls=%async_computation.2 | async-start | bytes 1048576 | tf_op jit(solution)/shard_map/all_to_all | solution.py:389
  94.2 15.5 %collective-permute-start.24 = (bf16[512,128]{1,0:T(8,128)(2,1)}, bf16[512,128]{1,0:T(8,128)(2,1)S(1)}, u32[]{:S(2)}, u32[]{:S(2)}) collective-permute-start(bf16[512,128]{1,0:T(8,128)(2,1)} %get-tuple-element.66), channel_id=1, source_target_pairs={{0,0},{4,1},{8,2},{12,3},{16,20},{20,21},{24,22},{28,23},{1,8},{5,... | collective-permute-start | bytes 393224 | tf_op jit(solution)/shard_map/ppermute | solution.py:380
  96.3 19.1 %collective-permute-start.25 = (bf16[512,128]{1,0:T(8,128)(2,1)}, bf16[512,128]{1,0:T(8,128)(2,1)S(1)}, u32[]{:S(2)}, u32[]{:S(2)}) collective-permute-start(bf16[512,128]{1,0:T(8,128)(2,1)} %get-tuple-element.67), channel_id=1, source_target_pairs={{0,1},{4,0},{8,3},{12,2},{16,21},{20,20},{24,23},{28,22},{1,9},{5,... | collective-permute-start | bytes 393224 | tf_op jit(solution)/shard_map/ppermute | solution.py:380
  100.2 18.2 %collective-permute-start.26 = (bf16[512,128]{1,0:T(8,128)(2,1)}, bf16[512,128]{1,0:T(8,128)(2,1)S(1)}, u32[]{:S(2)}, u32[]{:S(2)}) collective-permute-start(bf16[512,128]{1,0:T(8,128)(2,1)} %get-tuple-element.68), channel_id=1, source_target_pairs={{0,2},{4,3},{8,0},{12,1},{16,22},{20,23},{24,20},{28,21},{1,10},{5... | collective-permute-start | bytes 393224 | tf_op jit(solution)/shard_map/ppermute | solution.py:380
  106.2 13.4 %collective-permute-start.27 = (bf16[512,128]{1,0:T(8,128)(2,1)}, bf16[512,128]{1,0:T(8,128)(2,1)S(1)}, u32[]{:S(2)}, u32[]{:S(2)}) collective-permute-start(bf16[512,128]{1,0:T(8,128)(2,1)} %copy-done.10), channel_id=1, source_target_pairs={{0,3},{4,2},{8,1},{12,0},{16,23},{20,22},{24,21},{28,20},{1,11},{5... | collective-permute-start | bytes 393224 | tf_op jit(solution)/shard_map/ppermute | solution.py:380
  107.8 16.4 %collective-permute-start.31 = (bf16[512,128]{1,0:T(8,128)(2,1)}, bf16[512,128]{1,0:T(8,128)(2,1)}, u32[]{:S(2)}, u32[]{:S(2)}) collective-permute-start(bf16[512,128]{1,0:T(8,128)(2,1)} %copy-done.9), channel_id=1, source_target_pairs={{0,0},{4,1},{8,2},{12,3},{16,20},{20,21},{24,22},{28,23},{1,8},{5,... | collective-permute-start | bytes 393224 | tf_op jit(solution)/shard_map/ppermute | solution.py:370
  109.7 15.3 %collective-permute-start.32 = (bf16[512,128]{1,0:T(8,128)(2,1)S(1)}, bf16[512,128]{1,0:T(8,128)(2,1)}, u32[]{:S(2)}, u32[]{:S(2)}) collective-permute-start(bf16[512,128]{1,0:T(8,128)(2,1)S(1)} %get-tuple-element.63), channel_id=1, source_target_pairs={{0,1},{4,0},{8,3},{12,2},{16,21},{20,20},{24,23},{28,22},{1,9},{5,... | collective-permute-start | bytes 393224 | tf_op jit(solution)/shard_map/ppermute | solution.py:370
  115.5 9.9 %collective-permute-start.33 = (bf16[512,128]{1,0:T(8,128)(2,1)S(1)}, bf16[512,128]{1,0:T(8,128)(2,1)}, u32[]{:S(2)}, u32[]{:S(2)}) collective-permute-start(bf16[512,128]{1,0:T(8,128)(2,1)S(1)} %get-tuple-element.64), channel_id=1, source_target_pairs={{0,2},{4,3},{8,0},{12,1},{16,22},{20,23},{24,20},{28,21},{1,10},{5... | collective-permute-start | bytes 393224 | tf_op jit(solution)/shard_map/ppermute | solution.py:370
  118.3 7.1 %collective-permute-start.34 = (bf16[512,128]{1,0:T(8,128)(2,1)S(1)}, bf16[512,128]{1,0:T(8,128)(2,1)}, u32[]{:S(2)}, u32[]{:S(2)}) collective-permute-start(bf16[512,128]{1,0:T(8,128)(2,1)S(1)} %get-tuple-element.65), channel_id=1, source_target_pairs={{0,3},{4,2},{8,1},{12,0},{16,23},{20,22},{24,21},{28,20},{1,11},{5... | collective-permute-start | bytes 393224 | tf_op jit(solution)/shard_map/ppermute | solution.py:370
  121.4 7.9 %collective-permute-start.28 = (bf16[512,128]{1,0:T(8,128)(2,1)S(1)}, bf16[512,128]{1,0:T(8,128)(2,1)S(1)}, u32[]{:S(2)}, u32[]{:S(2)}) collective-permute-start(bf16[512,128]{1,0:T(8,128)(2,1)S(1)} %get-tuple-element.73), channel_id=1, source_target_pairs={{0,1},{1,0},{2,3},{3,2},{4,5},{5,4},{6,7},{7,6},{8,9},{9,8},{10,11... | collective-permute-start | bytes 393224 | tf_op jit(solution)/shard_map/ppermute | solution.py:80
  124.1 5.2 %collective-permute-start.29 = (bf16[512,128]{1,0:T(8,128)(2,1)S(1)}, bf16[512,128]{1,0:T(8,128)(2,1)S(1)}, u32[]{:S(2)}, u32[]{:S(2)}) collective-permute-start(bf16[512,128]{1,0:T(8,128)(2,1)S(1)} %get-tuple-element.74), channel_id=1, source_target_pairs={{0,2},{1,3},{2,0},{3,1},{4,6},{5,7},{6,4},{7,5},{8,10},{9,11},{10,... | collective-permute-start | bytes 393224 | tf_op jit(solution)/shard_map/ppermute | solution.py:80
  125.0 17.9 %collective-permute-start.30 = (bf16[512,128]{1,0:T(8,128)(2,1)S(1)}, bf16[512,128]{1,0:T(8,128)(2,1)S(1)}, u32[]{:S(2)}, u32[]{:S(2)}) collective-permute-start(bf16[512,128]{1,0:T(8,128)(2,1)S(1)} %get-tuple-element.75), channel_id=1, source_target_pairs={{0,3},{1,2},{2,1},{3,0},{4,7},{5,6},{6,5},{7,4},{8,11},{9,10},{10,... | collective-permute-start | bytes 393224 | tf_op jit(solution)/shard_map/ppermute | solution.py:80
  (22 other events, 191.0 us)

commit v3 on v1

v3 whole, which is shorter than its diff:
```python
import functools

import jax
import jax.numpy as jnp
from jax import lax
from jax.experimental import pallas as pl
from jax.experimental.pallas import tpu as pltpu
from jax.sharding import PartitionSpec as P

NB = 16
SLOTS = 8
CAP = 256
LANES = 128
DIGIT = 64
ID_ROWS = 16
BF = jnp.bfloat16
F32 = jnp.float32
VMEM_LIMIT = 40 * 1024 * 1024


def silu(v):
    return v / (1.0 + jnp.exp(-v))


def dot(a, b):
    return jnp.dot(a, b, preferred_element_type=F32)


def dot_t(a, b):
    return lax.dot_general(a, b, (((1,), (1,)), ((), ())), preferred_element_type=F32)


def call(kernel, out_shapes, info, args, scratch=(), grid=(1,), in_specs=None, out_specs=None, flops=0, moved=0, vmem=VMEM_LIMIT):
    whole = lambda s: pl.BlockSpec(s.shape, functools.partial(lambda n, *_: (0,) * n, len(s.shape)))
    in_specs = [whole(a) if in_specs is None or in_specs[i] is None else in_specs[i] for i, a in enumerate(args)]
    out_specs = [
        whole(o) if out_specs is None or out_specs[i] is None else out_specs[i] for i, o in enumerate(out_shapes)
    ]
    return pl.pallas_call(
        kernel,
        out_shape=list(out_shapes),
        grid_spec=pltpu.PrefetchScalarGridSpec(
            num_scalar_prefetch=1, grid=grid, in_specs=in_specs, out_specs=out_specs, scratch_shapes=list(scratch)
        ),
        compiler_params=pltpu.CompilerParams(vmem_limit_bytes=vmem),
        cost_estimate=pl.CostEstimate(flops=int(flops), bytes_accessed=moved, transcendentals=0),
    )(info, *args)


def sds(shape, dtype=BF):
    return jax.ShapeDtypeStruct(tuple(shape), dtype)


def block_rows(i):
    return pl.ds(pl.multiple_of(i * CAP, CAP), CAP)


def lanes(i, width):
    return pl.ds(pl.multiple_of(i * width, width), width)


def column(row):
    wide = jnp.broadcast_to(row.astype(F32), (8, row.shape[1]))
    return jnp.transpose(wide)[:, :1].astype(jnp.int32)


def solution(mesh):
    G = mesh.shape["graph"]
    M = mesh.shape["mp"]
    per = G // M
    both = ("graph", "mp")

    def over_mp(x, k):
        return lax.ppermute(x, "mp", [(i, i ^ k) for i in range(M)])

    def over_plane(x, k):
        return lax.ppermute(x, "graph", [(i, i ^ k) for i in range(G)])

    def at(plane, slot):
        return slot * M + plane

    devices = [(s, i, z) for s in range(per) for i in range(M) for z in range(M)]

    def home(x, r):
        return lax.ppermute(x, both, [(at(i, s) * M + z, at(z, s) * M + (i ^ r)) for s, i, z in devices])

    def away(x, r):
        return lax.ppermute(x, both, [(at(j, s) * M + m, at(m ^ r, s) * M + j) for s, j, m in devices])

    def split(info, ef, wm, wa, we, wu, *refs):
        g, m = info[0], info[1]
        outs, share, sem = refs[:M], refs[M], refs[M + 1]
        moves = []
        for k in range(M):
            for s in range(per):
                moves.append((ef.at[block_rows(at(m ^ k, s)), :], outs[k].at[s * CAP : (s + 1) * CAP, :]))
        start = 0
        for w in (wm, wa, we):
            n = w.shape[0] // G
            moves.append((w.at[pl.ds(pl.multiple_of(g * n, n), n), :], share.at[start : start + n, :]))
            start += n
        moves.append((wu, share.at[start:, :]))
        copies = [pltpu.make_async_copy(src, dst, sem.at[i]) for i, (src, dst) in enumerate(moves)]
        for c in copies:
            c.start()
        for c in copies:
            c.wait()

    def stack(info, *refs):
        parts, outs = refs[:M], refs[M:]
        n = outs[0].shape[1]
        for j, out in enumerate(outs):
            for k in range(M):
                out[k] = parts[k][j * n : (j + 1) * n, :]

    def digits(ids):
        high = lax.div(ids, DIGIT)
        return high.astype(F32), (ids - high * DIGIT).astype(F32)

    def quarters(info, af, src, *outs):
        m, atoms = info[1], info[2]
        part = outs[1].shape[0]
        for r in range(M):
            outs[r][:part, :] = af[pl.ds(pl.multiple_of((m ^ r) * part, part), part), :]
        high, low = digits(lax.rem(src[...], atoms))
        lines = [x[:, c : c + LANES] for x in (high, low) for c in range(0, CAP, LANES)]
        outs[0][part:, :] = jnp.concatenate(lines, axis=0).astype(BF)

    def triplets(info, *refs):
        m = info[1]
        xs, (partner, mask, basis, wdt, wbt, x_out, bil_out, mixed) = refs[:M], refs[M:]
        w = xs[0].shape[1]
        for k in range(M):
            x_out[:, lanes(m ^ k, w)] = xs[k][...]
        downt = dot_t(wdt[...], x_out[...]).astype(BF)
        dt = downt.shape[0]
        ids = lax.rem(partner[...], CAP)
        rows = lax.broadcasted_iota(jnp.int32, (CAP, CAP), 0)
        picked = []
        for s in range(SLOTS):
            onehot = (rows == ids[s : s + 1, :]).astype(F32).astype(BF)
            picked.append(dot(downt, onehot))
        basist = jnp.transpose(basis[...].astype(F32))
        maskf = mask[...].astype(F32)
        weight = [basist[s * NB : (s + 1) * NB, :] * maskf[s : s + 1, :] for s in range(SLOTS)]
        for b in range(NB):
            acc = weight[0][b : b + 1, :] * picked[0]
            for s in range(1, SLOTS):
                acc = acc + weight[s][b : b + 1, :] * picked[s]
            mixed[b * dt : (b + 1) * dt, :] = acc.astype(BF)
        bilt = dot(wbt[...], mixed[...])
        bil_out[...] = jnp.transpose(bilt).astype(BF)

    def put_weights(m, shares, dst):
        n, width = shares.shape[1] // M, shares.shape[2]

        def put(g, _):
            for k in range(M):
                dst[pl.ds(pl.multiple_of(g * n, n), n), lanes(m ^ k, width)] = shares[g, k * n : (k + 1) * n, :]
            return 0

        lax.fori_loop(0, G, put, 0, unroll=G <= 8)

    def messages(info, *refs):
        m, atoms = info[1], info[2]
        up, (shares, ride, x, bil, live, tgt, total_out, out, wm, wu) = refs[:M], refs[M:]
        width = out.shape[3]
        first = out.shape[2] - CAP - ID_ROWS
        dt = wu.shape[0]

        @pl.when(pl.program_id(0) == 0)
        def _():
            put_weights(m, shares, wm)
            for k in range(M):
                wu[:, lanes(m ^ k, width)] = up[k][up[k].shape[0] - dt :, :]

        hid = dot(x[...], wm[...])
        total = x[...].astype(F32) + silu(hid) + dot(bil[...], wu[...])
        total_out[...] = total
        block = pl.ds(at(m, pl.program_id(0)), 1)
        sent = (total * column(live[block, :]).astype(F32)).astype(BF)
        lines = [x[:, c : c + LANES] for x in digits(lax.rem(tgt[block, :], atoms)) for c in range(0, CAP, LANES)]
        lines.append(jnp.zeros((ID_ROWS - len(lines), LANES), F32))
        lines = jnp.concatenate(lines, axis=0).astype(BF)
        for f in range(M):
            for j in range(M // 2):
                out[0, f, j * ride.shape[1] : (j + 1) * ride.shape[1], :] = ride[f % 2 * (M // 2) + j]
            out[0, f, first : first + CAP, :] = sent[:, f * width : (f + 1) * width]
            out[0, f, first + CAP :, :] = lines

    def aggregate(info, incoming, *refs):
        f = info[0] % M
        outs, (ids, ride, onehot, values, agg) = refs[:M], refs[M:]
        part, width = outs[0].shape
        half = agg.shape[0] // 2
        step = onehot.shape[0]
        first = incoming.shape[1] - CAP - ID_ROWS
        low = lax.broadcasted_iota(jnp.int32, (LANES, CAP), 0)

        def place(g, _):
            lines = incoming[g, first + CAP :, :].astype(F32)
            n = CAP // LANES
            high = jnp.concatenate([lines[c : c + 1, :] for c in range(n)], axis=1)
            row = high * DIGIT + jnp.concatenate([lines[n + c : n + c + 1, :] for c in range(n)], axis=1)
            ids[g] = row.astype(jnp.int32)
            ride[g] = incoming[g, :first, :]
            upper = (column(row) >= half).astype(F32)
            rows = incoming[g, first : first + CAP, :].astype(F32)
            values[block_rows(g), :width] = (rows * (1.0 - upper)).astype(BF)
            values[block_rows(g), width:] = (rows * upper).astype(BF)
            return 0

        lax.fori_loop(0, G, place, 0, unroll=G <= 8)
        for q in range(half // step):

            def fill(g, _):
                row = lax.rem(ids[g], half)
                near = (low == lax.rem(row, LANES)).astype(F32).astype(BF)
                far = jnp.broadcast_to(lax.div(row, LANES) - q * (step // LANES), (LANES, CAP)).astype(F32).astype(BF)
                for h in range(step // LANES):
                    onehot[h * LANES : (h + 1) * LANES, lanes(g, CAP)] = jnp.where(
                        far == BF(h), near, jnp.zeros_like(near)
                    )
                return 0

            lax.fori_loop(0, G, fill, 0, unroll=G <= 8)
            acc = dot(onehot[...], values[...]).astype(BF)
            agg[q * step : (q + 1) * step, :] = acc[:, :width]
            agg[half + q * step : half + (q + 1) * step, :] = acc[:, width:]
        for r in range(M):
            outs[r][...] = agg[pl.ds(pl.multiple_of((f ^ r) * part, part), part), :]

    def atom_layer(info, *refs):
        g, m = info[0], info[1]
        f = g % M
        sums, feats, halves = refs[:M], refs[M : 2 * M], refs[2 * M : 2 * M + 2]
        outs, (x, wa) = refs[2 * M + 2 : 3 * M + 2], refs[3 * M + 2 :]
        part, width = sums[0].shape
        for r in range(M):
            x[:, lanes(f ^ r, width)] = (feats[r][:part, :].astype(F32) + sums[r][...].astype(F32)).astype(BF)
        n = halves[0].shape[1] // (M // 2)

        def put(d, _):
            for core, half in ((g % 2, halves[0]), ((g + 1) % 2, halves[1])):
                for j in range(M // 2):
                    cols = lanes(m ^ (core * (M // 2) + j), width)
                    wa[pl.ds(pl.multiple_of(d * n, n), n), cols] = half[d, j * n : (j + 1) * n, :]
            return 0

        lax.fori_loop(0, G, put, 0, unroll=G <= 8)
        ahid = dot(x[...], wa[...])
        x[...] = (x[...].astype(F32) + silu(ahid)).astype(BF)
        for r in range(M):
            outs[r][...] = x[:, lanes(f ^ r, width)]

    def gather(info, *refs):
        f = info[0] % M
        parts, ids, sent, ride = refs[:M], refs[M], refs[M + 1], refs[M + 2]
        srcs, tgt, (table, onehot, src) = refs[M + 3 : 2 * M + 3], refs[2 * M + 3], refs[2 * M + 4 :]
        part, width = parts[0].shape
        half = table.shape[0]
        share = ride.shape[1]
        for r in range(M):
            q = f ^ r
            per_half = half // part
            rows = pl.ds(pl.multiple_of(lax.rem(q, per_half) * part, part), part)
            table[rows, lanes(lax.div(q, per_half), width)] = parts[r][...]

        def mark(row, line):
            col = column(row)
            upper = col >= half
            col = lax.rem(col, half)
            near = (lax.broadcasted_iota(jnp.int32, (CAP, LANES), 1) == lax.rem(col, LANES)).astype(F32).astype(BF)
            far = jnp.broadcast_to(lax.div(col, LANES), (CAP, LANES)).astype(F32).astype(BF)
            for h in range(half // LANES):
                onehot[line * CAP : (line + 1) * CAP, h * LANES : (h + 1) * LANES] = jnp.where(
                    far == BF(h), near, jnp.zeros_like(near)
                )
            return upper

        def pick(line, upper):
            found = dot(onehot[line * CAP : (line + 1) * CAP, :], table[...])
            return jnp.where(upper, found[:, width:], found[:, :width]).astype(BF)

        lines = sent[part:, :].astype(F32)
        n = CAP // LANES
        high = jnp.concatenate([lines[c * G : (c + 1) * G, :] for c in range(n)], axis=1)
        low = jnp.concatenate([lines[(n + c) * G : (n + c + 1) * G, :] for c in range(n)], axis=1)
        src[...] = (high * DIGIT + low).astype(jnp.int32)
        group = onehot.shape[0] // CAP
        places = [(r, s) for r in range(M) for s in range(per)]
        for start in range(0, G, group):
            now = places[start : start + group]
            upper = [mark(src[pl.ds(at(f ^ r, s), 1), :], j) for j, (r, s) in enumerate(now)]
            for j, (r, s) in enumerate(now):
                srcs[r][s * CAP : (s + 1) * CAP, :] = pick(j, upper[j])

        def several(b, _):
            upper = [mark(ids[b * group + j], j) for j in range(group)]
            for j in range(group):
                tgt[b * group + j, :CAP, :] = pick(j, upper[j])
                for k in range(M):
                    tgt[b * group + j, CAP + k * share : CAP + (k + 1) * share, :] = ride[k]
            return 0

        lax.fori_loop(0, G // group, several, 0, unroll=True)

    def edges(info, *refs):
        m = info[1]
        srcs, (shares, tgt, total) = refs[:M], refs[M : M + 3]
        outs, (x, we) = refs[M + 3 : 2 * M + 3], refs[2 * M + 3 :]
        width = srcs[0].shape[1]

        @pl.when(pl.program_id(0) == 0)
        def _():
            put_weights(m, shares, we)

        for r in range(M):
            f = m ^ r
            x[:, lanes(f, width)] = (srcs[r][...].astype(F32) * tgt[0, f].astype(F32)).astype(BF)
        ehid = dot(x[...], we[...])
        x[...] = (total[...] + silu(ehid)).astype(BF)
        for k in range(M):
            outs[k][...] = x[:, lanes(m ^ k, width)]

    def assemble(info, *refs):
        m = info[1]
        parts, out = refs[:M], refs[M]
        for k in range(M):
            for s in range(per):
                out[block_rows(at(m ^ k, s)), :] = parts[k][s * CAP : (s + 1) * CAP, :]

    def assemble_atoms(info, *refs):
        m = info[1]
        parts, out = refs[:M], refs[M]
        part = parts[0].shape[0]
        for r in range(M):
            out[pl.ds(pl.multiple_of((m ^ r) * part, part), part), :] = parts[r][...]

    def local(ef, esrc, etgt, live, partner, mask, basis, af, w_msg, w_down, w_bil, w_up, w_atom, w_edge):
        rows, width = ef.shape
        atoms = af.shape[0]
        depth = w_msg.shape[0]
        dt = w_down.shape[1]
        chunk = per * CAP
        part = atoms // M
        g = lax.axis_index("graph")
        m = lax.axis_index("mp")
        info = jnp.stack([g, m, jnp.int32(atoms)]).astype(jnp.int32)
        share = depth // G
        *chunks, w = call(
            split,
            [sds((chunk, width))] * M + [sds((3 * share + dt, width))],
            info,
            [ef, w_msg, w_atom, w_edge, w_up],
            scratch=[pltpu.SemaphoreType.DMA((M * per + 4,))],
            in_specs=[pl.BlockSpec(memory_space=pl.ANY)] * 5,
            vmem=60 * 1024 * 1024,
        )
        ws = [w] + [over_mp(w, k) for k in range(1, M)]
        xs = [chunks[0]] + [over_mp(chunks[k], k) for k in range(1, M)]
        feats = call(
            quarters,
            [sds((part + 2 * rows // LANES, width))] + [sds((part, width))] * (M - 1),
            info,
            [af, esrc.reshape(G, CAP)],
            flops=0.5e9,
        )
        wm, wa, we = call(stack, [sds((M, share, width))] * 3, info, ws)
        wm = lax.all_gather(wm, "graph", axis=0)

        blk = lambda i, info: at(info[1], i)
        x, bil = call(
            triplets,
            [sds((chunk, depth)), sds((chunk, dt))],
            info,
            xs + [partner, mask, basis, w_down.T, w_bil.T],
            scratch=[pltpu.VMEM((NB * dt, CAP), BF)],
            grid=(per,),
            in_specs=[pl.BlockSpec((CAP, width), lambda i, info: (i, 0))] * M
            + [pl.BlockSpec((SLOTS, CAP), lambda i, info: (0, blk(i, info)))] * 2
            + [pl.BlockSpec((CAP, SLOTS * NB), lambda i, info: (blk(i, info), 0)), None, None],
            out_specs=[
                pl.BlockSpec((CAP, depth), lambda i, info: (i, 0)),
                pl.BlockSpec((CAP, dt), lambda i, info: (i, 0)),
            ],
        )
        total, outgoing = call(
            messages,
            [sds((chunk, depth), F32), sds((per, M, M // 2 * share + CAP + ID_ROWS, width))],
            info,
            ws + [wm.reshape(G, M * share, width), wa, x, bil, live.reshape(G, CAP), etgt.reshape(G, CAP)],
            scratch=[pltpu.VMEM((depth, depth), BF), pltpu.VMEM((dt, depth), BF)],
            grid=(per,),
            in_specs=[None] * (M + 2)
            + [
                pl.BlockSpec((CAP, depth), lambda i, info: (i, 0)),
                pl.BlockSpec((CAP, dt), lambda i, info: (i, 0)),
                None,
                None,
            ],
            out_specs=[
                pl.BlockSpec((CAP, depth), lambda i, info: (i, 0)),
                pl.BlockSpec((1, M, M // 2 * share + CAP + ID_ROWS, width), lambda i, info: (i, 0, 0, 0)),
            ],
        )
        incoming = lax.all_to_all(
            outgoing.reshape(G, M // 2 * share + CAP + ID_ROWS, width), "graph", split_axis=0, concat_axis=0, tiled=True
        )
        *feats, _ = lax.optimization_barrier((*feats, outgoing))
        feats = [away(feats[r], r) for r in range(M)]
        *sums, ids, wa = call(
            aggregate,
            [sds((part, width))] * M + [sds((G, 1, CAP), jnp.int32), sds((G, M // 2 * share, width))],
            info,
            [incoming],
            scratch=[pltpu.VMEM((part, G * CAP), BF), pltpu.VMEM((G * CAP, 2 * width), BF), pltpu.VMEM((atoms, width), BF)],
            flops=3.0e9,
        )
        sums = [sums[0]] + [over_plane(sums[r], r) for r in range(1, M)]
        outs = call(
            atom_layer,
            [sds((part, width))] * M,
            info,
            sums + feats + [wa, over_plane(wa, 1)],
            scratch=[pltpu.VMEM((part, depth), BF), pltpu.VMEM((depth, depth), BF)],
            flops=1.5e9,
        )
        homeward = [home(outs[r], r) for r in range(M)]
        outs = [outs[0]] + [over_plane(outs[r], r) for r in range(1, M)]
        *srcs, named = call(
            gather,
            [sds((chunk, width))] * M + [sds((G, CAP + M * share, width))],
            info,
            outs + [ids, feats[0], we],
            scratch=[
                pltpu.VMEM((atoms // 2, 2 * width), BF),
                pltpu.VMEM((min(G, 8) * CAP, atoms // 2), BF),
                pltpu.VMEM((G, CAP), jnp.int32),
            ],
            flops=6.0e9,
        )
        srcs = [home(srcs[r], r) for r in range(M)]
        *homeward, named = lax.optimization_barrier((*homeward, named))
        tgt = lax.all_to_all(named, "graph", split_axis=0, concat_axis=0, tiled=True)
        outs = call(
            edges,
            [sds((chunk, width))] * M,
            info,
            srcs + [tgt, tgt.reshape(per, M, CAP + M * share, width), total],
            scratch=[pltpu.VMEM((CAP, depth), BF), pltpu.VMEM((depth, depth), BF)],
            grid=(per,),
            in_specs=[pl.BlockSpec((CAP, width), lambda i, info: (i, 0))] * M
            + [
                pl.BlockSpec((G, M * share, width), lambda i, info: (0, CAP // (M * share), 0)),
                pl.BlockSpec((1, M, CAP, width), lambda i, info: (i, 0, 0, 0)),
                pl.BlockSpec((CAP, depth), lambda i, info: (i, 0)),
            ],
            out_specs=[pl.BlockSpec((CAP, width), lambda i, info: (i, 0))] * M,
        )
        outs = [outs[0]] + [over_mp(outs[k], k) for k in range(1, M)]
        (atom_out,) = call(assemble_atoms, [sds((atoms, width))], info, homeward, flops=1.0e9)
        (edge_out,) = call(assemble, [sds((rows, width))], info, list(outs), flops=1.0e9)
        return (edge_out, atom_out)

    return jax.shard_map(
        local,
        mesh=mesh,
        in_specs=(
            P("graph", "mp"),
            P("graph"),
            P("graph"),
            P("graph"),
            P(None, "graph"),
            P(None, "graph"),
            P("graph", None),
            P("graph", "mp"),
            P(None, "mp"),
            P(),
            P(),
            P(None, "mp"),
            P(None, "mp"),
            P(None, "mp"),
        ),
        out_specs=(P("graph", "mp"), P("graph", "mp")),
        check_vma=False,
    )
```

time: 162 us -> 134 us (0.83)
  waiting for transfers between devices: 54.3 us -> 38.7 us
  starting transfers between devices: 70.6 us -> 57.6 us
  blocking collectives: 0 us -> 10.3 us
  local copies, waits for them, and re-layouts: 9.8 us -> 1.52 us
    ppermute x12 -> x9, waiting for transfers between devices: 30.2 us -> 8.13 us  [over_mp(): return lax.ppermute(x, 'mp', [(i, i ^ k) for i in range(M)])]
    ppermute x12 -> x9, starting transfers between devices: 31.6 us -> 16.5 us  [over_mp(): return lax.ppermute(x, 'mp', [(i, i ^ k) for i in range(M)])]
    all_gather x0 -> x1, blocking collectives: none -> 10.3 us  [local(): wm = lax.all_gather(wm, 'graph', axis=0)]
    ppermute x14 -> x7, starting transfers between devices: 5.49 us -> 13.8 us  [over_plane(): return lax.ppermute(x, 'graph', [(i, i ^ k) for i in range(G)])]
    unnamed x35 -> x30, local copies, waits for them, and re-layouts: 9.79 us -> 1.51 us
    ppermute x6 -> x12, waiting for transfers between devices: 4.1 us -> 12.1 us  [the longest x8 12.1 us: home(): lax.ppermute(x, both, [(at(i, s) * M + z, at(z, s) * M + (i ^ r)) for s,...]
    all_to_all x2 -> x1, starting transfers between devices: 11.1 us -> 3.68 us  [local(): lax.all_to_all(outgoing.reshape(G, M // 2 * share + CAP + ID_ROWS, width)...]
    all_to_all x2 -> x1, waiting for transfers between devices: 5.24 us -> 8 us  [local(): lax.all_to_all(outgoing.reshape(G, M // 2 * share + CAP + ID_ROWS, width)...]
  transfers between devices with their start and end apart: 35 -> 30, of which waited for: 12 -> 9; matrix products, arithmetic and copies ran while one was open for 0% -> 0% of each run, Pallas kernels for 6% -> 8%
where the time goes in v3:
time: 134 us
  starting transfers between devices  57.6 us (43%)
  waiting for transfers between devices  38.7 us (29%)
  Pallas kernels  24 us (18%)
  blocking collectives  10.3 us (8%)
  local copies, waits for them, and re-layouts  1.52 us (1%)
    pallas_call x11, Pallas kernels, call(): pl.pallas_call(kernel, out_shape=list(out_shapes), grid_spec=pltpu.Prefet...  24 us
    ppermute x9, starting transfers between devices, over_mp(): return lax.ppermute(x, 'mp', [(i, i ^ k) for i in range(M)])  16.5 us
    ppermute x7, starting transfers between devices, over_plane(): return lax.ppermute(x, 'graph', [(i, i ^ k) for i in range(G)])  13.8 us
    ppermute x8, starting transfers between devices, home(): lax.ppermute(x, both, [(at(i, s) * M + z, at(z, s) * M + (i ^ r)) for s,...  12.4 us
    ppermute x8, waiting for transfers between devices, home(): lax.ppermute(x, both, [(at(i, s) * M + z, at(z, s) * M + (i ^ r)) for s,...  12.1 us
    ppermute x7, waiting for transfers between devices, over_plane(): return lax.ppermute(x, 'graph', [(i, i ^ k) for i in range(G)])  10.4 us
    all_gather x1, blocking collectives, local(): wm = lax.all_gather(wm, 'graph', axis=0)  10.3 us
    ppermute x9, waiting for transfers between devices, over_mp(): return lax.ppermute(x, 'mp', [(i, i ^ k) for i in range(M)])  8.13 us
  transfers between devices with their start and end apart: 30, of which 9 were waited for; matrix products, arithmetic and copies ran while one was open for 0% of the time, Pallas kernels for 8%

profile of v3, /device:TPU:0, one launch (start us, length us, event | category | flops | bytes accessed | tf_op | source)
XLA Modules:
  0.0 133.6 jit_solution(3961738318006181593)
XLA Ops:
  1.2 2.8 %shard_map.149 = (bf16[512,128]{1,0:T(8,128)(2,1)}, bf16[512,128]{1,0:T(8,128)(2,1)}, bf16[512,128]{1,0:T(8,128)(2,1)}, bf16[512,128]{1,0:T(8,128)(2,1)}, bf16[256,128]{1,0:T(8,128)(2,1)}) custom-call(s32[3]{0:T(128)} %pad_add_fusion.info, bf16[2048,128]{1,0:T(8,128)(2,1)} %ef.1, bf16[512,128]{1,0:T(8,128)(2,1)} %wm.1, bf16[512,128]{1,0:T(8,128)(2,1)} %wa.1, ...), custom_call_target="tpu_custom_call" | custom-call | tf_op jit(solution)/shard_map/pallas_call | solution.py:39
  4.0 5.1 %collective-permute-start.2 = (bf16[256,128]{1,0:T(8,128)(2,1)}, bf16[256,128]{1,0:T(8,128)(2,1)S(1)}, u32[]{:S(2)}, u32[]{:S(2)}) collective-permute-start(bf16[256,128]{1,0:T(8,128)(2,1)} %get-tuple-element.46.refs_0_), channel_id=1, source_target_pairs={{0,3},{1,2},{2,1},{3,0},{4,7},{5,6},{6,5},{7,4},{8,11},{9,10},{10,... | collective-permute-start | bytes 196616 | tf_op jit(solution)/shard_map/ppermute | solution.py:74
  9.8 1.4 %collective-permute-start.3 = (bf16[512,128]{1,0:T(8,128)(2,1)}, bf16[512,128]{1,0:T(8,128)(2,1)S(1)}, u32[]{:S(2)}, u32[]{:S(2)}) collective-permute-start(bf16[512,128]{1,0:T(8,128)(2,1)} %get-tuple-element.50), channel_id=1, source_target_pairs={{0,1},{1,0},{2,3},{3,2},{4,5},{5,4},{6,7},{7,6},{8,9},{9,8},{10,11... | collective-permute-start | bytes 393224 | tf_op jit(solution)/shard_map/ppermute | solution.py:74
  11.2 2.9 %collective-permute-start.4 = (bf16[512,128]{1,0:T(8,128)(2,1)}, bf16[512,128]{1,0:T(8,128)(2,1)S(1)}, u32[]{:S(2)}, u32[]{:S(2)}) collective-permute-start(bf16[512,128]{1,0:T(8,128)(2,1)} %get-tuple-element.51), channel_id=1, source_target_pairs={{0,2},{1,3},{2,0},{3,1},{4,6},{5,7},{6,4},{7,5},{8,10},{9,11},{10,... | collective-permute-start | bytes 393224 | tf_op jit(solution)/shard_map/ppermute | solution.py:74
  14.1 2.0 %collective-permute-start.5 = (bf16[512,128]{1,0:T(8,128)(2,1)}, bf16[512,128]{1,0:T(8,128)(2,1)S(1)}, u32[]{:S(2)}, u32[]{:S(2)}) collective-permute-start(bf16[512,128]{1,0:T(8,128)(2,1)} %get-tuple-element.52), channel_id=1, source_target_pairs={{0,3},{1,2},{2,1},{3,0},{4,7},{5,6},{6,5},{7,4},{8,11},{9,10},{10,... | collective-permute-start | bytes 393224 | tf_op jit(solution)/shard_map/ppermute | solution.py:74
  19.1 10.3 %all-gather = bf16[32,64,128]{2,1,0:T(8,128)(2,1)S(1)} all-gather(bf16[4,64,128]{2,1,0:T(8,128)(2,1)S(1)} %get-tuple-element.47), channel_id=2, replica_groups=mesh['graph'=8,'mp'=4] {'graph'}, dimensions={0}, use_global_device_ids=true | all-gather | bytes 589824 | tf_op jit(solution)/shard_map/all_gather | solution.py:370
  29.5 3.1 %shard_map.151 = (bf16[512,512]{1,0:T(8,128)(2,1)S(1)}, bf16[512,64]{1,0:T(8,128)(2,1)S(1)}) custom-call(s32[3]{0:T(128)S(1)} %copy-done.8, bf16[512,128]{1,0:T(8,128)(2,1)S(1)} %copy-done.4, bf16[512,128]{1,0:T(8,128)(2,1)S(1)} %collective-permute-done.3.refs_1_, bf16[512,128]{1,0:T(8,128)(2,1)S(1)} %collective-permute-done.4.refs_2_, ...), custom_call_target="tpu_custom_call" | custom-call | tf_op jit(solution)/shard_map/pallas_call | solution.py:39
  32.6 2.5 %shard_map.152 = (f32[512,512]{1,0:T(8,128)S(1)}, bf16[2,4,400,128]{3,2,1,0:T(8,128)(2,1)}) custom-call(s32[3]{0:T(128)S(1)} %copy-done.8, bf16[256,128]{1,0:T(8,128)(2,1)S(1)} %copy-done.2, bf16[256,128]{1,0:T(8,128)(2,1)S(1)} %collective-permute-done.refs_1_, bf16[256,128]{1,0:T(8,128)(2,1)S(1)} %collective-permute-done.1.refs_2_, ...), custom_call_target="tpu_custom_call" | custom-call | tf_op jit(solution)/shard_map/pallas_call | solution.py:39
  35.1 3.7 %all-to-all-start = ((bf16[8,400,128]{2,1,0:T(8,128)(2,1)}), bf16[8,400,128]{2,1,0:T(8,128)(2,1)S(1)}, u32[]{:S(2)}, u32[]{:S(2)}) async-start(bf16[8,400,128]{2,1,0:T(8,128)(2,1)} %bitcast.5), calls=%async_computation | async-start | bytes 1638400 | tf_op jit(solution)/shard_map/all_to_all | solution.py:407
  40.0 1.8 %collective-permute-start.11 = (bf16[512,128]{1,0:T(8,128)(2,1)S(1)}, bf16[512,128]{1,0:T(8,128)(2,1)S(1)}, u32[]{:S(2)}, u32[]{:S(2)}) collective-permute-start(bf16[512,128]{1,0:T(8,128)(2,1)S(1)} %get-tuple-element.66), channel_id=1, source_target_pairs={{0,8},{1,12},{2,0},{3,4},{4,9},{5,13},{6,1},{7,5},{8,10},{9,14},{1... | collective-permute-start | bytes 393224 | tf_op jit(solution)/shard_map/ppermute | solution.py:88
  41.8 2.4 %collective-permute-start.12 = (bf16[512,128]{1,0:T(8,128)(2,1)S(1)}, bf16[512,128]{1,0:T(8,128)(2,1)S(1)}, u32[]{:S(2)}, u32[]{:S(2)}) collective-permute-start(bf16[512,128]{1,0:T(8,128)(2,1)S(1)} %get-tuple-element.67), channel_id=1, source_target_pairs={{0,12},{1,8},{2,4},{3,0},{4,13},{5,9},{6,5},{7,1},{8,14},{9,10},{1... | collective-permute-start | bytes 393224 | tf_op jit(solution)/shard_map/ppermute | solution.py:88
  44.2 8.0 %all-to-all-done.incoming = bf16[8,400,128]{2,1,0:T(8,128)(2,1)S(1)} async-done(((bf16[8,400,128]{2,1,0:T(8,128)(2,1)}), bf16[8,400,128]{2,1,0:T(8,128)(2,1)S(1)}, u32[]{:S(2)}, u32[]{:S(2)}) %all-to-all-start) | async-done | bytes 819232 | tf_op jit(solution)/shard_map/all_to_all | solution.py:407
  52.2 2.4 %shard_map.153 = (bf16[512,128]{1,0:T(8,128)(2,1)S(1)}, bf16[512,128]{1,0:T(8,128)(2,1)S(1)}, bf16[512,128]{1,0:T(8,128)(2,1)S(1)}, bf16[512,128]{1,0:T(8,128)(2...) custom-call(s32[3]{0:T(128)S(1)} %copy-done.8, bf16[8,400,128]{2,1,0:T(8,128)(2,1)S(1)} %all-to-all-done.incoming), custom_call_target="tpu_custom_call" | custom-call | flops 3000000000 | tf_op jit(solution)/shard_map/pallas_call | solution.py:39
  55.4 3.6 %collective-permute-start.6 = (bf16[512,128]{1,0:T(8,128)(2,1)S(1)}, bf16[512,128]{1,0:T(8,128)(2,1)S(1)}, u32[]{:S(2)}, u32[]{:S(2)}) collective-permute-start(bf16[512,128]{1,0:T(8,128)(2,1)S(1)} %get-tuple-element.57), channel_id=1, source_target_pairs={{0,4},{4,0},{8,12},{12,8},{16,20},{20,16},{24,28},{28,24},{1,5},{5... | collective-permute-start | bytes 393224 | tf_op jit(solution)/shard_map/ppermute | solution.py:77
  59.0 7.8 %collective-permute-start.7 = (bf16[512,128]{1,0:T(8,128)(2,1)S(1)}, bf16[512,128]{1,0:T(8,128)(2,1)S(1)}, u32[]{:S(2)}, u32[]{:S(2)}) collective-permute-start(bf16[512,128]{1,0:T(8,128)(2,1)S(1)} %get-tuple-element.58), channel_id=1, source_target_pairs={{0,8},{4,12},{8,0},{12,4},{16,24},{20,28},{24,16},{28,20},{1,9},{5... | collective-permute-start | bytes 393224 | tf_op jit(solution)/shard_map/ppermute | solution.py:77
  66.8 4.5 %collective-permute-done.7.refs_2_ = bf16[512,128]{1,0:T(8,128)(2,1)S(1)} collective-permute-done((bf16[512,128]{1,0:T(8,128)(2,1)S(1)}, bf16[512,128]{1,0:T(8,128)(2,1)S(1)}, u32[]{:S(2)}, u32[]{:S(2)}) %collective-permute-start.7) | collective-permute-done | bytes 131104 | tf_op jit(solution)/shard_map/ppermute | solution.py:77
  71.3 2.4 %collective-permute-done.8.refs_3_ = bf16[512,128]{1,0:T(8,128)(2,1)S(1)} collective-permute-done((bf16[512,128]{1,0:T(8,128)(2,1)S(1)}, bf16[512,128]{1,0:T(8,128)(2,1)S(1)}, u32[]{:S(2)}, u32[]{:S(2)}) %collective-permute-start.8) | collective-permute-done | bytes 131104 | tf_op jit(solution)/shard_map/ppermute | solution.py:77
  73.7 1.5 %shard_map.155 = (bf16[512,128]{1,0:T(8,128)(2,1)S(1)}, bf16[512,128]{1,0:T(8,128)(2,1)S(1)}, bf16[512,128]{1,0:T(8,128)(2,1)S(1)}, bf16[512,128]{1,0:T(8,128)(2,1)S(1)}) custom-call(s32[3]{0:T(128)S(1)} %copy-done.8, bf16[512,128]{1,0:T(8,128)(2,1)S(1)} %get-tuple-element.56.refs_0_, bf16[512,128]{1,0:T(8,128)(2,1)S(1)} %collective-permute-done.6.refs_1_, ...), custom_call_target="tpu_custom_call" | custom-call | flops 1500000000 | tf_op jit(solution)/shard_map/pallas_call | solution.py:39
  75.3 2.3 %collective-permute-start.15 = (bf16[512,128]{1,0:T(8,128)(2,1)S(1)}, bf16[512,128]{1,0:T(8,128)(2,1)S(1)}, u32[]{:S(2)}, u32[]{:S(2)}) collective-permute-start(bf16[512,128]{1,0:T(8,128)(2,1)S(1)} %get-tuple-element.71), channel_id=1, source_target_pairs={{0,8},{4,12},{8,0},{12,4},{16,24},{20,28},{24,16},{28,20},{1,9},{5... | collective-permute-start | bytes 393224 | tf_op jit(solution)/shard_map/ppermute | solution.py:77
  77.7 2.5 %collective-permute-start.23 = (bf16[512,128]{1,0:T(8,128)(2,1)S(1)}, bf16[512,128]{1,0:T(8,128)(2,1)S(1)}, u32[]{:S(2)}, u32[]{:S(2)}) collective-permute-start(bf16[512,128]{1,0:T(8,128)(2,1)S(1)} %get-tuple-element.71), channel_id=1, source_target_pairs={{0,2},{1,6},{2,10},{3,14},{4,3},{5,7},{6,11},{7,15},{8,0},{9,4},{1... | collective-permute-start | bytes 393224 | tf_op jit(solution)/shard_map/ppermute | solution.py:85
  82.5 3.0 %collective-permute-done.16.refs_3_ = bf16[512,128]{1,0:T(8,128)(2,1)S(1)} collective-permute-done((bf16[512,128]{1,0:T(8,128)(2,1)S(1)}, bf16[512,128]{1,0:T(8,128)(2,1)S(1)}, u32[]{:S(2)}, u32[]{:S(2)}) %collective-permute-start.16) | collective-permute-done | bytes 131104 | tf_op jit(solution)/shard_map/ppermute | solution.py:77
  85.5 5.8 %shard_map.156 = (bf16[512,128]{1,0:T(8,128)(2,1)}, bf16[512,128]{1,0:T(8,128)(2,1)S(1)}, bf16[512,128]{1,0:T(8,128)(2,1)S(1)}, bf16[512,128]{1,0:T(8,128)(2,1)S(1)}, bf16[8,512,128]{2,1,0:T(8,128)(2,1)}) custom-call(s32[3]{0:T(128)S(1)} %copy-done.8, bf16[512,128]{1,0:T(8,128)(2,1)S(1)} %get-tuple-element.69.refs_0_, ...), custom_call_target="tpu_custom_call" | custom-call | flops 6000000000 | tf_op jit(solution)/shard_map/pallas_call | solution.py:39
  91.4 5.9 %all-to-all-start.1 = ((bf16[8,512,128]{2,1,0:T(8,128)(2,1)}), bf16[8,512,128]{2,1,0:T(8,128)(2,1)S(1)}, u32[]{:S(2)}, u32[]{:S(2)}) async-start(bf16[8,512,128]{2,1,0:T(8,128)(2,1)} %get-tuple-element.80), calls=%async_computation.1 | async-start | bytes 2097152 | tf_op jit(solution)/shard_map/all_to_all | solution.py:445
  97.2 1.6 %collective-permute-start.17 = (bf16[512,128]{1,0:T(8,128)(2,1)}, bf16[512,128]{1,0:T(8,128)(2,1)S(1)}, u32[]{:S(2)}, u32[]{:S(2)}) collective-permute-start(bf16[512,128]{1,0:T(8,128)(2,1)} %get-tuple-element.75), channel_id=1, source_target_pairs={{0,0},{1,4},{2,8},{3,12},{4,1},{5,5},{6,9},{7,13},{8,2},{9,6},{10,... | collective-permute-start | bytes 393224 | tf_op jit(solution)/shard_map/ppermute | solution.py:85
  98.8 2.5 %collective-permute-start.18 = (bf16[512,128]{1,0:T(8,128)(2,1)S(1)}, bf16[512,128]{1,0:T(8,128)(2,1)S(1)}, u32[]{:S(2)}, u32[]{:S(2)}) collective-permute-start(bf16[512,128]{1,0:T(8,128)(2,1)S(1)} %get-tuple-element.76), channel_id=1, source_target_pairs={{0,1},{1,5},{2,9},{3,13},{4,0},{5,4},{6,8},{7,12},{8,3},{9,7},{10,... | collective-permute-start | bytes 393224 | tf_op jit(solution)/shard_map/ppermute | solution.py:85
  101.3 2.5 %collective-permute-start.19 = (bf16[512,128]{1,0:T(8,128)(2,1)S(1)}, bf16[512,128]{1,0:T(8,128)(2,1)S(1)}, u32[]{:S(2)}, u32[]{:S(2)}) collective-permute-start(bf16[512,128]{1,0:T(8,128)(2,1)S(1)} %get-tuple-element.77), channel_id=1, source_target_pairs={{0,2},{1,6},{2,10},{3,14},{4,3},{5,7},{6,11},{7,15},{8,0},{9,4},{1... | collective-permute-start | bytes 393224 | tf_op jit(solution)/shard_map/ppermute | solution.py:85
  103.9 1.4 %collective-permute-start.20 = (bf16[512,128]{1,0:T(8,128)(2,1)S(1)}, bf16[512,128]{1,0:T(8,128)(2,1)S(1)}, u32[]{:S(2)}, u32[]{:S(2)}) collective-permute-start(bf16[512,128]{1,0:T(8,128)(2,1)S(1)} %get-tuple-element.78), channel_id=1, source_target_pairs={{0,3},{1,7},{2,11},{3,15},{4,2},{5,6},{6,10},{7,14},{8,1},{9,5},{1... | collective-permute-start | bytes 393224 | tf_op jit(solution)/shard_map/ppermute | solution.py:85
  105.3 12.1 %collective-permute-done.19.refs_2_ = bf16[512,128]{1,0:T(8,128)(2,1)S(1)} collective-permute-done((bf16[512,128]{1,0:T(8,128)(2,1)S(1)}, bf16[512,128]{1,0:T(8,128)(2,1)S(1)}, u32[]{:S(2)}, u32[]{:S(2)}) %collective-permute-start.19) | collective-permute-done | bytes 131104 | tf_op jit(solution)/shard_map/ppermute | solution.py:85
  117.4 1.8 %shard_map.157 = (bf16[512,128]{1,0:T(8,128)(2,1)S(1)}, bf16[512,128]{1,0:T(8,128)(2,1)S(1)}, bf16[512,128]{1,0:T(8,128)(2,1)S(1)}, bf16[512,128]{1,0:T(8,128)(2,1)S(1)}) custom-call(s32[3]{0:T(128)S(1)} %copy-done.8, bf16[512,128]{1,0:T(8,128)(2,1)S(1)} %collective-permute-done.17.refs_0_, bf16[512,128]{1,0:T(8,128)(2,1)S(1)} %collective-permute-done.18.refs_1_, ...), custom_call_target="tpu_custom_call" | custom-call | tf_op jit(solution)/shard_map/pallas_call | solution.py:39
  119.3 2.2 %collective-permute-start.26 = (bf16[512,128]{1,0:T(8,128)(2,1)S(1)}, bf16[512,128]{1,0:T(8,128)(2,1)S(1)}, u32[]{:S(2)}, u32[]{:S(2)}) collective-permute-start(bf16[512,128]{1,0:T(8,128)(2,1)S(1)} %get-tuple-element.84), channel_id=1, source_target_pairs={{0,2},{1,3},{2,0},{3,1},{4,6},{5,7},{6,4},{7,5},{8,10},{9,11},{10,... | collective-permute-start | bytes 393224 | tf_op jit(solution)/shard_map/ppermute | solution.py:74
  121.5 2.2 %collective-permute-start.27 = (bf16[512,128]{1,0:T(8,128)(2,1)S(1)}, bf16[512,128]{1,0:T(8,128)(2,1)S(1)}, u32[]{:S(2)}, u32[]{:S(2)}) collective-permute-start(bf16[512,128]{1,0:T(8,128)(2,1)S(1)} %get-tuple-element.85), channel_id=1, source_target_pairs={{0,3},{1,2},{2,1},{3,0},{4,7},{5,6},{6,5},{7,4},{8,11},{9,10},{10,... | collective-permute-start | bytes 393224 | tf_op jit(solution)/shard_map/ppermute | solution.py:74
  126.2 6.0 %collective-permute-done.26.refs_2_ = bf16[512,128]{1,0:T(8,128)(2,1)S(1)} collective-permute-done((bf16[512,128]{1,0:T(8,128)(2,1)S(1)}, bf16[512,128]{1,0:T(8,128)(2,1)S(1)}, u32[]{:S(2)}, u32[]{:S(2)}) %collective-permute-start.26) | collective-permute-done | bytes 131104 | tf_op jit(solution)/shard_map/ppermute | solution.py:74
  (74 shorter events, 12.6 us)
Async XLA Ops:
  1.2 28.2 %copy-start.6 = (s32[8,2048]{1,0:T(8,128)S(1)}, s32[8,2048]{1,0:T(8,128)}, u32[]{:S(2)}) copy-start(s32[8,2048]{1,0:T(8,128)} %refs_5_.1) | copy-start | bytes 196612
  1.2 28.2 %copy-start.7 = (bf16[512,64]{0,1:T(8,128)(2,1)S(1)}, bf16[512,64]{0,1:T(8,128)(2,1)}, u32[]{:S(2)}) copy-start(bf16[512,64]{0,1:T(8,128)(2,1)} %param.23) | copy-start | bytes 196612
  4.0 10.1 %collective-permute-start.2 = (bf16[256,128]{1,0:T(8,128)(2,1)}, bf16[256,128]{1,0:T(8,128)(2,1)S(1)}, u32[]{:S(2)}, u32[]{:S(2)}) collective-permute-start(bf16[256,128]{1,0:T(8,128)(2,1)} %get-tuple-element.46.refs_0_), channel_id=1, source_target_pairs={{0,3},{1,2},{2,1},{3,0},{4,7},{5,6},{6,5},{7,4},{8,11},{9,10},{10,... | collective-permute-start | bytes 196616 | tf_op jit(solution)/shard_map/ppermute | solution.py:74
  9.1 7.0 %collective-permute-start.1 = (bf16[256,128]{1,0:T(8,128)(2,1)}, bf16[256,128]{1,0:T(8,128)(2,1)S(1)}, u32[]{:S(2)}, u32[]{:S(2)}) collective-permute-start(bf16[256,128]{1,0:T(8,128)(2,1)} %get-tuple-element.46.refs_0_), channel_id=1, source_target_pairs={{0,2},{1,3},{2,0},{3,1},{4,6},{5,7},{6,4},{7,5},{8,10},{9,11},{10,... | collective-permute-start | bytes 196616 | tf_op jit(solution)/shard_map/ppermute | solution.py:74
  9.1 7.9 %collective-permute-start = (bf16[256,128]{1,0:T(8,128)(2,1)}, bf16[256,128]{1,0:T(8,128)(2,1)S(1)}, u32[]{:S(2)}, u32[]{:S(2)}) collective-permute-start(bf16[256,128]{1,0:T(8,128)(2,1)} %get-tuple-element.46.refs_0_), channel_id=1, source_target_pairs={{0,1},{1,0},{2,3},{3,2},{4,5},{5,4},{6,7},{7,6},{8,9},{9,8},{10,11... | collective-permute-start | bytes 196616 | tf_op jit(solution)/shard_map/ppermute | solution.py:74
  9.8 19.6 %collective-permute-start.3 = (bf16[512,128]{1,0:T(8,128)(2,1)}, bf16[512,128]{1,0:T(8,128)(2,1)S(1)}, u32[]{:S(2)}, u32[]{:S(2)}) collective-permute-start(bf16[512,128]{1,0:T(8,128)(2,1)} %get-tuple-element.50), channel_id=1, source_target_pairs={{0,1},{1,0},{2,3},{3,2},{4,5},{5,4},{6,7},{7,6},{8,9},{9,8},{10,11... | collective-permute-start | bytes 393224 | tf_op jit(solution)/shard_map/ppermute | solution.py:74
  11.2 18.2 %collective-permute-start.4 = (bf16[512,128]{1,0:T(8,128)(2,1)}, bf16[512,128]{1,0:T(8,128)(2,1)S(1)}, u32[]{:S(2)}, u32[]{:S(2)}) collective-permute-start(bf16[512,128]{1,0:T(8,128)(2,1)} %get-tuple-element.51), channel_id=1, source_target_pairs={{0,2},{1,3},{2,0},{3,1},{4,6},{5,7},{6,4},{7,5},{8,10},{9,11},{10,... | collective-permute-start | bytes 393224 | tf_op jit(solution)/shard_map/ppermute | solution.py:74
  14.1 15.3 %collective-permute-start.5 = (bf16[512,128]{1,0:T(8,128)(2,1)}, bf16[512,128]{1,0:T(8,128)(2,1)S(1)}, u32[]{:S(2)}, u32[]{:S(2)}) collective-permute-start(bf16[512,128]{1,0:T(8,128)(2,1)} %get-tuple-element.52), channel_id=1, source_target_pairs={{0,3},{1,2},{2,1},{3,0},{4,7},{5,6},{6,5},{7,4},{8,11},{9,10},{10,... | collective-permute-start | bytes 393224 | tf_op jit(solution)/shard_map/ppermute | solution.py:74
  35.1 17.0 %all-to-all-start = ((bf16[8,400,128]{2,1,0:T(8,128)(2,1)}), bf16[8,400,128]{2,1,0:T(8,128)(2,1)S(1)}, u32[]{:S(2)}, u32[]{:S(2)}) async-start(bf16[8,400,128]{2,1,0:T(8,128)(2,1)} %bitcast.5), calls=%async_computation | async-start | bytes 1638400 | tf_op jit(solution)/shard_map/all_to_all | solution.py:407
  39.5 15.8 %collective-permute-start.10 = (bf16[512,128]{1,0:T(8,128)(2,1)S(1)}, bf16[512,128]{1,0:T(8,128)(2,1)S(1)}, u32[]{:S(2)}, u32[]{:S(2)}) collective-permute-start(bf16[512,128]{1,0:T(8,128)(2,1)S(1)} %get-tuple-element.65), channel_id=1, source_target_pairs={{0,4},{1,0},{2,12},{3,8},{4,5},{5,1},{6,13},{7,9},{8,6},{9,2},{10,... | collective-permute-start | bytes 393224 | tf_op jit(solution)/shard_map/ppermute | solution.py:88
  40.0 19.0 %collective-permute-start.11 = (bf16[512,128]{1,0:T(8,128)(2,1)S(1)}, bf16[512,128]{1,0:T(8,128)(2,1)S(1)}, u32[]{:S(2)}, u32[]{:S(2)}) collective-permute-start(bf16[512,128]{1,0:T(8,128)(2,1)S(1)} %get-tuple-element.66), channel_id=1, source_target_pairs={{0,8},{1,12},{2,0},{3,4},{4,9},{5,13},{6,1},{7,5},{8,10},{9,14},{1... | collective-permute-start | bytes 393224 | tf_op jit(solution)/shard_map/ppermute | solution.py:88
  41.8 24.9 %collective-permute-start.12 = (bf16[512,128]{1,0:T(8,128)(2,1)S(1)}, bf16[512,128]{1,0:T(8,128)(2,1)S(1)}, u32[]{:S(2)}, u32[]{:S(2)}) collective-permute-start(bf16[512,128]{1,0:T(8,128)(2,1)S(1)} %get-tuple-element.67), channel_id=1, source_target_pairs={{0,12},{1,8},{2,4},{3,0},{4,13},{5,9},{6,5},{7,1},{8,14},{9,10},{1... | collective-permute-start | bytes 393224 | tf_op jit(solution)/shard_map/ppermute | solution.py:88
  54.6 19.1 %collective-permute-start.13 = (bf16[8,128,128]{2,1,0:T(8,128)(2,1)S(1)}, bf16[8,128,128]{2,1,0:T(8,128)(2,1)S(1)}, u32[]{:S(2)}, u32[]{:S(2)}) collective-permute-start(bf16[8,128,128]{2,1,0:T(8,128)(2,1)S(1)} %get-tuple-element.68.refs_8_), channel_id=1, source_target_pairs={{0,4},{4,0},{8,12},{12,8},{16,20},{20,16},{24,28},{28,24},{1,5},{5... | collective-permute-start | bytes 786440 | tf_op jit(solution)/shard_map/ppermute | solution.py:77
  54.7 12.1 %collective-permute-start.9 = (bf16[544,128]{1,0:T(8,128)(2,1)S(1)}, bf16[544,128]{1,0:T(8,128)(2,1)S(1)}, u32[]{:S(2)}, u32[]{:S(2)}) collective-permute-start(bf16[544,128]{1,0:T(8,128)(2,1)S(1)} %get-tuple-element.64), channel_id=1, source_target_pairs={{0,0},{1,4},{2,8},{3,12},{4,1},{5,5},{6,9},{7,13},{8,2},{9,6},{10,... | collective-permute-start | bytes 417800 | tf_op jit(solution)/shard_map/ppermute | solution.py:88
  55.4 11.4 %collective-permute-start.6 = (bf16[512,128]{1,0:T(8,128)(2,1)S(1)}, bf16[512,128]{1,0:T(8,128)(2,1)S(1)}, u32[]{:S(2)}, u32[]{:S(2)}) collective-permute-start(bf16[512,128]{1,0:T(8,128)(2,1)S(1)} %get-tuple-element.57), channel_id=1, source_target_pairs={{0,4},{4,0},{8,12},{12,8},{16,20},{20,16},{24,28},{28,24},{1,5},{5... | collective-permute-start | bytes 393224 | tf_op jit(solution)/shard_map/ppermute | solution.py:77
  59.0 12.3 %collective-permute-start.7 = (bf16[512,128]{1,0:T(8,128)(2,1)S(1)}, bf16[512,128]{1,0:T(8,128)(2,1)S(1)}, u32[]{:S(2)}, u32[]{:S(2)}) collective-permute-start(bf16[512,128]{1,0:T(8,128)(2,1)S(1)} %get-tuple-element.58), channel_id=1, source_target_pairs={{0,8},{4,12},{8,0},{12,4},{16,24},{20,28},{24,16},{28,20},{1,9},{5... | collective-permute-start | bytes 393224 | tf_op jit(solution)/shard_map/ppermute | solution.py:77
  66.7 6.9 %collective-permute-start.8 = (bf16[512,128]{1,0:T(8,128)(2,1)S(1)}, bf16[512,128]{1,0:T(8,128)(2,1)S(1)}, u32[]{:S(2)}, u32[]{:S(2)}) collective-permute-start(bf16[512,128]{1,0:T(8,128)(2,1)S(1)} %get-tuple-element.59), channel_id=1, source_target_pairs={{0,12},{4,8},{8,4},{12,0},{16,28},{20,24},{24,20},{28,16},{1,13},{... | collective-permute-start | bytes 393224 | tf_op jit(solution)/shard_map/ppermute | solution.py:77
  75.2 5.0 %collective-permute-start.14 = (bf16[512,128]{1,0:T(8,128)(2,1)S(1)}, bf16[512,128]{1,0:T(8,128)(2,1)S(1)}, u32[]{:S(2)}, u32[]{:S(2)}) collective-permute-start(bf16[512,128]{1,0:T(8,128)(2,1)S(1)} %get-tuple-element.70), channel_id=1, source_target_pairs={{0,4},{4,0},{8,12},{12,8},{16,20},{20,16},{24,28},{28,24},{1,5},{5... | collective-permute-start | bytes 393224 | tf_op jit(solution)/shard_map/ppermute | solution.py:77
  75.3 6.6 %collective-permute-start.15 = (bf16[512,128]{1,0:T(8,128)(2,1)S(1)}, bf16[512,128]{1,0:T(8,128)(2,1)S(1)}, u32[]{:S(2)}, u32[]{:S(2)}) collective-permute-start(bf16[512,128]{1,0:T(8,128)(2,1)S(1)} %get-tuple-element.71), channel_id=1, source_target_pairs={{0,8},{4,12},{8,0},{12,4},{16,24},{20,28},{24,16},{28,20},{1,9},{5... | collective-permute-start | bytes 393224 | tf_op jit(solution)/shard_map/ppermute | solution.py:77
  77.6 7.9 %collective-permute-start.16 = (bf16[512,128]{1,0:T(8,128)(2,1)S(1)}, bf16[512,128]{1,0:T(8,128)(2,1)S(1)}, u32[]{:S(2)}, u32[]{:S(2)}) collective-permute-start(bf16[512,128]{1,0:T(8,128)(2,1)S(1)} %get-tuple-element.72), channel_id=1, source_target_pairs={{0,12},{4,8},{8,4},{12,0},{16,28},{20,24},{24,20},{28,16},{1,13},{... | collective-permute-start | bytes 393224 | tf_op jit(solution)/shard_map/ppermute | solution.py:77
  77.6 13.8 %collective-permute-start.22 = (bf16[512,128]{1,0:T(8,128)(2,1)S(1)}, bf16[512,128]{1,0:T(8,128)(2,1)S(1)}, u32[]{:S(2)}, u32[]{:S(2)}) collective-permute-start(bf16[512,128]{1,0:T(8,128)(2,1)S(1)} %get-tuple-element.70), channel_id=1, source_target_pairs={{0,1},{1,5},{2,9},{3,13},{4,0},{5,4},{6,8},{7,12},{8,3},{9,7},{10,... | collective-permute-start | bytes 393224 | tf_op jit(solution)/shard_map/ppermute | solution.py:85
  77.7 13.6 %collective-permute-start.23 = (bf16[512,128]{1,0:T(8,128)(2,1)S(1)}, bf16[512,128]{1,0:T(8,128)(2,1)S(1)}, u32[]{:S(2)}, u32[]{:S(2)}) collective-permute-start(bf16[512,128]{1,0:T(8,128)(2,1)S(1)} %get-tuple-element.71), channel_id=1, source_target_pairs={{0,2},{1,6},{2,10},{3,14},{4,3},{5,7},{6,11},{7,15},{8,0},{9,4},{1... | collective-permute-start | bytes 393224 | tf_op jit(solution)/shard_map/ppermute | solution.py:85
  80.3 11.1 %collective-permute-start.24 = (bf16[512,128]{1,0:T(8,128)(2,1)S(1)}, bf16[512,128]{1,0:T(8,128)(2,1)S(1)}, u32[]{:S(2)}, u32[]{:S(2)}) collective-permute-start(bf16[512,128]{1,0:T(8,128)(2,1)S(1)} %get-tuple-element.72), channel_id=1, source_target_pairs={{0,3},{1,7},{2,11},{3,15},{4,2},{5,6},{6,10},{7,14},{8,1},{9,5},{1... | collective-permute-start | bytes 393224 | tf_op jit(solution)/shard_map/ppermute | solution.py:85
  81.8 9.5 %collective-permute-start.21 = (bf16[512,128]{1,0:T(8,128)(2,1)S(1)}, bf16[512,128]{1,0:T(8,128)(2,1)S(1)}, u32[]{:S(2)}, u32[]{:S(2)}) collective-permute-start(bf16[512,128]{1,0:T(8,128)(2,1)S(1)} %get-tuple-element.69.refs_0_), channel_id=1, source_target_pairs={{0,0},{1,4},{2,8},{3,12},{4,1},{5,5},{6,9},{7,13},{8,2},{9,6},{10,... | collective-permute-start | bytes 393224 | tf_op jit(solution)/shard_map/ppermute | solution.py:85
  91.4 26.0 %all-to-all-start.1 = ((bf16[8,512,128]{2,1,0:T(8,128)(2,1)}), bf16[8,512,128]{2,1,0:T(8,128)(2,1)S(1)}, u32[]{:S(2)}, u32[]{:S(2)}) async-start(bf16[8,512,128]{2,1,0:T(8,128)(2,1)} %get-tuple-element.80), calls=%async_computation.1 | async-start | bytes 2097152 | tf_op jit(solution)/shard_map/all_to_all | solution.py:445
  97.2 8.1 %collective-permute-start.17 = (bf16[512,128]{1,0:T(8,128)(2,1)}, bf16[512,128]{1,0:T(8,128)(2,1)S(1)}, u32[]{:S(2)}, u32[]{:S(2)}) collective-permute-start(bf16[512,128]{1,0:T(8,128)(2,1)} %get-tuple-element.75), channel_id=1, source_target_pairs={{0,0},{1,4},{2,8},{3,12},{4,1},{5,5},{6,9},{7,13},{8,2},{9,6},{10,... | collective-permute-start | bytes 393224 | tf_op jit(solution)/shard_map/ppermute | solution.py:85
  98.8 6.5 %collective-permute-start.18 = (bf16[512,128]{1,0:T(8,128)(2,1)S(1)}, bf16[512,128]{1,0:T(8,128)(2,1)S(1)}, u32[]{:S(2)}, u32[]{:S(2)}) collective-permute-start(bf16[512,128]{1,0:T(8,128)(2,1)S(1)} %get-tuple-element.76), channel_id=1, source_target_pairs={{0,1},{1,5},{2,9},{3,13},{4,0},{5,4},{6,8},{7,12},{8,3},{9,7},{10,... | collective-permute-start | bytes 393224 | tf_op jit(solution)/shard_map/ppermute | solution.py:85
  101.3 16.0 %collective-permute-start.19 = (bf16[512,128]{1,0:T(8,128)(2,1)S(1)}, bf16[512,128]{1,0:T(8,128)(2,1)S(1)}, u32[]{:S(2)}, u32[]{:S(2)}) collective-permute-start(bf16[512,128]{1,0:T(8,128)(2,1)S(1)} %get-tuple-element.77), channel_id=1, source_target_pairs={{0,2},{1,6},{2,10},{3,14},{4,3},{5,7},{6,11},{7,15},{8,0},{9,4},{1... | collective-permute-start | bytes 393224 | tf_op jit(solution)/shard_map/ppermute | solution.py:85
  103.9 13.5 %collective-permute-start.20 = (bf16[512,128]{1,0:T(8,128)(2,1)S(1)}, bf16[512,128]{1,0:T(8,128)(2,1)S(1)}, u32[]{:S(2)}, u32[]{:S(2)}) collective-permute-start(bf16[512,128]{1,0:T(8,128)(2,1)S(1)} %get-tuple-element.78), channel_id=1, source_target_pairs={{0,3},{1,7},{2,11},{3,15},{4,2},{5,6},{6,10},{7,14},{8,1},{9,5},{1... | collective-permute-start | bytes 393224 | tf_op jit(solution)/shard_map/ppermute | solution.py:85
  119.2 7.0 %collective-permute-start.25 = (bf16[512,128]{1,0:T(8,128)(2,1)S(1)}, bf16[512,128]{1,0:T(8,128)(2,1)S(1)}, u32[]{:S(2)}, u32[]{:S(2)}) collective-permute-start(bf16[512,128]{1,0:T(8,128)(2,1)S(1)} %get-tuple-element.83), channel_id=1, source_target_pairs={{0,1},{1,0},{2,3},{3,2},{4,5},{5,4},{6,7},{7,6},{8,9},{9,8},{10,11... | collective-permute-start | bytes 393224 | tf_op jit(solution)/shard_map/ppermute | solution.py:74
  119.3 13.0 %collective-permute-start.26 = (bf16[512,128]{1,0:T(8,128)(2,1)S(1)}, bf16[512,128]{1,0:T(8,128)(2,1)S(1)}, u32[]{:S(2)}, u32[]{:S(2)}) collective-permute-start(bf16[512,128]{1,0:T(8,128)(2,1)S(1)} %get-tuple-element.84), channel_id=1, source_target_pairs={{0,2},{1,3},{2,0},{3,1},{4,6},{5,7},{6,4},{7,5},{8,10},{9,11},{10,... | collective-permute-start | bytes 393224 | tf_op jit(solution)/shard_map/ppermute | solution.py:74
  121.5 10.7 %collective-permute-start.27 = (bf16[512,128]{1,0:T(8,128)(2,1)S(1)}, bf16[512,128]{1,0:T(8,128)(2,1)S(1)}, u32[]{:S(2)}, u32[]{:S(2)}) collective-permute-start(bf16[512,128]{1,0:T(8,128)(2,1)S(1)} %get-tuple-element.85), channel_id=1, source_target_pairs={{0,3},{1,2},{2,1},{3,0},{4,7},{5,6},{6,5},{7,4},{8,11},{9,10},{10,... | collective-permute-start | bytes 393224 | tf_op jit(solution)/shard_map/ppermute | solution.py:74
  (13 other events, 126.1 us)

commit v4 on v3

--- a/solution.py
+++ b/solution.py
@@ -87,9 +87,10 @@
     def away(x, r):
         return lax.ppermute(x, both, [(at(j, s) * M + m, at(m ^ r, s) * M + j) for s, j, m in devices])
 
-    def split(info, ef, wm, wa, we, wu, *refs):
+    def split(info, ef, wm, wa, we, wu, af, *refs):
         g, m = info[0], info[1]
-        outs, share, sem = refs[:M], refs[M], refs[M + 1]
+        outs, share, quarters, sem = refs[:M], refs[M], refs[M + 1 : 2 * M + 1], refs[2 * M + 1]
+        part = quarters[0].shape[0]
         moves = []
         for k in range(M):
             for s in range(per):
@@ -100,6 +101,8 @@
             moves.append((w.at[pl.ds(pl.multiple_of(g * n, n), n), :], share.at[start : start + n, :]))
             start += n
         moves.append((wu, share.at[start:, :]))
+        for r in range(M):
+            moves.append((af.at[pl.ds(pl.multiple_of((m ^ r) * part, part), part), :], quarters[r].at[:, :]))
         copies = [pltpu.make_async_copy(src, dst, sem.at[i]) for i, (src, dst) in enumerate(moves)]
         for c in copies:
             c.start()
@@ -107,24 +110,16 @@
             c.wait()
 
     def stack(info, *refs):
-        parts, outs = refs[:M], refs[M:]
-        n = outs[0].shape[1]
-        for j, out in enumerate(outs):
-            for k in range(M):
-                out[k] = parts[k][j * n : (j + 1) * n, :]
+        parts, (out, we) = refs[:M], refs[M:]
+        n = we.shape[1]
+        for k in range(M):
+            for j in range(out.shape[0] // (M * n)):
+                out[(j * M + k) * n : (j * M + k + 1) * n, :] = parts[k][j * n : (j + 1) * n, :]
+            we[k] = parts[k][2 * n : 3 * n, :]
 
     def digits(ids):
         high = lax.div(ids, DIGIT)
         return high.astype(F32), (ids - high * DIGIT).astype(F32)
-
-    def quarters(info, af, src, *outs):
-        m, atoms = info[1], info[2]
-        part = outs[1].shape[0]
-        for r in range(M):
-            outs[r][:part, :] = af[pl.ds(pl.multiple_of((m ^ r) * part, part), part), :]
-        high, low = digits(lax.rem(src[...], atoms))
-        lines = [x[:, c : c + LANES] for x in (high, low) for c in range(0, CAP, LANES)]
-        outs[0][part:, :] = jnp.concatenate(lines, axis=0).astype(BF)
 
     def triplets(info, *refs):
         m = info[1]
@@ -161,16 +156,23 @@
 
         lax.fori_loop(0, G, put, 0, unroll=G <= 8)
 
+    def put_shares(info, shares, dst):
+        g, m = info[0], info[1]
+        n, width = shares[0].shape[0] // M, shares[0].shape[1]
+        for d in range(G):
+            for k in range(M):
+                here = pl.ds(pl.multiple_of((g ^ d) * n, n), n)
+                dst[here, lanes(m ^ k, width)] = shares[d][k * n : (k + 1) * n, :]
+
     def messages(info, *refs):
         m, atoms = info[1], info[2]
-        up, (shares, ride, x, bil, live, tgt, total_out, out, wm, wu) = refs[:M], refs[M:]
+        up, shares, (x, bil, live, tgt, src, total_out, out, wm, wu) = refs[:M], refs[M : M + G], refs[M + G :]
         width = out.shape[3]
-        first = out.shape[2] - CAP - ID_ROWS
         dt = wu.shape[0]
 
         @pl.when(pl.program_id(0) == 0)
         def _():
-            put_weights(m, shares, wm)
+            put_shares(info, shares, wm)
             for k in range(M):
                 wu[:, lanes(m ^ k, width)] = up[k][up[k].shape[0] - dt :, :]
 
@@ -179,38 +181,40 @@
         total_out[...] = total
         block = pl.ds(at(m, pl.program_id(0)), 1)
         sent = (total * column(live[block, :]).astype(F32)).astype(BF)
-        lines = [x[:, c : c + LANES] for x in digits(lax.rem(tgt[block, :], atoms)) for c in range(0, CAP, LANES)]
-        lines.append(jnp.zeros((ID_ROWS - len(lines), LANES), F32))
-        lines = jnp.concatenate(lines, axis=0).astype(BF)
+        ends = [digits(lax.rem(ids, atoms)) for ids in (tgt[block, :], src[...])]
+        lines = [[x[:, c : c + LANES] for x in pair for c in range(0, CAP, LANES)] for pair in ends]
+        lines[0].append(jnp.zeros((ID_ROWS - len(lines[0]), LANES), F32))
+        lines = [jnp.concatenate(part, axis=0).astype(BF) for part in lines]
         for f in range(M):
-            for j in range(M // 2):
-                out[0, f, j * ride.shape[1] : (j + 1) * ride.shape[1], :] = ride[f % 2 * (M // 2) + j]
-            out[0, f, first : first + CAP, :] = sent[:, f * width : (f + 1) * width]
-            out[0, f, first + CAP :, :] = lines
-
-    def aggregate(info, incoming, *refs):
+            out[0, f, :CAP, :] = sent[:, f * width : (f + 1) * width]
+            out[0, f, CAP : CAP + ID_ROWS, :] = lines[0]
+            out[0, f, CAP + ID_ROWS :, :] = lines[1]
+
+    def arrived(info, *refs):
+        refs[-1][...] = jnp.zeros(refs[-1].shape, F32)
+
+    def aggregate(info, incoming, _, *refs):
         f = info[0] % M
-        outs, (ids, ride, onehot, values, agg) = refs[:M], refs[M:]
+        outs, (ids, sent, onehot, values, agg) = refs[:M], refs[M:]
         part, width = outs[0].shape
         half = agg.shape[0] // 2
         step = onehot.shape[0]
-        first = incoming.shape[1] - CAP - ID_ROWS
         low = lax.broadcasted_iota(jnp.int32, (LANES, CAP), 0)
 
         def place(g, _):
-            lines = incoming[g, first + CAP :, :].astype(F32)
+            lines = incoming[g, CAP : CAP + ID_ROWS, :].astype(F32)
             n = CAP // LANES
             high = jnp.concatenate([lines[c : c + 1, :] for c in range(n)], axis=1)
             row = high * DIGIT + jnp.concatenate([lines[n + c : n + c + 1, :] for c in range(n)], axis=1)
             ids[g] = row.astype(jnp.int32)
-            ride[g] = incoming[g, :first, :]
             upper = (column(row) >= half).astype(F32)
-            rows = incoming[g, first : first + CAP, :].astype(F32)
+            rows = incoming[g, :CAP, :].astype(F32)
             values[block_rows(g), :width] = (rows * (1.0 - upper)).astype(BF)
             values[block_rows(g), width:] = (rows * upper).astype(BF)
             return 0
 
         lax.fori_loop(0, G, place, 0, unroll=G <= 8)
+        sent[...] = incoming[at(info[1], info[0] // M), CAP + ID_ROWS :, :]
         for q in range(half // step):
 
             def fill(g, _):
@@ -233,21 +237,12 @@
     def atom_layer(info, *refs):
         g, m = info[0], info[1]
         f = g % M
-        sums, feats, halves = refs[:M], refs[M : 2 * M], refs[2 * M : 2 * M + 2]
-        outs, (x, wa) = refs[2 * M + 2 : 3 * M + 2], refs[3 * M + 2 :]
+        sums, feats, shares = refs[:M], refs[M : 2 * M], refs[2 * M : 2 * M + G]
+        outs, (x, wa) = refs[2 * M + G : 3 * M + G], refs[3 * M + G :]
         part, width = sums[0].shape
         for r in range(M):
-            x[:, lanes(f ^ r, width)] = (feats[r][:part, :].astype(F32) + sums[r][...].astype(F32)).astype(BF)
-        n = halves[0].shape[1] // (M // 2)
-
-        def put(d, _):
-            for core, half in ((g % 2, halves[0]), ((g + 1) % 2, halves[1])):
-                for j in range(M // 2):
-                    cols = lanes(m ^ (core * (M // 2) + j), width)
-                    wa[pl.ds(pl.multiple_of(d * n, n), n), cols] = half[d, j * n : (j + 1) * n, :]
-            return 0
-
-        lax.fori_loop(0, G, put, 0, unroll=G <= 8)
+            x[:, lanes(f ^ r, width)] = (feats[r][...].astype(F32) + sums[r][...].astype(F32)).astype(BF)
+        put_shares(info, shares, wa)
         ahid = dot(x[...], wa[...])
         x[...] = (x[...].astype(F32) + silu(ahid)).astype(BF)
         for r in range(M):
@@ -282,7 +277,7 @@
             found = dot(onehot[line * CAP : (line + 1) * CAP, :], table[...])
             return jnp.where(upper, found[:, width:], found[:, :width]).astype(BF)
 
-        lines = sent[part:, :].astype(F32)
+        lines = sent[...].astype(F32)
         n = CAP // LANES
         high = jnp.concatenate([lines[c * G : (c + 1) * G, :] for c in range(n)], axis=1)
         low = jnp.concatenate([lines[(n + c) * G : (n + c + 1) * G, :] for c in range(n)], axis=1)
@@ -343,31 +338,29 @@
         depth = w_msg.shape[0]
         dt = w_down.shape[1]
         chunk = per * CAP
+        id_rows = ID_ROWS + 2 * rows // LANES
         part = atoms // M
         g = lax.axis_index("graph")
         m = lax.axis_index("mp")
         info = jnp.stack([g, m, jnp.int32(atoms)]).astype(jnp.int32)
         share = depth // G
-        *chunks, w = call(
+        first = call(
             split,
-            [sds((chunk, width))] * M + [sds((3 * share + dt, width))],
-            info,
-            [ef, w_msg, w_atom, w_edge, w_up],
-            scratch=[pltpu.SemaphoreType.DMA((M * per + 4,))],
-            in_specs=[pl.BlockSpec(memory_space=pl.ANY)] * 5,
+            [sds((chunk, width))] * M + [sds((3 * share + dt, width))] + [sds((part, width))] * M,
+            info,
+            [ef, w_msg, w_atom, w_edge, w_up, af],
+            scratch=[pltpu.SemaphoreType.DMA((M * per + M + 4,))],
+            in_specs=[pl.BlockSpec(memory_space=pl.ANY)] * 6,
             vmem=60 * 1024 * 1024,
         )
+        chunks, w, feats = first[:M], first[M], first[M + 1 :]
         ws = [w] + [over_mp(w, k) for k in range(1, M)]
         xs = [chunks[0]] + [over_mp(chunks[k], k) for k in range(1, M)]
-        feats = call(
-            quarters,
-            [sds((part + 2 * rows // LANES, width))] + [sds((part, width))] * (M - 1),
-            info,
-            [af, esrc.reshape(G, CAP)],
-            flops=0.5e9,
-        )
-        wm, wa, we = call(stack, [sds((M, share, width))] * 3, info, ws)
-        wm = lax.all_gather(wm, "graph", axis=0)
+        wm, we = call(stack, [sds((2 * M * share, width)), sds((M, share, width))], info, ws, flops=3e10)
+        even = [wm] + [over_plane(wm, x) for x in range(2, G, 2)]
+        odd = [over_plane(w, 1) for w in even]
+        wm = [w for pair in zip(even, odd) for w in pair]
+        share_spec = lambda j: [pl.BlockSpec((M * share, width), lambda i, info: (j, 0))] * G
 
         blk = lambda i, info: at(info[1], i)
         x, bil = call(
@@ -387,33 +380,41 @@
         )
         total, outgoing = call(
             messages,
-            [sds((chunk, depth), F32), sds((per, M, M // 2 * share + CAP + ID_ROWS, width))],
-            info,
-            ws + [wm.reshape(G, M * share, width), wa, x, bil, live.reshape(G, CAP), etgt.reshape(G, CAP)],
+            [sds((chunk, depth), F32), sds((per, M, CAP + id_rows, width))],
+            info,
+            ws + wm + [x, bil, live.reshape(G, CAP), etgt.reshape(G, CAP), esrc.reshape(G, CAP)],
             scratch=[pltpu.VMEM((depth, depth), BF), pltpu.VMEM((dt, depth), BF)],
             grid=(per,),
-            in_specs=[None] * (M + 2)
+            in_specs=[None] * M + share_spec(0)
             + [
                 pl.BlockSpec((CAP, depth), lambda i, info: (i, 0)),
                 pl.BlockSpec((CAP, dt), lambda i, info: (i, 0)),
                 None,
                 None,
+                None,
             ],
             out_specs=[
                 pl.BlockSpec((CAP, depth), lambda i, info: (i, 0)),
-                pl.BlockSpec((1, M, M // 2 * share + CAP + ID_ROWS, width), lambda i, info: (i, 0, 0, 0)),
+                pl.BlockSpec((1, M, CAP + id_rows, width), lambda i, info: (i, 0, 0, 0)),
             ],
         )
         incoming = lax.all_to_all(
-            outgoing.reshape(G, M // 2 * share + CAP + ID_ROWS, width), "graph", split_axis=0, concat_axis=0, tiled=True
-        )
-        *feats, _ = lax.optimization_barrier((*feats, outgoing))
+            outgoing.reshape(G, CAP + id_rows, width), "graph", split_axis=0, concat_axis=0, tiled=True
+        )
         feats = [away(feats[r], r) for r in range(M)]
-        *sums, ids, wa = call(
+        (token,) = call(
+            arrived,
+            [sds((8, LANES), F32)],
+            info,
+            feats,
+            in_specs=[pl.BlockSpec(memory_space=pl.ANY)] * M,
+            flops=3e10,
+        )
+        *sums, ids, sent = call(
             aggregate,
-            [sds((part, width))] * M + [sds((G, 1, CAP), jnp.int32), sds((G, M // 2 * share, width))],
-            info,
-            [incoming],
+            [sds((part, width))] * M + [sds((G, 1, CAP), jnp.int32), sds((2 * rows // LANES, width))],
+            info,
+            [incoming, token],
             scratch=[pltpu.VMEM((part, G * CAP), BF), pltpu.VMEM((G * CAP, 2 * width), BF), pltpu.VMEM((atoms, width), BF)],
             flops=3.0e9,
         )
@@ -422,8 +423,9 @@
             atom_layer,
             [sds((part, width))] * M,
             info,
-            sums + feats + [wa, over_plane(wa, 1)],
+            sums + feats + wm,
             scratch=[pltpu.VMEM((part, depth), BF), pltpu.VMEM((depth, depth), BF)],
+            in_specs=[None] * (2 * M) + share_spec(1),
             flops=1.5e9,
         )
         homeward = [home(outs[r], r) for r in range(M)]
@@ -432,7 +434,7 @@
             gather,
             [sds((chunk, width))] * M + [sds((G, CAP + M * share, width))],
             info,
-            outs + [ids, feats[0], we],
+            outs + [ids, sent, we],
             scratch=[
                 pltpu.VMEM((atoms // 2, 2 * width), BF),
                 pltpu.VMEM((min(G, 8) * CAP, atoms // 2), BF),

time: 134 us -> 130 us (0.970)
  blocking collectives: 10.3 us -> 0 us
  waiting for transfers between devices: 38.7 us -> 49 us
  starting transfers between devices: 57.6 us -> 52.2 us
  Pallas kernels: 24 us -> 25.4 us
    all_gather x1 -> x0, blocking collectives: 10.3 us -> none  [local(): wm = lax.all_gather(wm, 'graph', axis=0)]
    ppermute x4, waiting for transfers between devices: 0.01 us -> 6.34 us  [away(): lax.ppermute(x, both, [(at(j, s) * M + m, at(m ^ r, s) * M + j) for s, j,...]
    ppermute x7 -> x13, starting transfers between devices: 13.8 us -> 7.61 us  [over_plane(): return lax.ppermute(x, 'graph', [(i, i ^ k) for i in range(G)])]
    ppermute x7 -> x13, waiting for transfers between devices: 10.4 us -> 15.5 us  [over_plane(): return lax.ppermute(x, 'graph', [(i, i ^ k) for i in range(G)])]
    all_to_all x1, waiting for transfers between devices: 8 us -> 3.9 us  [local(): lax.all_to_all(outgoing.reshape(G, CAP + id_rows, width), 'graph', split_...]
    ppermute x9, waiting for transfers between devices: 8.13 us -> 11.3 us  [over_mp(): return lax.ppermute(x, 'mp', [(i, i ^ k) for i in range(M)])]
    all_to_all x1, starting transfers between devices: 3.68 us -> 6.04 us  [local(): lax.all_to_all(outgoing.reshape(G, CAP + id_rows, width), 'graph', split_...]
    all_to_all x1, starting transfers between devices: 5.86 us -> 3.57 us  [local(): lax.all_to_all(named, 'graph', split_axis=0, concat_axis=0, tiled=True)]
  transfers between devices with their start and end apart: 30 -> 36, of which waited for: 9 -> 15; matrix products, arithmetic and copies ran while one was open for 0% -> 0% of each run, Pallas kernels for 8% -> 11%
where the time goes in v4:
time: 130 us
  starting transfers between devices  52.2 us (40%)
  waiting for transfers between devices  49 us (38%)
  Pallas kernels  25.4 us (20%)
  local copies, waits for them, and re-layouts  1.54 us (1%)
    pallas_call x11, Pallas kernels, call(): pl.pallas_call(kernel, out_shape=list(out_shapes), grid_spec=pltpu.Prefet...  25.4 us
    ppermute x9, starting transfers between devices, over_mp(): return lax.ppermute(x, 'mp', [(i, i ^ k) for i in range(M)])  16 us
    ppermute x13, waiting for transfers between devices, over_plane(): return lax.ppermute(x, 'graph', [(i, i ^ k) for i in range(G)])  15.5 us
    ppermute x8, waiting for transfers between devices, home(): lax.ppermute(x, both, [(at(i, s) * M + z, at(z, s) * M + (i ^ r)) for s,...  12 us
    ppermute x8, starting transfers between devices, home(): lax.ppermute(x, both, [(at(i, s) * M + z, at(z, s) * M + (i ^ r)) for s,...  11.5 us
    ppermute x9, waiting for transfers between devices, over_mp(): return lax.ppermute(x, 'mp', [(i, i ^ k) for i in range(M)])  11.3 us
    ppermute x13, starting transfers between devices, over_plane(): return lax.ppermute(x, 'graph', [(i, i ^ k) for i in range(G)])  7.61 us
    ppermute x4, starting transfers between devices, away(): lax.ppermute(x, both, [(at(j, s) * M + m, at(m ^ r, s) * M + j) for s, j,...  7.46 us
  transfers between devices with their start and end apart: 36, of which 15 were waited for; matrix products, arithmetic and copies ran while one was open for 0% of the time, Pallas kernels for 11%

profile of v4, /device:TPU:0, one launch (start us, length us, event | category | flops | bytes accessed | tf_op | source)
XLA Modules:
  0.0 129.7 jit_solution(12270807556379809518)
XLA Ops:
  1.2 3.1 %shard_map.149 = (bf16[512,128]{1,0:T(8,128)(2,1)}, bf16[512,128]{1,0:T(8,128)(2,1)}, bf16[512,128]{1,0:T(8,128)(2,1)}, bf16[512,128]{1,0:T(8,128)(2,1)}, bf16[2...) custom-call(s32[3]{0:T(128)} %pad_add_fusion.info, ...), custom_call_target="tpu_custom_call" | custom-call | tf_op jit(solution)/shard_map/pallas_call | solution.py:39
  4.3 3.1 %collective-permute-start = (bf16[256,128]{1,0:T(8,128)(2,1)}, bf16[256,128]{1,0:T(8,128)(2,1)S(1)}, u32[]{:S(2)}, u32[]{:S(2)}) collective-permute-start(bf16[256,128]{1,0:T(8,128)(2,1)} %get-tuple-element.41.refs_0_), channel_id=1, source_target_pairs={{0,1},{1,0},{2,3},{3,2},{4,5},{5,4},{6,7},{7,6},{8,9},{9,8},{10,11... | collective-permute-start | bytes 196616 | tf_op jit(solution)/shard_map/ppermute | solution.py:74
  7.4 2.6 %collective-permute-start.1 = (bf16[256,128]{1,0:T(8,128)(2,1)}, bf16[256,128]{1,0:T(8,128)(2,1)S(1)}, u32[]{:S(2)}, u32[]{:S(2)}) collective-permute-start(bf16[256,128]{1,0:T(8,128)(2,1)} %get-tuple-element.41.refs_0_), channel_id=1, source_target_pairs={{0,2},{1,3},{2,0},{3,1},{4,6},{5,7},{6,4},{7,5},{8,10},{9,11},{10,... | collective-permute-start | bytes 196616 | tf_op jit(solution)/shard_map/ppermute | solution.py:74
  10.9 3.5 %collective-permute-start.11 = (bf16[512,128]{1,0:T(8,128)(2,1)}, bf16[512,128]{1,0:T(8,128)(2,1)S(1)}, u32[]{:S(2)}, u32[]{:S(2)}) collective-permute-start(bf16[512,128]{1,0:T(8,128)(2,1)} %get-tuple-element.45), channel_id=1, source_target_pairs={{0,2},{1,3},{2,0},{3,1},{4,6},{5,7},{6,4},{7,5},{8,10},{9,11},{10,... | collective-permute-start | bytes 393224 | tf_op jit(solution)/shard_map/ppermute | solution.py:74
  15.0 2.1 %collective-permute-done.2.refs_3_ = bf16[256,128]{1,0:T(8,128)(2,1)S(1)} collective-permute-done((bf16[256,128]{1,0:T(8,128)(2,1)}, bf16[256,128]{1,0:T(8,128)(2,1)S(1)}, u32[]{:S(2)}, u32[]{:S(2)}) %collective-permute-start.2) | collective-permute-done | bytes 65568 | tf_op jit(solution)/shard_map/ppermute | solution.py:74
  19.3 1.5 %collective-permute-start.4 = (bf16[512,128]{1,0:T(8,128)(2,1)S(1)}, bf16[512,128]{1,0:T(8,128)(2,1)S(1)}, u32[]{:S(2)}, u32[]{:S(2)}) collective-permute-start(bf16[512,128]{1,0:T(8,128)(2,1)S(1)} %get-tuple-element.42.refs_4_.refs_8_), channel_id=1, source_target_pairs={{0,8},{4,12},{8,0},{12,4},{16,24},{20,28},{24,16},{28,20},{1,9},{5... | collective-permute-start | bytes 393224 | tf_op jit(solution)/shard_map/ppermute | solution.py:77
  20.7 1.5 %collective-permute-start.6 = (bf16[512,128]{1,0:T(8,128)(2,1)S(1)}, bf16[512,128]{1,0:T(8,128)(2,1)S(1)}, u32[]{:S(2)}, u32[]{:S(2)}) collective-permute-start(bf16[512,128]{1,0:T(8,128)(2,1)S(1)} %get-tuple-element.42.refs_4_.refs_8_), channel_id=1, source_target_pairs={{0,16},{4,20},{8,24},{12,28},{16,0},{20,4},{24,8},{28,12},{1,17},{... | collective-permute-start | bytes 393224 | tf_op jit(solution)/shard_map/ppermute | solution.py:77
  22.8 1.5 %collective-permute-start.12 = (bf16[512,128]{1,0:T(8,128)(2,1)S(1)}, bf16[512,128]{1,0:T(8,128)(2,1)S(1)}, u32[]{:S(2)}, u32[]{:S(2)}) collective-permute-start(bf16[512,128]{1,0:T(8,128)(2,1)S(1)} %copy-done.14), channel_id=1, source_target_pairs={{0,3},{1,2},{2,1},{3,0},{4,7},{5,6},{6,5},{7,4},{8,11},{9,10},{10,... | collective-permute-start | bytes 393224 | tf_op jit(solution)/shard_map/ppermute | solution.py:74
  25.7 2.4 %collective-permute-done.8.refs_10_.refs_14_ = bf16[512,128]{1,0:T(8,128)(2,1)S(1)} collective-permute-done((bf16[512,128]{1,0:T(8,128)(2,1)S(1)}, bf16[512,128]{1,0:T(8,128)(2,1)S(1)}, u32[]{:S(2)}, u32[]{:S(2)}) %collective-permute-start.8) | collective-permute-done | bytes 131104 | tf_op jit(solution)/shard_map/ppermute | solution.py:77
  29.6 1.6 %collective-permute-start.13 = (bf16[512,128]{1,0:T(8,128)(2,1)}, bf16[512,128]{1,0:T(8,128)(2,1)S(1)}, u32[]{:S(2)}, u32[]{:S(2)}) collective-permute-start(bf16[512,128]{1,0:T(8,128)(2,1)} %get-tuple-element.50), channel_id=1, source_target_pairs={{0,0},{1,4},{2,8},{3,12},{4,1},{5,5},{6,9},{7,13},{8,2},{9,6},{10,... | collective-permute-start | bytes 393224 | tf_op jit(solution)/shard_map/ppermute | solution.py:88
  31.1 2.5 %collective-permute-start.14 = (bf16[512,128]{1,0:T(8,128)(2,1)}, bf16[512,128]{1,0:T(8,128)(2,1)}, u32[]{:S(2)}, u32[]{:S(2)}) collective-permute-start(bf16[512,128]{1,0:T(8,128)(2,1)} %get-tuple-element.51), channel_id=1, source_target_pairs={{0,4},{1,0},{2,12},{3,8},{4,5},{5,1},{6,13},{7,9},{8,6},{9,2},{10,... | collective-permute-start | bytes 393224 | tf_op jit(solution)/shard_map/ppermute | solution.py:88
  33.6 3.5 %collective-permute-start.15 = (bf16[512,128]{1,0:T(8,128)(2,1)}, bf16[512,128]{1,0:T(8,128)(2,1)}, u32[]{:S(2)}, u32[]{:S(2)}) collective-permute-start(bf16[512,128]{1,0:T(8,128)(2,1)} %get-tuple-element.52), channel_id=1, source_target_pairs={{0,8},{1,12},{2,0},{3,4},{4,9},{5,13},{6,1},{7,5},{8,10},{9,14},{1... | collective-permute-start | bytes 393224 | tf_op jit(solution)/shard_map/ppermute | solution.py:88
  37.2 3.1 %shard_map.151 = (bf16[512,512]{1,0:T(8,128)(2,1)S(1)}, bf16[512,64]{1,0:T(8,128)(2,1)S(1)}) custom-call(s32[3]{0:T(128)S(1)} %copy-done.8, bf16[512,128]{1,0:T(8,128)(2,1)S(1)} %copy-done.2, bf16[512,128]{1,0:T(8,128)(2,1)S(1)} %collective-permute-done.10.refs_1_, bf16[512,128]{1,0:T(8,128)(2,1)S(1)} %collective-permute-done.11.refs_2_, ...), custom_call_target="tpu_custom_call" | custom-call | tf_op jit(solution)/shard_map/pallas_call | solution.py:39
  40.3 2.7 %shard_map.152 = (f32[512,512]{1,0:T(8,128)S(1)}, bf16[2,4,304,128]{3,2,1,0:T(8,128)(2,1)}) custom-call(s32[3]{0:T(128)S(1)} %copy-done.8, bf16[256,128]{1,0:T(8,128)(2,1)S(1)} %copy-done.7, bf16[256,128]{1,0:T(8,128)(2,1)S(1)} %collective-permute-done.refs_1_, bf16[256,128]{1,0:T(8,128)(2,1)S(1)} %collective-permute-done.1.refs_2_, ...), custom_call_target="tpu_custom_call" | custom-call | tf_op jit(solution)/shard_map/pallas_call | solution.py:39
  43.0 6.0 %all-to-all-start = ((bf16[8,304,128]{2,1,0:T(8,128)(2,1)}), bf16[8,304,128]{2,1,0:T(8,128)(2,1)S(1)}, u32[]{:S(2)}, u32[]{:S(2)}) async-start(bf16[8,304,128]{2,1,0:T(8,128)(2,1)} %bitcast.4), calls=%async_computation | async-start | bytes 1245184 | tf_op jit(solution)/shard_map/all_to_all | solution.py:401
  49.1 6.3 %collective-permute-done.15.refs_2_.refs_6_ = bf16[512,128]{1,0:T(8,128)(2,1)} collective-permute-done((bf16[512,128]{1,0:T(8,128)(2,1)}, bf16[512,128]{1,0:T(8,128)(2,1)}, u32[]{:S(2)}, u32[]{:S(2)}) %collective-permute-start.15) | collective-permute-done | bytes 131104 | tf_op jit(solution)/shard_map/ppermute | solution.py:88
  56.0 3.9 %all-to-all-done.incoming = bf16[8,304,128]{2,1,0:T(8,128)(2,1)S(1)} async-done(((bf16[8,304,128]{2,1,0:T(8,128)(2,1)}), bf16[8,304,128]{2,1,0:T(8,128)(2,1)S(1)}, u32[]{:S(2)}, u32[]{:S(2)}) %all-to-all-start) | async-done | bytes 622624 | tf_op jit(solution)/shard_map/all_to_all | solution.py:401
  59.9 2.4 %shard_map.154 = (bf16[512,128]{1,0:T(8,128)(2,1)S(1)}, bf16[512,128]{1,0:T(8,128)(2,1)S(1)}, bf16[512,128]{1,0:T(8,128)(2,1)S(1)}, bf16[512,128]{1,0:T(8,128)(2...) custom-call(s32[3]{0:T(128)S(1)} %copy-done.8, bf16[8,304,128]{2,1,0:T(8,128)(2,1)S(1)} %all-to-all-done.incoming, ...), custom_call_target="tpu_custom_call" | custom-call | flops 3000000000 | tf_op jit(solution)/shard_map/pallas_call | solution.py:39
  64.2 4.5 %collective-permute-done.18.refs_2_ = bf16[512,128]{1,0:T(8,128)(2,1)S(1)} collective-permute-done((bf16[512,128]{1,0:T(8,128)(2,1)S(1)}, bf16[512,128]{1,0:T(8,128)(2,1)S(1)}, u32[]{:S(2)}, u32[]{:S(2)}) %collective-permute-start.18) | collective-permute-done | bytes 131104 | tf_op jit(solution)/shard_map/ppermute | solution.py:77
  68.7 1.9 %collective-permute-done.19.refs_3_ = bf16[512,128]{1,0:T(8,128)(2,1)S(1)} collective-permute-done((bf16[512,128]{1,0:T(8,128)(2,1)S(1)}, bf16[512,128]{1,0:T(8,128)(2,1)S(1)}, u32[]{:S(2)}, u32[]{:S(2)}) %collective-permute-start.19) | collective-permute-done | bytes 131104 | tf_op jit(solution)/shard_map/ppermute | solution.py:77
  70.6 2.6 %shard_map.155 = (bf16[512,128]{1,0:T(8,128)(2,1)S(1)}, bf16[512,128]{1,0:T(8,128)(2,1)S(1)}, bf16[512,128]{1,0:T(8,128)(2,1)S(1)}, bf16[512,128]{1,0:T(8,128)(2,1)S(1)}) custom-call(s32[3]{0:T(128)S(1)} %copy-done.8, bf16[512,128]{1,0:T(8,128)(2,1)S(1)} %get-tuple-element.54.refs_0_, bf16[512,128]{1,0:T(8,128)(2,1)S(1)} %collective-permute-done.17.refs_1_, ...), custom_call_target="tpu_custom_call" | custom-call | flops 1500000000 | tf_op jit(solution)/shard_map/pallas_call | solution.py:39
  78.0 4.7 %collective-permute-done.21.refs_2_ = bf16[512,128]{1,0:T(8,128)(2,1)S(1)} collective-permute-done((bf16[512,128]{1,0:T(8,128)(2,1)S(1)}, bf16[512,128]{1,0:T(8,128)(2,1)S(1)}, u32[]{:S(2)}, u32[]{:S(2)}) %collective-permute-start.21) | collective-permute-done | bytes 131104 | tf_op jit(solution)/shard_map/ppermute | solution.py:77
  84.1 5.9 %shard_map.156 = (bf16[512,128]{1,0:T(8,128)(2,1)}, bf16[512,128]{1,0:T(8,128)(2,1)}, bf16[512,128]{1,0:T(8,128)(2,1)}, bf16[512,128]{1,0:T(8,128)(2,1)S(1)}, bf16[8,512,128]{2,1,0:T(8,128)(2,1)}) custom-call(s32[3]{0:T(128)S(1)} %copy-done.8, bf16[512,128]{1,0:T(8,128)(2,1)S(1)} %get-tuple-element.58.refs_0_, ...), custom_call_target="tpu_custom_call" | custom-call | flops 6000000000 | tf_op jit(solution)/shard_map/pallas_call | solution.py:39
  90.0 3.6 %all-to-all-start.1 = ((bf16[8,512,128]{2,1,0:T(8,128)(2,1)}), bf16[8,512,128]{2,1,0:T(8,128)(2,1)S(1)}, u32[]{:S(2)}, u32[]{:S(2)}) async-start(bf16[8,512,128]{2,1,0:T(8,128)(2,1)} %get-tuple-element.70), calls=%async_computation.1 | async-start | bytes 2097152 | tf_op jit(solution)/shard_map/all_to_all | solution.py:447
  93.6 1.6 %collective-permute-start.23 = (bf16[512,128]{1,0:T(8,128)(2,1)}, bf16[512,128]{1,0:T(8,128)(2,1)S(1)}, u32[]{:S(2)}, u32[]{:S(2)}) collective-permute-start(bf16[512,128]{1,0:T(8,128)(2,1)} %get-tuple-element.65), channel_id=1, source_target_pairs={{0,0},{1,4},{2,8},{3,12},{4,1},{5,5},{6,9},{7,13},{8,2},{9,6},{10,... | collective-permute-start | bytes 393224 | tf_op jit(solution)/shard_map/ppermute | solution.py:85
  95.1 3.5 %collective-permute-start.24 = (bf16[512,128]{1,0:T(8,128)(2,1)}, bf16[512,128]{1,0:T(8,128)(2,1)S(1)}, u32[]{:S(2)}, u32[]{:S(2)}) collective-permute-start(bf16[512,128]{1,0:T(8,128)(2,1)} %get-tuple-element.66), channel_id=1, source_target_pairs={{0,1},{1,5},{2,9},{3,13},{4,0},{5,4},{6,8},{7,12},{8,3},{9,7},{10,... | collective-permute-start | bytes 393224 | tf_op jit(solution)/shard_map/ppermute | solution.py:85
  98.6 1.6 %collective-permute-start.25 = (bf16[512,128]{1,0:T(8,128)(2,1)}, bf16[512,128]{1,0:T(8,128)(2,1)S(1)}, u32[]{:S(2)}, u32[]{:S(2)}) collective-permute-start(bf16[512,128]{1,0:T(8,128)(2,1)} %get-tuple-element.67), channel_id=1, source_target_pairs={{0,2},{1,6},{2,10},{3,14},{4,3},{5,7},{6,11},{7,15},{8,0},{9,4},{1... | collective-permute-start | bytes 393224 | tf_op jit(solution)/shard_map/ppermute | solution.py:85
  101.6 12.0 %collective-permute-done.25.refs_2_ = bf16[512,128]{1,0:T(8,128)(2,1)S(1)} collective-permute-done((bf16[512,128]{1,0:T(8,128)(2,1)}, bf16[512,128]{1,0:T(8,128)(2,1)S(1)}, u32[]{:S(2)}, u32[]{:S(2)}) %collective-permute-start.25) | collective-permute-done | bytes 131104 | tf_op jit(solution)/shard_map/ppermute | solution.py:85
  113.6 1.8 %shard_map.157 = (bf16[512,128]{1,0:T(8,128)(2,1)S(1)}, bf16[512,128]{1,0:T(8,128)(2,1)S(1)}, bf16[512,128]{1,0:T(8,128)(2,1)S(1)}, bf16[512,128]{1,0:T(8,128)(2,1)S(1)}) custom-call(s32[3]{0:T(128)S(1)} %copy-done.8, bf16[512,128]{1,0:T(8,128)(2,1)S(1)} %collective-permute-done.23.refs_0_, bf16[512,128]{1,0:T(8,128)(2,1)S(1)} %collective-permute-done.24.refs_1_, ...), custom_call_target="tpu_custom_call" | custom-call | tf_op jit(solution)/shard_map/pallas_call | solution.py:39
  115.5 2.4 %collective-permute-start.32 = (bf16[512,128]{1,0:T(8,128)(2,1)S(1)}, bf16[512,128]{1,0:T(8,128)(2,1)S(1)}, u32[]{:S(2)}, u32[]{:S(2)}) collective-permute-start(bf16[512,128]{1,0:T(8,128)(2,1)S(1)} %get-tuple-element.74), channel_id=1, source_target_pairs={{0,2},{1,3},{2,0},{3,1},{4,6},{5,7},{6,4},{7,5},{8,10},{9,11},{10,... | collective-permute-start | bytes 393224 | tf_op jit(solution)/shard_map/ppermute | solution.py:74
  117.9 2.0 %collective-permute-start.33 = (bf16[512,128]{1,0:T(8,128)(2,1)S(1)}, bf16[512,128]{1,0:T(8,128)(2,1)S(1)}, u32[]{:S(2)}, u32[]{:S(2)}) collective-permute-start(bf16[512,128]{1,0:T(8,128)(2,1)S(1)} %get-tuple-element.75), channel_id=1, source_target_pairs={{0,3},{1,2},{2,1},{3,0},{4,7},{5,6},{6,5},{7,4},{8,11},{9,10},{10,... | collective-permute-start | bytes 393224 | tf_op jit(solution)/shard_map/ppermute | solution.py:74
  121.5 6.8 %collective-permute-done.32.refs_2_ = bf16[512,128]{1,0:T(8,128)(2,1)S(1)} collective-permute-done((bf16[512,128]{1,0:T(8,128)(2,1)S(1)}, bf16[512,128]{1,0:T(8,128)(2,1)S(1)}, u32[]{:S(2)}, u32[]{:S(2)}) %collective-permute-start.32) | collective-permute-done | bytes 131104 | tf_op jit(solution)/shard_map/ppermute | solution.py:74
  (85 shorter events, 20.8 us)
Async XLA Ops:
  4.3 10.1 %collective-permute-start = (bf16[256,128]{1,0:T(8,128)(2,1)}, bf16[256,128]{1,0:T(8,128)(2,1)S(1)}, u32[]{:S(2)}, u32[]{:S(2)}) collective-permute-start(bf16[256,128]{1,0:T(8,128)(2,1)} %get-tuple-element.41.refs_0_), channel_id=1, source_target_pairs={{0,1},{1,0},{2,3},{3,2},{4,5},{5,4},{6,7},{7,6},{8,9},{9,8},{10,11... | collective-permute-start | bytes 196616 | tf_op jit(solution)/shard_map/ppermute | solution.py:74
  7.4 7.6 %collective-permute-start.1 = (bf16[256,128]{1,0:T(8,128)(2,1)}, bf16[256,128]{1,0:T(8,128)(2,1)S(1)}, u32[]{:S(2)}, u32[]{:S(2)}) collective-permute-start(bf16[256,128]{1,0:T(8,128)(2,1)} %get-tuple-element.41.refs_0_), channel_id=1, source_target_pairs={{0,2},{1,3},{2,0},{3,1},{4,6},{5,7},{6,4},{7,5},{8,10},{9,11},{10,... | collective-permute-start | bytes 196616 | tf_op jit(solution)/shard_map/ppermute | solution.py:74
  10.0 7.1 %collective-permute-start.2 = (bf16[256,128]{1,0:T(8,128)(2,1)}, bf16[256,128]{1,0:T(8,128)(2,1)S(1)}, u32[]{:S(2)}, u32[]{:S(2)}) collective-permute-start(bf16[256,128]{1,0:T(8,128)(2,1)} %get-tuple-element.41.refs_0_), channel_id=1, source_target_pairs={{0,3},{1,2},{2,1},{3,0},{4,7},{5,6},{6,5},{7,4},{8,11},{9,10},{10,... | collective-permute-start | bytes 196616 | tf_op jit(solution)/shard_map/ppermute | solution.py:74
  10.0 12.7 %collective-permute-start.10 = (bf16[512,128]{1,0:T(8,128)(2,1)}, bf16[512,128]{1,0:T(8,128)(2,1)S(1)}, u32[]{:S(2)}, u32[]{:S(2)}) collective-permute-start(bf16[512,128]{1,0:T(8,128)(2,1)} %get-tuple-element.44), channel_id=1, source_target_pairs={{0,1},{1,0},{2,3},{3,2},{4,5},{5,4},{6,7},{7,6},{8,9},{9,8},{10,11... | collective-permute-start | bytes 393224 | tf_op jit(solution)/shard_map/ppermute | solution.py:74
  10.9 13.3 %collective-permute-start.11 = (bf16[512,128]{1,0:T(8,128)(2,1)}, bf16[512,128]{1,0:T(8,128)(2,1)S(1)}, u32[]{:S(2)}, u32[]{:S(2)}) collective-permute-start(bf16[512,128]{1,0:T(8,128)(2,1)} %get-tuple-element.45), channel_id=1, source_target_pairs={{0,2},{1,3},{2,0},{3,1},{4,6},{5,7},{6,4},{7,5},{8,10},{9,11},{10,... | collective-permute-start | bytes 393224 | tf_op jit(solution)/shard_map/ppermute | solution.py:74
  22.3 5.9 %collective-permute-start.8 = (bf16[512,128]{1,0:T(8,128)(2,1)S(1)}, bf16[512,128]{1,0:T(8,128)(2,1)S(1)}, u32[]{:S(2)}, u32[]{:S(2)}) collective-permute-start(bf16[512,128]{1,0:T(8,128)(2,1)S(1)} %get-tuple-element.42.refs_4_.refs_8_), channel_id=1, source_target_pairs={{0,24},{4,28},{8,16},{12,20},{16,8},{20,12},{24,0},{28,4},{1,25},{... | collective-permute-start | bytes 393224 | tf_op jit(solution)/shard_map/ppermute | solution.py:77
  22.8 6.8 %collective-permute-start.12 = (bf16[512,128]{1,0:T(8,128)(2,1)S(1)}, bf16[512,128]{1,0:T(8,128)(2,1)S(1)}, u32[]{:S(2)}, u32[]{:S(2)}) collective-permute-start(bf16[512,128]{1,0:T(8,128)(2,1)S(1)} %copy-done.14), channel_id=1, source_target_pairs={{0,3},{1,2},{2,1},{3,0},{4,7},{5,6},{6,5},{7,4},{8,11},{9,10},{10,... | collective-permute-start | bytes 393224 | tf_op jit(solution)/shard_map/ppermute | solution.py:74
  24.3 6.9 %collective-permute-start.3 = (bf16[512,128]{1,0:T(8,128)(2,1)S(1)}, bf16[512,128]{1,0:T(8,128)(2,1)S(1)}, u32[]{:S(2)}, u32[]{:S(2)}) collective-permute-start(bf16[512,128]{1,0:T(8,128)(2,1)S(1)} %get-tuple-element.42.refs_4_.refs_8_), channel_id=1, source_target_pairs={{0,4},{4,0},{8,12},{12,8},{16,20},{20,16},{24,28},{28,24},{1,5},{5... | collective-permute-start | bytes 393224 | tf_op jit(solution)/shard_map/ppermute | solution.py:77
  24.5 9.1 %collective-permute-start.5 = (bf16[512,128]{1,0:T(8,128)(2,1)S(1)}, bf16[512,128]{1,0:T(8,128)(2,1)S(1)}, u32[]{:S(2)}, u32[]{:S(2)}) collective-permute-start(bf16[512,128]{1,0:T(8,128)(2,1)S(1)} %collective-permute-done.4.refs_6_.refs_10_), channel_id=1, source_target_pairs={{0,4},{4,0},{8,12},{12,8},{16,20},{20,16},{24,28},{28,24},{1,5},{5... | collective-permute-start | bytes 393224 | tf_op jit(solution)/shard_map/ppermute | solution.py:77
  25.7 11.3 %collective-permute-start.7 = (bf16[512,128]{1,0:T(8,128)(2,1)S(1)}, bf16[512,128]{1,0:T(8,128)(2,1)S(1)}, u32[]{:S(2)}, u32[]{:S(2)}) collective-permute-start(bf16[512,128]{1,0:T(8,128)(2,1)S(1)} %collective-permute-done.6.refs_8_.refs_12_), channel_id=1, source_target_pairs={{0,4},{4,0},{8,12},{12,8},{16,20},{20,16},{24,28},{28,24},{1,5},{5... | collective-permute-start | bytes 393224 | tf_op jit(solution)/shard_map/ppermute | solution.py:77
  28.1 12.2 %collective-permute-start.9 = (bf16[512,128]{1,0:T(8,128)(2,1)S(1)}, bf16[512,128]{1,0:T(8,128)(2,1)S(1)}, u32[]{:S(2)}, u32[]{:S(2)}) collective-permute-start(bf16[512,128]{1,0:T(8,128)(2,1)S(1)} %collective-permute-done.8.refs_10_.refs_14_), channel_id=1, source_target_pairs={{0,4},{4,0},{8,12},{12,8},{16,20},{20,16},{24,28},{28,24},{1,5},{5... | collective-permute-start | bytes 393224 | tf_op jit(solution)/shard_map/ppermute | solution.py:77
  29.6 19.5 %collective-permute-start.13 = (bf16[512,128]{1,0:T(8,128)(2,1)}, bf16[512,128]{1,0:T(8,128)(2,1)S(1)}, u32[]{:S(2)}, u32[]{:S(2)}) collective-permute-start(bf16[512,128]{1,0:T(8,128)(2,1)} %get-tuple-element.50), channel_id=1, source_target_pairs={{0,0},{1,4},{2,8},{3,12},{4,1},{5,5},{6,9},{7,13},{8,2},{9,6},{10,... | collective-permute-start | bytes 393224 | tf_op jit(solution)/shard_map/ppermute | solution.py:88
  31.1 17.9 %collective-permute-start.14 = (bf16[512,128]{1,0:T(8,128)(2,1)}, bf16[512,128]{1,0:T(8,128)(2,1)}, u32[]{:S(2)}, u32[]{:S(2)}) collective-permute-start(bf16[512,128]{1,0:T(8,128)(2,1)} %get-tuple-element.51), channel_id=1, source_target_pairs={{0,4},{1,0},{2,12},{3,8},{4,5},{5,1},{6,13},{7,9},{8,6},{9,2},{10,... | collective-permute-start | bytes 393224 | tf_op jit(solution)/shard_map/ppermute | solution.py:88
  33.6 21.8 %collective-permute-start.15 = (bf16[512,128]{1,0:T(8,128)(2,1)}, bf16[512,128]{1,0:T(8,128)(2,1)}, u32[]{:S(2)}, u32[]{:S(2)}) collective-permute-start(bf16[512,128]{1,0:T(8,128)(2,1)} %get-tuple-element.52), channel_id=1, source_target_pairs={{0,8},{1,12},{2,0},{3,4},{4,9},{5,13},{6,1},{7,5},{8,10},{9,14},{1... | collective-permute-start | bytes 393224 | tf_op jit(solution)/shard_map/ppermute | solution.py:88
  37.0 18.4 %collective-permute-start.16 = (bf16[512,128]{1,0:T(8,128)(2,1)}, bf16[512,128]{1,0:T(8,128)(2,1)}, u32[]{:S(2)}, u32[]{:S(2)}) collective-permute-start(bf16[512,128]{1,0:T(8,128)(2,1)} %get-tuple-element.53), channel_id=1, source_target_pairs={{0,12},{1,8},{2,4},{3,0},{4,13},{5,9},{6,5},{7,1},{8,14},{9,10},{1... | collective-permute-start | bytes 393224 | tf_op jit(solution)/shard_map/ppermute | solution.py:88
  43.0 16.8 %all-to-all-start = ((bf16[8,304,128]{2,1,0:T(8,128)(2,1)}), bf16[8,304,128]{2,1,0:T(8,128)(2,1)S(1)}, u32[]{:S(2)}, u32[]{:S(2)}) async-start(bf16[8,304,128]{2,1,0:T(8,128)(2,1)} %bitcast.4), calls=%async_computation | async-start | bytes 1245184 | tf_op jit(solution)/shard_map/all_to_all | solution.py:401
  62.4 6.4 %collective-permute-start.18 = (bf16[512,128]{1,0:T(8,128)(2,1)S(1)}, bf16[512,128]{1,0:T(8,128)(2,1)S(1)}, u32[]{:S(2)}, u32[]{:S(2)}) collective-permute-start(bf16[512,128]{1,0:T(8,128)(2,1)S(1)} %get-tuple-element.56), channel_id=1, source_target_pairs={{0,8},{4,12},{8,0},{12,4},{16,24},{20,28},{24,16},{28,20},{1,9},{5... | collective-permute-start | bytes 393224 | tf_op jit(solution)/shard_map/ppermute | solution.py:77
  63.0 7.6 %collective-permute-start.19 = (bf16[512,128]{1,0:T(8,128)(2,1)S(1)}, bf16[512,128]{1,0:T(8,128)(2,1)S(1)}, u32[]{:S(2)}, u32[]{:S(2)}) collective-permute-start(bf16[512,128]{1,0:T(8,128)(2,1)S(1)} %get-tuple-element.57), channel_id=1, source_target_pairs={{0,12},{4,8},{8,4},{12,0},{16,28},{20,24},{24,20},{28,16},{1,13},{... | collective-permute-start | bytes 393224 | tf_op jit(solution)/shard_map/ppermute | solution.py:77
  73.5 9.1 %collective-permute-start.21 = (bf16[512,128]{1,0:T(8,128)(2,1)S(1)}, bf16[512,128]{1,0:T(8,128)(2,1)S(1)}, u32[]{:S(2)}, u32[]{:S(2)}) collective-permute-start(bf16[512,128]{1,0:T(8,128)(2,1)S(1)} %get-tuple-element.60), channel_id=1, source_target_pairs={{0,8},{4,12},{8,0},{12,4},{16,24},{20,28},{24,16},{28,20},{1,9},{5... | collective-permute-start | bytes 393224 | tf_op jit(solution)/shard_map/ppermute | solution.py:77
  74.1 10.0 %collective-permute-start.22 = (bf16[512,128]{1,0:T(8,128)(2,1)S(1)}, bf16[512,128]{1,0:T(8,128)(2,1)S(1)}, u32[]{:S(2)}, u32[]{:S(2)}) collective-permute-start(bf16[512,128]{1,0:T(8,128)(2,1)S(1)} %get-tuple-element.61), channel_id=1, source_target_pairs={{0,12},{4,8},{8,4},{12,0},{16,28},{20,24},{24,20},{28,16},{1,13},{... | collective-permute-start | bytes 393224 | tf_op jit(solution)/shard_map/ppermute | solution.py:77
  75.1 14.8 %collective-permute-start.28 = (bf16[512,128]{1,0:T(8,128)(2,1)S(1)}, bf16[512,128]{1,0:T(8,128)(2,1)S(1)}, u32[]{:S(2)}, u32[]{:S(2)}) collective-permute-start(bf16[512,128]{1,0:T(8,128)(2,1)S(1)} %get-tuple-element.59), channel_id=1, source_target_pairs={{0,1},{1,5},{2,9},{3,13},{4,0},{5,4},{6,8},{7,12},{8,3},{9,7},{10,... | collective-permute-start | bytes 393224 | tf_op jit(solution)/shard_map/ppermute | solution.py:85
  75.1 14.8 %collective-permute-start.29 = (bf16[512,128]{1,0:T(8,128)(2,1)S(1)}, bf16[512,128]{1,0:T(8,128)(2,1)S(1)}, u32[]{:S(2)}, u32[]{:S(2)}) collective-permute-start(bf16[512,128]{1,0:T(8,128)(2,1)S(1)} %get-tuple-element.60), channel_id=1, source_target_pairs={{0,2},{1,6},{2,10},{3,14},{4,3},{5,7},{6,11},{7,15},{8,0},{9,4},{1... | collective-permute-start | bytes 393224 | tf_op jit(solution)/shard_map/ppermute | solution.py:85
  76.5 13.5 %collective-permute-start.30 = (bf16[512,128]{1,0:T(8,128)(2,1)S(1)}, bf16[512,128]{1,0:T(8,128)(2,1)S(1)}, u32[]{:S(2)}, u32[]{:S(2)}) collective-permute-start(bf16[512,128]{1,0:T(8,128)(2,1)S(1)} %get-tuple-element.61), channel_id=1, source_target_pairs={{0,3},{1,7},{2,11},{3,15},{4,2},{5,6},{6,10},{7,14},{8,1},{9,5},{1... | collective-permute-start | bytes 393224 | tf_op jit(solution)/shard_map/ppermute | solution.py:85
  82.7 7.3 %collective-permute-start.27 = (bf16[512,128]{1,0:T(8,128)(2,1)S(1)}, bf16[512,128]{1,0:T(8,128)(2,1)S(1)}, u32[]{:S(2)}, u32[]{:S(2)}) collective-permute-start(bf16[512,128]{1,0:T(8,128)(2,1)S(1)} %get-tuple-element.58.refs_0_), channel_id=1, source_target_pairs={{0,0},{1,4},{2,8},{3,12},{4,1},{5,5},{6,9},{7,13},{8,2},{9,6},{10,... | collective-permute-start | bytes 393224 | tf_op jit(solution)/shard_map/ppermute | solution.py:85
  90.0 23.6 %all-to-all-start.1 = ((bf16[8,512,128]{2,1,0:T(8,128)(2,1)}), bf16[8,512,128]{2,1,0:T(8,128)(2,1)S(1)}, u32[]{:S(2)}, u32[]{:S(2)}) async-start(bf16[8,512,128]{2,1,0:T(8,128)(2,1)} %get-tuple-element.70), calls=%async_computation.1 | async-start | bytes 2097152 | tf_op jit(solution)/shard_map/all_to_all | solution.py:447
  93.6 8.0 %collective-permute-start.23 = (bf16[512,128]{1,0:T(8,128)(2,1)}, bf16[512,128]{1,0:T(8,128)(2,1)S(1)}, u32[]{:S(2)}, u32[]{:S(2)}) collective-permute-start(bf16[512,128]{1,0:T(8,128)(2,1)} %get-tuple-element.65), channel_id=1, source_target_pairs={{0,0},{1,4},{2,8},{3,12},{4,1},{5,5},{6,9},{7,13},{8,2},{9,6},{10,... | collective-permute-start | bytes 393224 | tf_op jit(solution)/shard_map/ppermute | solution.py:85
  95.1 6.5 %collective-permute-start.24 = (bf16[512,128]{1,0:T(8,128)(2,1)}, bf16[512,128]{1,0:T(8,128)(2,1)S(1)}, u32[]{:S(2)}, u32[]{:S(2)}) collective-permute-start(bf16[512,128]{1,0:T(8,128)(2,1)} %get-tuple-element.66), channel_id=1, source_target_pairs={{0,1},{1,5},{2,9},{3,13},{4,0},{5,4},{6,8},{7,12},{8,3},{9,7},{10,... | collective-permute-start | bytes 393224 | tf_op jit(solution)/shard_map/ppermute | solution.py:85
  98.6 15.0 %collective-permute-start.25 = (bf16[512,128]{1,0:T(8,128)(2,1)}, bf16[512,128]{1,0:T(8,128)(2,1)S(1)}, u32[]{:S(2)}, u32[]{:S(2)}) collective-permute-start(bf16[512,128]{1,0:T(8,128)(2,1)} %get-tuple-element.67), channel_id=1, source_target_pairs={{0,2},{1,6},{2,10},{3,14},{4,3},{5,7},{6,11},{7,15},{8,0},{9,4},{1... | collective-permute-start | bytes 393224 | tf_op jit(solution)/shard_map/ppermute | solution.py:85
  100.2 13.4 %collective-permute-start.26 = (bf16[512,128]{1,0:T(8,128)(2,1)S(1)}, bf16[512,128]{1,0:T(8,128)(2,1)S(1)}, u32[]{:S(2)}, u32[]{:S(2)}) collective-permute-start(bf16[512,128]{1,0:T(8,128)(2,1)S(1)} %get-tuple-element.68), channel_id=1, source_target_pairs={{0,3},{1,7},{2,11},{3,15},{4,2},{5,6},{6,10},{7,14},{8,1},{9,5},{1... | collective-permute-start | bytes 393224 | tf_op jit(solution)/shard_map/ppermute | solution.py:85
  115.4 6.1 %collective-permute-start.31 = (bf16[512,128]{1,0:T(8,128)(2,1)S(1)}, bf16[512,128]{1,0:T(8,128)(2,1)S(1)}, u32[]{:S(2)}, u32[]{:S(2)}) collective-permute-start(bf16[512,128]{1,0:T(8,128)(2,1)S(1)} %get-tuple-element.73), channel_id=1, source_target_pairs={{0,1},{1,0},{2,3},{3,2},{4,5},{5,4},{6,7},{7,6},{8,9},{9,8},{10,11... | collective-permute-start | bytes 393224 | tf_op jit(solution)/shard_map/ppermute | solution.py:74
  115.5 12.8 %collective-permute-start.32 = (bf16[512,128]{1,0:T(8,128)(2,1)S(1)}, bf16[512,128]{1,0:T(8,128)(2,1)S(1)}, u32[]{:S(2)}, u32[]{:S(2)}) collective-permute-start(bf16[512,128]{1,0:T(8,128)(2,1)S(1)} %get-tuple-element.74), channel_id=1, source_target_pairs={{0,2},{1,3},{2,0},{3,1},{4,6},{5,7},{6,4},{7,5},{8,10},{9,11},{10,... | collective-permute-start | bytes 393224 | tf_op jit(solution)/shard_map/ppermute | solution.py:74
  117.9 10.4 %collective-permute-start.33 = (bf16[512,128]{1,0:T(8,128)(2,1)S(1)}, bf16[512,128]{1,0:T(8,128)(2,1)S(1)}, u32[]{:S(2)}, u32[]{:S(2)}) collective-permute-start(bf16[512,128]{1,0:T(8,128)(2,1)S(1)} %get-tuple-element.75), channel_id=1, source_target_pairs={{0,3},{1,2},{2,1},{3,0},{4,7},{5,6},{6,5},{7,4},{8,11},{9,10},{10,... | collective-permute-start | bytes 393224 | tf_op jit(solution)/shard_map/ppermute | solution.py:74
  (19 other events, 223.2 us)

commit v5 on v4

--- a/solution.py
+++ b/solution.py
@@ -11,7 +11,9 @@
 SLOTS = 8
 CAP = 256
 LANES = 128
+LANE_BITS = 7
 DIGIT = 64
+DIGIT_BITS = 6
 ID_ROWS = 16
 BF = jnp.bfloat16
 F32 = jnp.float32
@@ -88,7 +90,7 @@
         return lax.ppermute(x, both, [(at(j, s) * M + m, at(m ^ r, s) * M + j) for s, j, m in devices])
 
     def split(info, ef, wm, wa, we, wu, af, *refs):
-        g, m = info[0], info[1]
+        g, m = lax.axis_index("graph"), lax.axis_index("mp")
         outs, share, quarters, sem = refs[:M], refs[M], refs[M + 1 : 2 * M + 1], refs[2 * M + 1]
         part = quarters[0].shape[0]
         moves = []
@@ -110,16 +112,15 @@
             c.wait()
 
     def stack(info, *refs):
-        parts, (out, we) = refs[:M], refs[M:]
+        parts, (wm, wa, we) = refs[:M], refs[M:]
         n = we.shape[1]
         for k in range(M):
-            for j in range(out.shape[0] // (M * n)):
-                out[(j * M + k) * n : (j * M + k + 1) * n, :] = parts[k][j * n : (j + 1) * n, :]
+            wm[k * n : (k + 1) * n, :] = parts[k][:n, :]
+            wa[k] = parts[k][n : 2 * n, :]
             we[k] = parts[k][2 * n : 3 * n, :]
 
     def digits(ids):
-        high = lax.div(ids, DIGIT)
-        return high.astype(F32), (ids - high * DIGIT).astype(F32)
+        return (ids >> DIGIT_BITS).astype(F32), (ids & (DIGIT - 1)).astype(F32)
 
     def triplets(info, *refs):
         m = info[1]
@@ -129,7 +130,7 @@
             x_out[:, lanes(m ^ k, w)] = xs[k][...]
         downt = dot_t(wdt[...], x_out[...]).astype(BF)
         dt = downt.shape[0]
-        ids = lax.rem(partner[...], CAP)
+        ids = partner[...] & (CAP - 1)
         rows = lax.broadcasted_iota(jnp.int32, (CAP, CAP), 0)
         picked = []
         for s in range(SLOTS):
@@ -164,9 +165,22 @@
                 here = pl.ds(pl.multiple_of((g ^ d) * n, n), n)
                 dst[here, lanes(m ^ k, width)] = shares[d][k * n : (k + 1) * n, :]
 
+    def whole_weight(info, own, other, wa):
+        g, m = info[0], info[1]
+        n, width = own.shape[1] // (M // 2), own.shape[2]
+
+        def put(d, _):
+            for core, half in ((g % 2, own), ((g + 1) % 2, other)):
+                for j in range(M // 2):
+                    cols = lanes(m ^ (core * (M // 2) + j), width)
+                    wa[pl.ds(pl.multiple_of(d * n, n), n), cols] = half[d, j * n : (j + 1) * n, :]
+            return 0
+
+        lax.fori_loop(0, G, put, 0, unroll=G <= 8)
+
     def messages(info, *refs):
         m, atoms = info[1], info[2]
-        up, shares, (x, bil, live, tgt, src, total_out, out, wm, wu) = refs[:M], refs[M : M + G], refs[M + G :]
+        up, shares, (ride, x, bil, live, tgt, src, total_out, out, wm, wu) = refs[:M], refs[M : M + G], refs[M + G :]
         width = out.shape[3]
         dt = wu.shape[0]
 
@@ -185,17 +199,21 @@
         lines = [[x[:, c : c + LANES] for x in pair for c in range(0, CAP, LANES)] for pair in ends]
         lines[0].append(jnp.zeros((ID_ROWS - len(lines[0]), LANES), F32))
         lines = [jnp.concatenate(part, axis=0).astype(BF) for part in lines]
+        id_rows = CAP + ID_ROWS + lines[1].shape[0]
         for f in range(M):
             out[0, f, :CAP, :] = sent[:, f * width : (f + 1) * width]
             out[0, f, CAP : CAP + ID_ROWS, :] = lines[0]
-            out[0, f, CAP + ID_ROWS :, :] = lines[1]
+            out[0, f, CAP + ID_ROWS : id_rows, :] = lines[1]
+            for j in range(M // 2):
+                here = slice(id_rows + j * ride.shape[1], id_rows + (j + 1) * ride.shape[1])
+                out[0, f, here, :] = ride[f % 2 * (M // 2) + j]
 
     def arrived(info, *refs):
         refs[-1][...] = jnp.zeros(refs[-1].shape, F32)
 
     def aggregate(info, incoming, _, *refs):
         f = info[0] % M
-        outs, (ids, sent, onehot, values, agg) = refs[:M], refs[M:]
+        outs, (ids, sent, ride, onehot, values, agg) = refs[:M], refs[M:]
         part, width = outs[0].shape
         half = agg.shape[0] // 2
         step = onehot.shape[0]
@@ -207,6 +225,7 @@
             high = jnp.concatenate([lines[c : c + 1, :] for c in range(n)], axis=1)
             row = high * DIGIT + jnp.concatenate([lines[n + c : n + c + 1, :] for c in range(n)], axis=1)
             ids[g] = row.astype(jnp.int32)
+            ride[g] = incoming[g, incoming.shape[1] - ride.shape[1] :, :]
             upper = (column(row) >= half).astype(F32)
             rows = incoming[g, :CAP, :].astype(F32)
             values[block_rows(g), :width] = (rows * (1.0 - upper)).astype(BF)
@@ -214,13 +233,15 @@
             return 0
 
         lax.fori_loop(0, G, place, 0, unroll=G <= 8)
-        sent[...] = incoming[at(info[1], info[0] // M), CAP + ID_ROWS :, :]
+        n = CAP + ID_ROWS
+        sent[...] = incoming[at(info[1], info[0] // M), n : n + sent.shape[0], :]
         for q in range(half // step):
 
             def fill(g, _):
-                row = lax.rem(ids[g], half)
-                near = (low == lax.rem(row, LANES)).astype(F32).astype(BF)
-                far = jnp.broadcast_to(lax.div(row, LANES) - q * (step // LANES), (LANES, CAP)).astype(F32).astype(BF)
+                row = ids[g]
+                row = jnp.where(row >= half, row - half, row)
+                near = (low == (row & (LANES - 1))).astype(F32).astype(BF)
+                far = jnp.broadcast_to(((row >> LANE_BITS) - q * (step // LANES)).astype(F32), (LANES, CAP)).astype(BF)
                 for h in range(step // LANES):
                     onehot[h * LANES : (h + 1) * LANES, lanes(g, CAP)] = jnp.where(
                         far == BF(h), near, jnp.zeros_like(near)
@@ -237,12 +258,11 @@
     def atom_layer(info, *refs):
         g, m = info[0], info[1]
         f = g % M
-        sums, feats, shares = refs[:M], refs[M : 2 * M], refs[2 * M : 2 * M + G]
-        outs, (x, wa) = refs[2 * M + G : 3 * M + G], refs[3 * M + G :]
+        sums, feats, wa = refs[:M], refs[M : 2 * M], refs[2 * M]
+        outs, x = refs[2 * M + 1 : 3 * M + 1], refs[3 * M + 1]
         part, width = sums[0].shape
         for r in range(M):
             x[:, lanes(f ^ r, width)] = (feats[r][...].astype(F32) + sums[r][...].astype(F32)).astype(BF)
-        put_shares(info, shares, wa)
         ahid = dot(x[...], wa[...])
         x[...] = (x[...].astype(F32) + silu(ahid)).astype(BF)
         for r in range(M):
@@ -261,17 +281,20 @@
             rows = pl.ds(pl.multiple_of(lax.rem(q, per_half) * part, part), part)
             table[rows, lanes(lax.div(q, per_half), width)] = parts[r][...]
 
+        spread = lax.broadcasted_iota(jnp.int32, (CAP, LANES), 1).astype(F32)
+
         def mark(row, line):
-            col = column(row)
-            upper = col >= half
-            col = lax.rem(col, half)
-            near = (lax.broadcasted_iota(jnp.int32, (CAP, LANES), 1) == lax.rem(col, LANES)).astype(F32).astype(BF)
-            far = jnp.broadcast_to(lax.div(col, LANES), (CAP, LANES)).astype(F32).astype(BF)
+            upper = row >= half
+            row = jnp.where(upper, row - half, row)
+            lines = [row & (LANES - 1), row >> LANE_BITS, upper.astype(jnp.int32), jnp.zeros((5, CAP), jnp.int32)]
+            cols = jnp.transpose(jnp.concatenate(lines, axis=0).astype(F32))
+            near = (spread == cols[:, 0:1]).astype(F32).astype(BF)
+            far = jnp.broadcast_to(cols[:, 1:2], (CAP, LANES)).astype(BF)
             for h in range(half // LANES):
                 onehot[line * CAP : (line + 1) * CAP, h * LANES : (h + 1) * LANES] = jnp.where(
                     far == BF(h), near, jnp.zeros_like(near)
                 )
-            return upper
+            return cols[:, 2:3] > 0.5
 
         def pick(line, upper):
             found = dot(onehot[line * CAP : (line + 1) * CAP, :], table[...])
@@ -347,7 +370,7 @@
         first = call(
             split,
             [sds((chunk, width))] * M + [sds((3 * share + dt, width))] + [sds((part, width))] * M,
-            info,
+            jnp.zeros((1,), jnp.int32),
             [ef, w_msg, w_atom, w_edge, w_up, af],
             scratch=[pltpu.SemaphoreType.DMA((M * per + M + 4,))],
             in_specs=[pl.BlockSpec(memory_space=pl.ANY)] * 6,
@@ -356,11 +379,16 @@
         chunks, w, feats = first[:M], first[M], first[M + 1 :]
         ws = [w] + [over_mp(w, k) for k in range(1, M)]
         xs = [chunks[0]] + [over_mp(chunks[k], k) for k in range(1, M)]
-        wm, we = call(stack, [sds((2 * M * share, width)), sds((M, share, width))], info, ws, flops=3e10)
+        wm, wa, we = call(
+            stack,
+            [sds((M * share, width)), sds((M, share, width)), sds((M, share, width))],
+            info,
+            ws,
+            flops=3e10,
+        )
         even = [wm] + [over_plane(wm, x) for x in range(2, G, 2)]
         odd = [over_plane(w, 1) for w in even]
         wm = [w for pair in zip(even, odd) for w in pair]
-        share_spec = lambda j: [pl.BlockSpec((M * share, width), lambda i, info: (j, 0))] * G
 
         blk = lambda i, info: at(info[1], i)
         x, bil = call(
@@ -380,12 +408,12 @@
         )
         total, outgoing = call(
             messages,
-            [sds((chunk, depth), F32), sds((per, M, CAP + id_rows, width))],
-            info,
-            ws + wm + [x, bil, live.reshape(G, CAP), etgt.reshape(G, CAP), esrc.reshape(G, CAP)],
+            [sds((chunk, depth), F32), sds((per, M, CAP + id_rows + M // 2 * share, width))],
+            info,
+            ws + wm + [wa, x, bil, live.reshape(G, CAP), etgt.reshape(G, CAP), esrc.reshape(G, CAP)],
             scratch=[pltpu.VMEM((depth, depth), BF), pltpu.VMEM((dt, depth), BF)],
             grid=(per,),
-            in_specs=[None] * M + share_spec(0)
+            in_specs=[None] * (M + G + 1)
             + [
                 pl.BlockSpec((CAP, depth), lambda i, info: (i, 0)),
                 pl.BlockSpec((CAP, dt), lambda i, info: (i, 0)),
@@ -395,11 +423,11 @@
             ],
             out_specs=[
                 pl.BlockSpec((CAP, depth), lambda i, info: (i, 0)),
-                pl.BlockSpec((1, M, CAP + id_rows, width), lambda i, info: (i, 0, 0, 0)),
+                pl.BlockSpec((1, M, CAP + id_rows + M // 2 * share, width), lambda i, info: (i, 0, 0, 0)),
             ],
         )
         incoming = lax.all_to_all(
-            outgoing.reshape(G, CAP + id_rows, width), "graph", split_axis=0, concat_axis=0, tiled=True
+            outgoing.reshape(G, CAP + id_rows + M // 2 * share, width), "graph", split_axis=0, concat_axis=0, tiled=True
         )
         feats = [away(feats[r], r) for r in range(M)]
         (token,) = call(
@@ -410,22 +438,22 @@
             in_specs=[pl.BlockSpec(memory_space=pl.ANY)] * M,
             flops=3e10,
         )
-        *sums, ids, sent = call(
+        *sums, ids, sent, wa = call(
             aggregate,
-            [sds((part, width))] * M + [sds((G, 1, CAP), jnp.int32), sds((2 * rows // LANES, width))],
+            [sds((part, width))] * M + [sds((G, 1, CAP), jnp.int32), sds((2 * rows // LANES, width)), sds((G, M // 2 * share, width))],
             info,
             [incoming, token],
             scratch=[pltpu.VMEM((part, G * CAP), BF), pltpu.VMEM((G * CAP, 2 * width), BF), pltpu.VMEM((atoms, width), BF)],
             flops=3.0e9,
         )
         sums = [sums[0]] + [over_plane(sums[r], r) for r in range(1, M)]
+        (wa,) = call(whole_weight, [sds((depth, depth))], info, [wa, over_plane(wa, 1)], flops=1e9)
         outs = call(
             atom_layer,
             [sds((part, width))] * M,
             info,
-            sums + feats + wm,
-            scratch=[pltpu.VMEM((part, depth), BF), pltpu.VMEM((depth, depth), BF)],
-            in_specs=[None] * (2 * M) + share_spec(1),
+            sums + feats + [wa],
+            scratch=[pltpu.VMEM((part, depth), BF)],
             flops=1.5e9,
         )
         homeward = [home(outs[r], r) for r in range(M)]

time: 130 us -> 128 us (0.985)
  waiting for transfers between devices: 49 us -> 46.5 us
  starting transfers between devices: 52.2 us -> 54 us
    ppermute x13 -> x14, waiting for transfers between devices: 15.5 us -> 11 us  [over_plane(): return lax.ppermute(x, 'graph', [(i, i ^ k) for i in range(G)])]
    all_to_all x1, waiting for transfers between devices: 3.9 us -> 6.97 us  [local(): lax.all_to_all(outgoing.reshape(G, CAP + id_rows + M // 2 * share, width)...]
    ppermute x9, waiting for transfers between devices: 11.3 us -> 9.6 us  [over_mp(): return lax.ppermute(x, 'mp', [(i, i ^ k) for i in range(M)])]
    ppermute x13 -> x14, starting transfers between devices: 7.61 us -> 9.26 us  [over_plane(): return lax.ppermute(x, 'graph', [(i, i ^ k) for i in range(G)])]
    all_to_all x1, starting transfers between devices: 3.57 us -> 5.17 us  [local(): lax.all_to_all(named, 'graph', split_axis=0, concat_axis=0, tiled=True)]
    pallas_call x11 -> x12, Pallas kernels: 25.4 us -> 24.1 us  [call(): pl.pallas_call(kernel, out_shape=list(out_shapes), grid_spec=pltpu.Prefet...]
  transfers between devices with their start and end apart: 36 -> 37, of which waited for: 15 -> 11; matrix products, arithmetic and copies ran while one was open for 0% -> 0% of each run, Pallas kernels for 11% -> 12%
where the time goes in v5:
time: 128 us; the launch traced here: 127 us
  starting transfers between devices  54 us (42%)
  waiting for transfers between devices  46.5 us (36%)
  Pallas kernels  24.1 us (19%)
  local copies, waits for them, and re-layouts  1.57 us (1%)
    pallas_call x12, Pallas kernels, call(): pl.pallas_call(kernel, out_shape=list(out_shapes), grid_spec=pltpu.Prefet...  24.1 us
    ppermute x9, starting transfers between devices, over_mp(): return lax.ppermute(x, 'mp', [(i, i ^ k) for i in range(M)])  16.5 us
    ppermute x8, waiting for transfers between devices, home(): lax.ppermute(x, both, [(at(i, s) * M + z, at(z, s) * M + (i ^ r)) for s,...  12.8 us
    ppermute x14, waiting for transfers between devices, over_plane(): return lax.ppermute(x, 'graph', [(i, i ^ k) for i in range(G)])  11 us
    ppermute x8, starting transfers between devices, home(): lax.ppermute(x, both, [(at(i, s) * M + z, at(z, s) * M + (i ^ r)) for s,...  10.7 us
    ppermute x9, waiting for transfers between devices, over_mp(): return lax.ppermute(x, 'mp', [(i, i ^ k) for i in range(M)])  9.6 us
    ppermute x14, starting transfers between devices, over_plane(): return lax.ppermute(x, 'graph', [(i, i ^ k) for i in range(G)])  9.26 us
    all_to_all x1, waiting for transfers between devices, local(): lax.all_to_all(outgoing.reshape(G, CAP + id_rows + M // 2 * share, width)...  6.97 us
  transfers between devices with their start and end apart: 37, of which 11 were waited for; matrix products, arithmetic and copies ran while one was open for 0% of the time, Pallas kernels for 12%

profile of v5, /device:TPU:0, one launch (start us, length us, event | category | flops | bytes accessed | tf_op | source)
XLA Modules:
  0.0 127.1 jit_solution(10852525339045081608)
XLA Ops:
  0.6 2.4 %shard_map.149 = (bf16[512,128]{1,0:T(8,128)(2,1)}, bf16[512,128]{1,0:T(8,128)(2,1)}, bf16[512,128]{1,0:T(8,128)(2,1)}, bf16[512,128]{1,0:T(8,128)(2,1)}, bf16[2...) custom-call(s32[1]{0:T(128)} %constant.12.clone.1.info, ...), custom_call_target="tpu_custom_call" | custom-call | tf_op jit(solution)/shard_map/pallas_call | solution.py:41
  3.1 5.1 %collective-permute-start.2 = (bf16[256,128]{1,0:T(8,128)(2,1)}, bf16[256,128]{1,0:T(8,128)(2,1)S(1)}, u32[]{:S(2)}, u32[]{:S(2)}) collective-permute-start(bf16[256,128]{1,0:T(8,128)(2,1)} %get-tuple-element.43.refs_0_), channel_id=1, source_target_pairs={{0,3},{1,2},{2,1},{3,0},{4,7},{5,6},{6,5},{7,4},{8,11},{9,10},{10,... | collective-permute-start | bytes 196616 | tf_op jit(solution)/shard_map/ppermute | solution.py:76
  8.8 1.4 %collective-permute-start.10 = (bf16[512,128]{1,0:T(8,128)(2,1)}, bf16[512,128]{1,0:T(8,128)(2,1)S(1)}, u32[]{:S(2)}, u32[]{:S(2)}) collective-permute-start(bf16[512,128]{1,0:T(8,128)(2,1)} %get-tuple-element.47), channel_id=1, source_target_pairs={{0,1},{1,0},{2,3},{3,2},{4,5},{5,4},{6,7},{7,6},{8,9},{9,8},{10,11... | collective-permute-start | bytes 393224 | tf_op jit(solution)/shard_map/ppermute | solution.py:76
  10.2 2.9 %collective-permute-start.11 = (bf16[512,128]{1,0:T(8,128)(2,1)}, bf16[512,128]{1,0:T(8,128)(2,1)S(1)}, u32[]{:S(2)}, u32[]{:S(2)}) collective-permute-start(bf16[512,128]{1,0:T(8,128)(2,1)} %get-tuple-element.48), channel_id=1, source_target_pairs={{0,2},{1,3},{2,0},{3,1},{4,6},{5,7},{6,4},{7,5},{8,10},{9,11},{10,... | collective-permute-start | bytes 393224 | tf_op jit(solution)/shard_map/ppermute | solution.py:76
  13.2 2.0 %collective-permute-start.12 = (bf16[512,128]{1,0:T(8,128)(2,1)}, bf16[512,128]{1,0:T(8,128)(2,1)S(1)}, u32[]{:S(2)}, u32[]{:S(2)}) collective-permute-start(bf16[512,128]{1,0:T(8,128)(2,1)} %get-tuple-element.49), channel_id=1, source_target_pairs={{0,3},{1,2},{2,1},{3,0},{4,7},{5,6},{6,5},{7,4},{8,11},{9,10},{10,... | collective-permute-start | bytes 393224 | tf_op jit(solution)/shard_map/ppermute | solution.py:76
  17.6 2.8 %collective-permute-start.8 = (bf16[256,128]{1,0:T(8,128)(2,1)S(1)}, bf16[256,128]{1,0:T(8,128)(2,1)S(1)}, u32[]{:S(2)}, u32[]{:S(2)}) collective-permute-start(bf16[256,128]{1,0:T(8,128)(2,1)S(1)} %get-tuple-element.44.refs_4_), channel_id=1, source_target_pairs={{0,24},{4,28},{8,16},{12,20},{16,8},{20,12},{24,0},{28,4},{1,25},{... | collective-permute-start | bytes 196616 | tf_op jit(solution)/shard_map/ppermute | solution.py:79
  21.4 2.0 %collective-permute-done.11.refs_2_ = bf16[512,128]{1,0:T(8,128)(2,1)S(1)} collective-permute-done((bf16[512,128]{1,0:T(8,128)(2,1)}, bf16[512,128]{1,0:T(8,128)(2,1)S(1)}, u32[]{:S(2)}, u32[]{:S(2)}) %collective-permute-start.11) | collective-permute-done | bytes 131104 | tf_op jit(solution)/shard_map/ppermute | solution.py:76
  24.7 1.6 %collective-permute-start.13 = (bf16[512,128]{1,0:T(8,128)(2,1)}, bf16[512,128]{1,0:T(8,128)(2,1)S(1)}, u32[]{:S(2)}, u32[]{:S(2)}) collective-permute-start(bf16[512,128]{1,0:T(8,128)(2,1)} %get-tuple-element.53), channel_id=1, source_target_pairs={{0,0},{1,4},{2,8},{3,12},{4,1},{5,5},{6,9},{7,13},{8,2},{9,6},{10,... | collective-permute-start | bytes 393224 | tf_op jit(solution)/shard_map/ppermute | solution.py:90
  26.2 1.7 %collective-permute-start.14 = (bf16[512,128]{1,0:T(8,128)(2,1)}, bf16[512,128]{1,0:T(8,128)(2,1)S(1)}, u32[]{:S(2)}, u32[]{:S(2)}) collective-permute-start(bf16[512,128]{1,0:T(8,128)(2,1)} %get-tuple-element.54), channel_id=1, source_target_pairs={{0,4},{1,0},{2,12},{3,8},{4,5},{5,1},{6,13},{7,9},{8,6},{9,2},{10,... | collective-permute-start | bytes 393224 | tf_op jit(solution)/shard_map/ppermute | solution.py:90
  27.9 3.5 %collective-permute-start.15 = (bf16[512,128]{1,0:T(8,128)(2,1)}, bf16[512,128]{1,0:T(8,128)(2,1)S(1)}, u32[]{:S(2)}, u32[]{:S(2)}) collective-permute-start(bf16[512,128]{1,0:T(8,128)(2,1)} %get-tuple-element.55), channel_id=1, source_target_pairs={{0,8},{1,12},{2,0},{3,4},{4,9},{5,13},{6,1},{7,5},{8,10},{9,14},{1... | collective-permute-start | bytes 393224 | tf_op jit(solution)/shard_map/ppermute | solution.py:90
  32.9 3.1 %shard_map.151 = (bf16[512,512]{1,0:T(8,128)(2,1)S(1)}, bf16[512,64]{1,0:T(8,128)(2,1)S(1)}) custom-call(s32[3]{0:T(128)S(1)} %pad_add_fusion.info, bf16[512,128]{1,0:T(8,128)(2,1)S(1)} %copy-done.2, bf16[512,128]{1,0:T(8,128)(2,1)S(1)} %collective-permute-done.10.refs_1_, bf16[512,128]{1,0:T(8,128)(2,1)S(1)} %collective-permute-done.11.refs_2_, ...), custom_call_target="tpu_custom_call" | custom-call | tf_op jit(solution)/shard_map/pallas_call | solution.py:41
  36.0 2.8 %shard_map.152 = (f32[512,512]{1,0:T(8,128)S(1)}, bf16[2,4,432,128]{3,2,1,0:T(8,128)(2,1)}) custom-call(s32[3]{0:T(128)S(1)} %pad_add_fusion.info, bf16[256,128]{1,0:T(8,128)(2,1)S(1)} %copy-done.7, bf16[256,128]{1,0:T(8,128)(2,1)S(1)} %collective-permute-done.refs_1_, bf16[256,128]{1,0:T(8,128)(2,1)S(1)} %collective-permute-done.1.refs_2_, ...), custom_call_target="tpu_custom_call" | custom-call | tf_op jit(solution)/shard_map/pallas_call | solution.py:41
  38.8 5.7 %all-to-all-start = ((bf16[8,432,128]{2,1,0:T(8,128)(2,1)}), bf16[8,432,128]{2,1,0:T(8,128)(2,1)S(1)}, u32[]{:S(2)}, u32[]{:S(2)}) async-start(bf16[8,432,128]{2,1,0:T(8,128)(2,1)} %bitcast.4), calls=%async_computation | async-start | bytes 1769472 | tf_op jit(solution)/shard_map/all_to_all | solution.py:429
  44.6 6.1 %collective-permute-done.15.refs_2_.refs_6_ = bf16[512,128]{1,0:T(8,128)(2,1)S(1)} collective-permute-done((bf16[512,128]{1,0:T(8,128)(2,1)}, bf16[512,128]{1,0:T(8,128)(2,1)S(1)}, u32[]{:S(2)}, u32[]{:S(2)}) %collective-permute-start.15) | collective-permute-done | bytes 131104 | tf_op jit(solution)/shard_map/ppermute | solution.py:90
  51.2 7.0 %all-to-all-done.incoming = bf16[8,432,128]{2,1,0:T(8,128)(2,1)S(1)} async-done(((bf16[8,432,128]{2,1,0:T(8,128)(2,1)}), bf16[8,432,128]{2,1,0:T(8,128)(2,1)S(1)}, u32[]{:S(2)}, u32[]{:S(2)}) %all-to-all-start) | async-done | bytes 884768 | tf_op jit(solution)/shard_map/all_to_all | solution.py:429
  58.2 2.4 %shard_map.154 = (bf16[512,128]{1,0:T(8,128)(2,1)S(1)}, bf16[512,128]{1,0:T(8,128)(2,1)S(1)}, bf16[512,128]{1,0:T(8,128)(2,1)S(1)}, bf16[512,128]{1,0:T(8,128)(2...) custom-call(s32[3]{0:T(128)S(1)} %pad_add_fusion.info, ...), custom_call_target="tpu_custom_call" | custom-call | flops 3000000000 | tf_op jit(solution)/shard_map/pallas_call | solution.py:41
  63.3 4.3 %collective-permute-done.18.refs_2_ = bf16[512,128]{1,0:T(8,128)(2,1)S(1)} collective-permute-done((bf16[512,128]{1,0:T(8,128)(2,1)S(1)}, bf16[512,128]{1,0:T(8,128)(2,1)S(1)}, u32[]{:S(2)}, u32[]{:S(2)}) %collective-permute-start.18) | collective-permute-done | bytes 131104 | tf_op jit(solution)/shard_map/ppermute | solution.py:79
  68.6 1.4 %shard_map.156 = (bf16[512,128]{1,0:T(8,128)(2,1)S(1)}, bf16[512,128]{1,0:T(8,128)(2,1)S(1)}, bf16[512,128]{1,0:T(8,128)(2,1)S(1)}, bf16[512,128]{1,0:T(8,128)(2,1)S(1)}) custom-call(s32[3]{0:T(128)S(1)} %pad_add_fusion.info, bf16[512,128]{1,0:T(8,128)(2,1)S(1)} %get-tuple-element.57.refs_0_, bf16[512,128]{1,0:T(8,128)(2,1)S(1)} %collective-permute-done.17.refs_1_, ...), custom_call_target="tpu_custom_call" | custom-call | flops 1500000000 | tf_op jit(solution)/shard_map/pallas_call | solution.py:41
  73.3 1.6 %collective-permute-start.31 = (bf16[512,128]{1,0:T(8,128)(2,1)S(1)}, bf16[512,128]{1,0:T(8,128)(2,1)S(1)}, u32[]{:S(2)}, u32[]{:S(2)}) collective-permute-start(bf16[512,128]{1,0:T(8,128)(2,1)S(1)} %get-tuple-element.65), channel_id=1, source_target_pairs={{0,3},{1,7},{2,11},{3,15},{4,2},{5,6},{6,10},{7,14},{8,1},{9,5},{1... | collective-permute-start | bytes 393224 | tf_op jit(solution)/shard_map/ppermute | solution.py:87
  74.9 2.3 %collective-permute-done.22.refs_2_ = bf16[512,128]{1,0:T(8,128)(2,1)S(1)} collective-permute-done((bf16[512,128]{1,0:T(8,128)(2,1)S(1)}, bf16[512,128]{1,0:T(8,128)(2,1)S(1)}, u32[]{:S(2)}, u32[]{:S(2)}) %collective-permute-start.22) | collective-permute-done | bytes 131104 | tf_op jit(solution)/shard_map/ppermute | solution.py:79
  77.8 2.6 %collective-permute-done.23.refs_3_ = bf16[512,128]{1,0:T(8,128)(2,1)S(1)} collective-permute-done((bf16[512,128]{1,0:T(8,128)(2,1)S(1)}, bf16[512,128]{1,0:T(8,128)(2,1)S(1)}, u32[]{:S(2)}, u32[]{:S(2)}) %collective-permute-start.23) | collective-permute-done | bytes 131104 | tf_op jit(solution)/shard_map/ppermute | solution.py:79
  80.5 5.7 %shard_map.157 = (bf16[512,128]{1,0:T(8,128)(2,1)}, bf16[512,128]{1,0:T(8,128)(2,1)}, bf16[512,128]{1,0:T(8,128)(2,1)S(1)}, bf16[512,128]{1,0:T(8,128)(2,1)S(1)}, bf16[8,512,128]{2,1,0:T(8,128)(2,1)}) custom-call(s32[3]{0:T(128)S(1)} %pad_add_fusion.info, bf16[512,128]{1,0:T(8,128)(2,1)S(1)} %get-tuple-element.62.refs_0_, ...), custom_call_target="tpu_custom_call" | custom-call | flops 6000000000 | tf_op jit(solution)/shard_map/pallas_call | solution.py:41
  86.1 5.2 %all-to-all-start.1 = ((bf16[8,512,128]{2,1,0:T(8,128)(2,1)}), bf16[8,512,128]{2,1,0:T(8,128)(2,1)S(1)}, u32[]{:S(2)}, u32[]{:S(2)}) async-start(bf16[8,512,128]{2,1,0:T(8,128)(2,1)} %get-tuple-element.74), calls=%async_computation.1 | async-start | bytes 2097152 | tf_op jit(solution)/shard_map/all_to_all | solution.py:475
  91.3 1.6 %collective-permute-start.24 = (bf16[512,128]{1,0:T(8,128)(2,1)}, bf16[512,128]{1,0:T(8,128)(2,1)S(1)}, u32[]{:S(2)}, u32[]{:S(2)}) collective-permute-start(bf16[512,128]{1,0:T(8,128)(2,1)} %get-tuple-element.69), channel_id=1, source_target_pairs={{0,0},{1,4},{2,8},{3,12},{4,1},{5,5},{6,9},{7,13},{8,2},{9,6},{10,... | collective-permute-start | bytes 393224 | tf_op jit(solution)/shard_map/ppermute | solution.py:87
  92.9 2.5 %collective-permute-start.25 = (bf16[512,128]{1,0:T(8,128)(2,1)}, bf16[512,128]{1,0:T(8,128)(2,1)S(1)}, u32[]{:S(2)}, u32[]{:S(2)}) collective-permute-start(bf16[512,128]{1,0:T(8,128)(2,1)} %get-tuple-element.70), channel_id=1, source_target_pairs={{0,1},{1,5},{2,9},{3,13},{4,0},{5,4},{6,8},{7,12},{8,3},{9,7},{10,... | collective-permute-start | bytes 393224 | tf_op jit(solution)/shard_map/ppermute | solution.py:87
  95.4 2.3 %collective-permute-start.26 = (bf16[512,128]{1,0:T(8,128)(2,1)S(1)}, bf16[512,128]{1,0:T(8,128)(2,1)S(1)}, u32[]{:S(2)}, u32[]{:S(2)}) collective-permute-start(bf16[512,128]{1,0:T(8,128)(2,1)S(1)} %get-tuple-element.71), channel_id=1, source_target_pairs={{0,2},{1,6},{2,10},{3,14},{4,3},{5,7},{6,11},{7,15},{8,0},{9,4},{1... | collective-permute-start | bytes 393224 | tf_op jit(solution)/shard_map/ppermute | solution.py:87
  98.7 12.8 %collective-permute-done.26.refs_2_ = bf16[512,128]{1,0:T(8,128)(2,1)S(1)} collective-permute-done((bf16[512,128]{1,0:T(8,128)(2,1)S(1)}, bf16[512,128]{1,0:T(8,128)(2,1)S(1)}, u32[]{:S(2)}, u32[]{:S(2)}) %collective-permute-start.26) | collective-permute-done | bytes 131104 | tf_op jit(solution)/shard_map/ppermute | solution.py:87
  111.4 1.8 %shard_map.158 = (bf16[512,128]{1,0:T(8,128)(2,1)S(1)}, bf16[512,128]{1,0:T(8,128)(2,1)S(1)}, bf16[512,128]{1,0:T(8,128)(2,1)S(1)}, bf16[512,128]{1,0:T(8,128)(2,1)S(1)}) custom-call(s32[3]{0:T(128)S(1)} %pad_add_fusion.info, bf16[512,128]{1,0:T(8,128)(2,1)S(1)} %collective-permute-done.24.refs_0_, bf16[512,128]{1,0:T(8,128)(2,1)S(1)} %collective-permute-done.25.refs_1_, ...), custom_call_target="tpu_custom_call" | custom-call | tf_op jit(solution)/shard_map/pallas_call | solution.py:41
  113.3 2.4 %collective-permute-start.33 = (bf16[512,128]{1,0:T(8,128)(2,1)S(1)}, bf16[512,128]{1,0:T(8,128)(2,1)S(1)}, u32[]{:S(2)}, u32[]{:S(2)}) collective-permute-start(bf16[512,128]{1,0:T(8,128)(2,1)S(1)} %get-tuple-element.78), channel_id=1, source_target_pairs={{0,2},{1,3},{2,0},{3,1},{4,6},{5,7},{6,4},{7,5},{8,10},{9,11},{10,... | collective-permute-start | bytes 393224 | tf_op jit(solution)/shard_map/ppermute | solution.py:76
  115.7 2.0 %collective-permute-start.34 = (bf16[512,128]{1,0:T(8,128)(2,1)S(1)}, bf16[512,128]{1,0:T(8,128)(2,1)S(1)}, u32[]{:S(2)}, u32[]{:S(2)}) collective-permute-start(bf16[512,128]{1,0:T(8,128)(2,1)S(1)} %get-tuple-element.79), channel_id=1, source_target_pairs={{0,3},{1,2},{2,1},{3,0},{4,7},{5,6},{6,5},{7,4},{8,11},{9,10},{10,... | collective-permute-start | bytes 393224 | tf_op jit(solution)/shard_map/ppermute | solution.py:76
  119.1 6.7 %collective-permute-done.33.refs_2_ = bf16[512,128]{1,0:T(8,128)(2,1)S(1)} collective-permute-done((bf16[512,128]{1,0:T(8,128)(2,1)S(1)}, bf16[512,128]{1,0:T(8,128)(2,1)S(1)}, u32[]{:S(2)}, u32[]{:S(2)}) %collective-permute-start.33) | collective-permute-done | bytes 131104 | tf_op jit(solution)/shard_map/ppermute | solution.py:76
  125.8 1.4 %shard_map.159 = bf16[2048,128]{1,0:T(8,128)(2,1)} custom-call(s32[3]{0:T(128)S(1)} %pad_add_fusion.info, bf16[512,128]{1,0:T(8,128)(2,1)S(1)} %get-tuple-element.76.refs_0_, bf16[512,128]{1,0:T(8,128)(2,1)S(1)} %collective-permute-done.32.refs_1_, bf16[512,128]{1,0:T(8,128)(2,1)S(1)} %collective-permute-done.33.refs_2_, ...), custom_call_target="tpu_custom_call" | custom-call | flops 1000000000 | tf_op jit(solution)/shard_map/pallas_call | solution.py:41
  (80 shorter events, 17.3 us)
Async XLA Ops:
  3.1 10.1 %collective-permute-start.2 = (bf16[256,128]{1,0:T(8,128)(2,1)}, bf16[256,128]{1,0:T(8,128)(2,1)S(1)}, u32[]{:S(2)}, u32[]{:S(2)}) collective-permute-start(bf16[256,128]{1,0:T(8,128)(2,1)} %get-tuple-element.43.refs_0_), channel_id=1, source_target_pairs={{0,3},{1,2},{2,1},{3,0},{4,7},{5,6},{6,5},{7,4},{8,11},{9,10},{10,... | collective-permute-start | bytes 196616 | tf_op jit(solution)/shard_map/ppermute | solution.py:76
  8.2 7.0 %collective-permute-start.1 = (bf16[256,128]{1,0:T(8,128)(2,1)}, bf16[256,128]{1,0:T(8,128)(2,1)S(1)}, u32[]{:S(2)}, u32[]{:S(2)}) collective-permute-start(bf16[256,128]{1,0:T(8,128)(2,1)} %get-tuple-element.43.refs_0_), channel_id=1, source_target_pairs={{0,2},{1,3},{2,0},{3,1},{4,6},{5,7},{6,4},{7,5},{8,10},{9,11},{10,... | collective-permute-start | bytes 196616 | tf_op jit(solution)/shard_map/ppermute | solution.py:76
  8.2 7.9 %collective-permute-start = (bf16[256,128]{1,0:T(8,128)(2,1)}, bf16[256,128]{1,0:T(8,128)(2,1)S(1)}, u32[]{:S(2)}, u32[]{:S(2)}) collective-permute-start(bf16[256,128]{1,0:T(8,128)(2,1)} %get-tuple-element.43.refs_0_), channel_id=1, source_target_pairs={{0,1},{1,0},{2,3},{3,2},{4,5},{5,4},{6,7},{7,6},{8,9},{9,8},{10,11... | collective-permute-start | bytes 196616 | tf_op jit(solution)/shard_map/ppermute | solution.py:76
  8.8 12.1 %collective-permute-start.10 = (bf16[512,128]{1,0:T(8,128)(2,1)}, bf16[512,128]{1,0:T(8,128)(2,1)S(1)}, u32[]{:S(2)}, u32[]{:S(2)}) collective-permute-start(bf16[512,128]{1,0:T(8,128)(2,1)} %get-tuple-element.47), channel_id=1, source_target_pairs={{0,1},{1,0},{2,3},{3,2},{4,5},{5,4},{6,7},{7,6},{8,9},{9,8},{10,11... | collective-permute-start | bytes 393224 | tf_op jit(solution)/shard_map/ppermute | solution.py:76
  10.2 13.2 %collective-permute-start.11 = (bf16[512,128]{1,0:T(8,128)(2,1)}, bf16[512,128]{1,0:T(8,128)(2,1)S(1)}, u32[]{:S(2)}, u32[]{:S(2)}) collective-permute-start(bf16[512,128]{1,0:T(8,128)(2,1)} %get-tuple-element.48), channel_id=1, source_target_pairs={{0,2},{1,3},{2,0},{3,1},{4,6},{5,7},{6,4},{7,5},{8,10},{9,11},{10,... | collective-permute-start | bytes 393224 | tf_op jit(solution)/shard_map/ppermute | solution.py:76
  13.2 11.4 %collective-permute-start.12 = (bf16[512,128]{1,0:T(8,128)(2,1)}, bf16[512,128]{1,0:T(8,128)(2,1)S(1)}, u32[]{:S(2)}, u32[]{:S(2)}) collective-permute-start(bf16[512,128]{1,0:T(8,128)(2,1)} %get-tuple-element.49), channel_id=1, source_target_pairs={{0,3},{1,2},{2,1},{3,0},{4,7},{5,6},{6,5},{7,4},{8,11},{9,10},{10,... | collective-permute-start | bytes 393224 | tf_op jit(solution)/shard_map/ppermute | solution.py:76
  17.6 5.8 %collective-permute-start.8 = (bf16[256,128]{1,0:T(8,128)(2,1)S(1)}, bf16[256,128]{1,0:T(8,128)(2,1)S(1)}, u32[]{:S(2)}, u32[]{:S(2)}) collective-permute-start(bf16[256,128]{1,0:T(8,128)(2,1)S(1)} %get-tuple-element.44.refs_4_), channel_id=1, source_target_pairs={{0,24},{4,28},{8,16},{12,20},{16,8},{20,12},{24,0},{28,4},{1,25},{... | collective-permute-start | bytes 196616 | tf_op jit(solution)/shard_map/ppermute | solution.py:79
  20.9 5.3 %collective-permute-start.4 = (bf16[256,128]{1,0:T(8,128)(2,1)S(1)}, bf16[256,128]{1,0:T(8,128)(2,1)S(1)}, u32[]{:S(2)}, u32[]{:S(2)}) collective-permute-start(bf16[256,128]{1,0:T(8,128)(2,1)S(1)} %get-tuple-element.44.refs_4_), channel_id=1, source_target_pairs={{0,8},{4,12},{8,0},{12,4},{16,24},{20,28},{24,16},{28,20},{1,9},{5... | collective-permute-start | bytes 196616 | tf_op jit(solution)/shard_map/ppermute | solution.py:79
  23.4 8.0 %collective-permute-start.9 = (bf16[256,128]{1,0:T(8,128)(2,1)S(1)}, bf16[256,128]{1,0:T(8,128)(2,1)S(1)}, u32[]{:S(2)}, u32[]{:S(2)}) collective-permute-start(bf16[256,128]{1,0:T(8,128)(2,1)S(1)} %collective-permute-done.8.refs_10_), channel_id=1, source_target_pairs={{0,4},{4,0},{8,12},{12,8},{16,20},{20,16},{24,28},{28,24},{1,5},{5... | collective-permute-start | bytes 196616 | tf_op jit(solution)/shard_map/ppermute | solution.py:79
  24.7 6.8 %collective-permute-start.7 = (bf16[256,128]{1,0:T(8,128)(2,1)S(1)}, bf16[256,128]{1,0:T(8,128)(2,1)S(1)}, u32[]{:S(2)}, u32[]{:S(2)}) collective-permute-start(bf16[256,128]{1,0:T(8,128)(2,1)S(1)} %collective-permute-done.6.refs_8_), channel_id=1, source_target_pairs={{0,4},{4,0},{8,12},{12,8},{16,20},{20,16},{24,28},{28,24},{1,5},{5... | collective-permute-start | bytes 196616 | tf_op jit(solution)/shard_map/ppermute | solution.py:79
  24.7 19.9 %collective-permute-start.13 = (bf16[512,128]{1,0:T(8,128)(2,1)}, bf16[512,128]{1,0:T(8,128)(2,1)S(1)}, u32[]{:S(2)}, u32[]{:S(2)}) collective-permute-start(bf16[512,128]{1,0:T(8,128)(2,1)} %get-tuple-element.53), channel_id=1, source_target_pairs={{0,0},{1,4},{2,8},{3,12},{4,1},{5,5},{6,9},{7,13},{8,2},{9,6},{10,... | collective-permute-start | bytes 393224 | tf_op jit(solution)/shard_map/ppermute | solution.py:90
  26.2 18.3 %collective-permute-start.14 = (bf16[512,128]{1,0:T(8,128)(2,1)}, bf16[512,128]{1,0:T(8,128)(2,1)S(1)}, u32[]{:S(2)}, u32[]{:S(2)}) collective-permute-start(bf16[512,128]{1,0:T(8,128)(2,1)} %get-tuple-element.54), channel_id=1, source_target_pairs={{0,4},{1,0},{2,12},{3,8},{4,5},{5,1},{6,13},{7,9},{8,6},{9,2},{10,... | collective-permute-start | bytes 393224 | tf_op jit(solution)/shard_map/ppermute | solution.py:90
  27.9 22.7 %collective-permute-start.15 = (bf16[512,128]{1,0:T(8,128)(2,1)}, bf16[512,128]{1,0:T(8,128)(2,1)S(1)}, u32[]{:S(2)}, u32[]{:S(2)}) collective-permute-start(bf16[512,128]{1,0:T(8,128)(2,1)} %get-tuple-element.55), channel_id=1, source_target_pairs={{0,8},{1,12},{2,0},{3,4},{4,9},{5,13},{6,1},{7,5},{8,10},{9,14},{1... | collective-permute-start | bytes 393224 | tf_op jit(solution)/shard_map/ppermute | solution.py:90
  31.4 19.3 %collective-permute-start.16 = (bf16[512,128]{1,0:T(8,128)(2,1)}, bf16[512,128]{1,0:T(8,128)(2,1)S(1)}, u32[]{:S(2)}, u32[]{:S(2)}) collective-permute-start(bf16[512,128]{1,0:T(8,128)(2,1)} %get-tuple-element.56), channel_id=1, source_target_pairs={{0,12},{1,8},{2,4},{3,0},{4,13},{5,9},{6,5},{7,1},{8,14},{9,10},{1... | collective-permute-start | bytes 393224 | tf_op jit(solution)/shard_map/ppermute | solution.py:90
  31.4 4.6 %collective-permute-start.5 = (bf16[256,128]{1,0:T(8,128)(2,1)S(1)}, bf16[256,128]{1,0:T(8,128)(2,1)S(1)}, u32[]{:S(2)}, u32[]{:S(2)}) collective-permute-start(bf16[256,128]{1,0:T(8,128)(2,1)S(1)} %collective-permute-done.4.refs_6_), channel_id=1, source_target_pairs={{0,4},{4,0},{8,12},{12,8},{16,20},{20,16},{24,28},{28,24},{1,5},{5... | collective-permute-start | bytes 196616 | tf_op jit(solution)/shard_map/ppermute | solution.py:79
  38.8 19.4 %all-to-all-start = ((bf16[8,432,128]{2,1,0:T(8,128)(2,1)}), bf16[8,432,128]{2,1,0:T(8,128)(2,1)S(1)}, u32[]{:S(2)}, u32[]{:S(2)}) async-start(bf16[8,432,128]{2,1,0:T(8,128)(2,1)} %bitcast.4), calls=%async_computation | async-start | bytes 1769472 | tf_op jit(solution)/shard_map/all_to_all | solution.py:429
  61.2 6.4 %collective-permute-start.18 = (bf16[512,128]{1,0:T(8,128)(2,1)S(1)}, bf16[512,128]{1,0:T(8,128)(2,1)S(1)}, u32[]{:S(2)}, u32[]{:S(2)}) collective-permute-start(bf16[512,128]{1,0:T(8,128)(2,1)S(1)} %get-tuple-element.59), channel_id=1, source_target_pairs={{0,8},{4,12},{8,0},{12,4},{16,24},{20,28},{24,16},{28,20},{1,9},{5... | collective-permute-start | bytes 393224 | tf_op jit(solution)/shard_map/ppermute | solution.py:79
  61.7 6.9 %collective-permute-start.19 = (bf16[512,128]{1,0:T(8,128)(2,1)S(1)}, bf16[512,128]{1,0:T(8,128)(2,1)S(1)}, u32[]{:S(2)}, u32[]{:S(2)}) collective-permute-start(bf16[512,128]{1,0:T(8,128)(2,1)S(1)} %get-tuple-element.60), channel_id=1, source_target_pairs={{0,12},{4,8},{8,4},{12,0},{16,28},{20,24},{24,20},{28,16},{1,13},{... | collective-permute-start | bytes 393224 | tf_op jit(solution)/shard_map/ppermute | solution.py:79
  70.8 6.4 %collective-permute-start.22 = (bf16[512,128]{1,0:T(8,128)(2,1)S(1)}, bf16[512,128]{1,0:T(8,128)(2,1)S(1)}, u32[]{:S(2)}, u32[]{:S(2)}) collective-permute-start(bf16[512,128]{1,0:T(8,128)(2,1)S(1)} %get-tuple-element.64), channel_id=1, source_target_pairs={{0,8},{4,12},{8,0},{12,4},{16,24},{20,28},{24,16},{28,20},{1,9},{5... | collective-permute-start | bytes 393224 | tf_op jit(solution)/shard_map/ppermute | solution.py:79
  71.3 9.1 %collective-permute-start.23 = (bf16[512,128]{1,0:T(8,128)(2,1)S(1)}, bf16[512,128]{1,0:T(8,128)(2,1)S(1)}, u32[]{:S(2)}, u32[]{:S(2)}) collective-permute-start(bf16[512,128]{1,0:T(8,128)(2,1)S(1)} %get-tuple-element.65), channel_id=1, source_target_pairs={{0,12},{4,8},{8,4},{12,0},{16,28},{20,24},{24,20},{28,16},{1,13},{... | collective-permute-start | bytes 393224 | tf_op jit(solution)/shard_map/ppermute | solution.py:79
  72.2 13.9 %collective-permute-start.29 = (bf16[512,128]{1,0:T(8,128)(2,1)S(1)}, bf16[512,128]{1,0:T(8,128)(2,1)S(1)}, u32[]{:S(2)}, u32[]{:S(2)}) collective-permute-start(bf16[512,128]{1,0:T(8,128)(2,1)S(1)} %get-tuple-element.63), channel_id=1, source_target_pairs={{0,1},{1,5},{2,9},{3,13},{4,0},{5,4},{6,8},{7,12},{8,3},{9,7},{10,... | collective-permute-start | bytes 393224 | tf_op jit(solution)/shard_map/ppermute | solution.py:87
  72.2 13.9 %collective-permute-start.30 = (bf16[512,128]{1,0:T(8,128)(2,1)S(1)}, bf16[512,128]{1,0:T(8,128)(2,1)S(1)}, u32[]{:S(2)}, u32[]{:S(2)}) collective-permute-start(bf16[512,128]{1,0:T(8,128)(2,1)S(1)} %get-tuple-element.64), channel_id=1, source_target_pairs={{0,2},{1,6},{2,10},{3,14},{4,3},{5,7},{6,11},{7,15},{8,0},{9,4},{1... | collective-permute-start | bytes 393224 | tf_op jit(solution)/shard_map/ppermute | solution.py:87
  73.3 12.9 %collective-permute-start.31 = (bf16[512,128]{1,0:T(8,128)(2,1)S(1)}, bf16[512,128]{1,0:T(8,128)(2,1)S(1)}, u32[]{:S(2)}, u32[]{:S(2)}) collective-permute-start(bf16[512,128]{1,0:T(8,128)(2,1)S(1)} %get-tuple-element.65), channel_id=1, source_target_pairs={{0,3},{1,7},{2,11},{3,15},{4,2},{5,6},{6,10},{7,14},{8,1},{9,5},{1... | collective-permute-start | bytes 393224 | tf_op jit(solution)/shard_map/ppermute | solution.py:87
  77.2 9.0 %collective-permute-start.28 = (bf16[512,128]{1,0:T(8,128)(2,1)S(1)}, bf16[512,128]{1,0:T(8,128)(2,1)S(1)}, u32[]{:S(2)}, u32[]{:S(2)}) collective-permute-start(bf16[512,128]{1,0:T(8,128)(2,1)S(1)} %get-tuple-element.62.refs_0_), channel_id=1, source_target_pairs={{0,0},{1,4},{2,8},{3,12},{4,1},{5,5},{6,9},{7,13},{8,2},{9,6},{10,... | collective-permute-start | bytes 393224 | tf_op jit(solution)/shard_map/ppermute | solution.py:87
  86.1 25.3 %all-to-all-start.1 = ((bf16[8,512,128]{2,1,0:T(8,128)(2,1)}), bf16[8,512,128]{2,1,0:T(8,128)(2,1)S(1)}, u32[]{:S(2)}, u32[]{:S(2)}) async-start(bf16[8,512,128]{2,1,0:T(8,128)(2,1)} %get-tuple-element.74), calls=%async_computation.1 | async-start | bytes 2097152 | tf_op jit(solution)/shard_map/all_to_all | solution.py:475
  91.3 7.4 %collective-permute-start.24 = (bf16[512,128]{1,0:T(8,128)(2,1)}, bf16[512,128]{1,0:T(8,128)(2,1)S(1)}, u32[]{:S(2)}, u32[]{:S(2)}) collective-permute-start(bf16[512,128]{1,0:T(8,128)(2,1)} %get-tuple-element.69), channel_id=1, source_target_pairs={{0,0},{1,4},{2,8},{3,12},{4,1},{5,5},{6,9},{7,13},{8,2},{9,6},{10,... | collective-permute-start | bytes 393224 | tf_op jit(solution)/shard_map/ppermute | solution.py:87
  92.9 5.8 %collective-permute-start.25 = (bf16[512,128]{1,0:T(8,128)(2,1)}, bf16[512,128]{1,0:T(8,128)(2,1)S(1)}, u32[]{:S(2)}, u32[]{:S(2)}) collective-permute-start(bf16[512,128]{1,0:T(8,128)(2,1)} %get-tuple-element.70), channel_id=1, source_target_pairs={{0,1},{1,5},{2,9},{3,13},{4,0},{5,4},{6,8},{7,12},{8,3},{9,7},{10,... | collective-permute-start | bytes 393224 | tf_op jit(solution)/shard_map/ppermute | solution.py:87
  95.4 16.0 %collective-permute-start.26 = (bf16[512,128]{1,0:T(8,128)(2,1)S(1)}, bf16[512,128]{1,0:T(8,128)(2,1)S(1)}, u32[]{:S(2)}, u32[]{:S(2)}) collective-permute-start(bf16[512,128]{1,0:T(8,128)(2,1)S(1)} %get-tuple-element.71), channel_id=1, source_target_pairs={{0,2},{1,6},{2,10},{3,14},{4,3},{5,7},{6,11},{7,15},{8,0},{9,4},{1... | collective-permute-start | bytes 393224 | tf_op jit(solution)/shard_map/ppermute | solution.py:87
  97.8 13.7 %collective-permute-start.27 = (bf16[512,128]{1,0:T(8,128)(2,1)S(1)}, bf16[512,128]{1,0:T(8,128)(2,1)S(1)}, u32[]{:S(2)}, u32[]{:S(2)}) collective-permute-start(bf16[512,128]{1,0:T(8,128)(2,1)S(1)} %get-tuple-element.72), channel_id=1, source_target_pairs={{0,3},{1,7},{2,11},{3,15},{4,2},{5,6},{6,10},{7,14},{8,1},{9,5},{1... | collective-permute-start | bytes 393224 | tf_op jit(solution)/shard_map/ppermute | solution.py:87
  113.2 5.8 %collective-permute-start.32 = (bf16[512,128]{1,0:T(8,128)(2,1)S(1)}, bf16[512,128]{1,0:T(8,128)(2,1)S(1)}, u32[]{:S(2)}, u32[]{:S(2)}) collective-permute-start(bf16[512,128]{1,0:T(8,128)(2,1)S(1)} %get-tuple-element.77), channel_id=1, source_target_pairs={{0,1},{1,0},{2,3},{3,2},{4,5},{5,4},{6,7},{7,6},{8,9},{9,8},{10,11... | collective-permute-start | bytes 393224 | tf_op jit(solution)/shard_map/ppermute | solution.py:76
  113.3 12.4 %collective-permute-start.33 = (bf16[512,128]{1,0:T(8,128)(2,1)S(1)}, bf16[512,128]{1,0:T(8,128)(2,1)S(1)}, u32[]{:S(2)}, u32[]{:S(2)}) collective-permute-start(bf16[512,128]{1,0:T(8,128)(2,1)S(1)} %get-tuple-element.78), channel_id=1, source_target_pairs={{0,2},{1,3},{2,0},{3,1},{4,6},{5,7},{6,4},{7,5},{8,10},{9,11},{10,... | collective-permute-start | bytes 393224 | tf_op jit(solution)/shard_map/ppermute | solution.py:76
  115.7 10.0 %collective-permute-start.34 = (bf16[512,128]{1,0:T(8,128)(2,1)S(1)}, bf16[512,128]{1,0:T(8,128)(2,1)S(1)}, u32[]{:S(2)}, u32[]{:S(2)}) collective-permute-start(bf16[512,128]{1,0:T(8,128)(2,1)S(1)} %get-tuple-element.79), channel_id=1, source_target_pairs={{0,3},{1,2},{2,1},{3,0},{4,7},{5,6},{6,5},{7,4},{8,11},{9,10},{10,... | collective-permute-start | bytes 393224 | tf_op jit(solution)/shard_map/ppermute | solution.py:76
  (16 other events, 135.8 us)

commit v6 on v5

--- a/solution.py
+++ b/solution.py
@@ -296,8 +296,8 @@
                 )
             return cols[:, 2:3] > 0.5
 
-        def pick(line, upper):
-            found = dot(onehot[line * CAP : (line + 1) * CAP, :], table[...])
+        def pick(found, line, upper):
+            found = found[line * CAP : (line + 1) * CAP, :]
             return jnp.where(upper, found[:, width:], found[:, :width]).astype(BF)
 
         lines = sent[...].astype(F32)
@@ -310,13 +310,15 @@
         for start in range(0, G, group):
             now = places[start : start + group]
             upper = [mark(src[pl.ds(at(f ^ r, s), 1), :], j) for j, (r, s) in enumerate(now)]
+            found = dot(onehot[...], table[...])
             for j, (r, s) in enumerate(now):
-                srcs[r][s * CAP : (s + 1) * CAP, :] = pick(j, upper[j])
+                srcs[r][s * CAP : (s + 1) * CAP, :] = pick(found, j, upper[j])
 
         def several(b, _):
             upper = [mark(ids[b * group + j], j) for j in range(group)]
+            found = dot(onehot[...], table[...])
             for j in range(group):
-                tgt[b * group + j, :CAP, :] = pick(j, upper[j])
+                tgt[b * group + j, :CAP, :] = pick(found, j, upper[j])
                 for k in range(M):
                     tgt[b * group + j, CAP + k * share : CAP + (k + 1) * share, :] = ride[k]
             return 0

time: 128 us -> 128 us (level)
  no operation moved by 1% of the time
where the time goes in v6:
time: 128 us; the launch traced here: 127 us
  starting transfers between devices  53.5 us (42%)
  waiting for transfers between devices  46.5 us (36%)
  Pallas kernels  24.6 us (19%)
  local copies, waits for them, and re-layouts  1.57 us (1%)
    pallas_call x12, Pallas kernels, call(): pl.pallas_call(kernel, out_shape=list(out_shapes), grid_spec=pltpu.Prefet...  24.6 us
    ppermute x9, starting transfers between devices, over_mp(): return lax.ppermute(x, 'mp', [(i, i ^ k) for i in range(M)])  16.5 us
    ppermute x8, waiting for transfers between devices, home(): lax.ppermute(x, both, [(at(i, s) * M + z, at(z, s) * M + (i ^ r)) for s,...  12.8 us
    ppermute x14, waiting for transfers between devices, over_plane(): return lax.ppermute(x, 'graph', [(i, i ^ k) for i in range(G)])  11 us
    ppermute x8, starting transfers between devices, home(): lax.ppermute(x, both, [(at(i, s) * M + z, at(z, s) * M + (i ^ r)) for s,...  10.6 us
    ppermute x9, waiting for transfers between devices, over_mp(): return lax.ppermute(x, 'mp', [(i, i ^ k) for i in range(M)])  9.56 us
    ppermute x14, starting transfers between devices, over_plane(): return lax.ppermute(x, 'graph', [(i, i ^ k) for i in range(G)])  9.26 us
    all_to_all x1, waiting for transfers between devices, local(): lax.all_to_all(outgoing.reshape(G, CAP + id_rows + M // 2 * share, width)...  6.97 us
  transfers between devices with their start and end apart: 37, of which 11 were waited for; matrix products, arithmetic and copies ran while one was open for 0% of the time, Pallas kernels for 12%

profile of v6, /device:TPU:0, one launch (start us, length us, event | category | flops | bytes accessed | tf_op | source)
XLA Modules:
  0.0 127.1 jit_solution(2149785853449123361)
XLA Ops:
  0.6 2.4 %shard_map.149 = (bf16[512,128]{1,0:T(8,128)(2,1)}, bf16[512,128]{1,0:T(8,128)(2,1)}, bf16[512,128]{1,0:T(8,128)(2,1)}, bf16[512,128]{1,0:T(8,128)(2,1)}, bf16[2...) custom-call(s32[1]{0:T(128)} %constant.12.clone.1.info, ...), custom_call_target="tpu_custom_call" | custom-call | tf_op jit(solution)/shard_map/pallas_call | solution.py:41
  3.1 5.1 %collective-permute-start.2 = (bf16[256,128]{1,0:T(8,128)(2,1)}, bf16[256,128]{1,0:T(8,128)(2,1)S(1)}, u32[]{:S(2)}, u32[]{:S(2)}) collective-permute-start(bf16[256,128]{1,0:T(8,128)(2,1)} %get-tuple-element.43.refs_0_), channel_id=1, source_target_pairs={{0,3},{1,2},{2,1},{3,0},{4,7},{5,6},{6,5},{7,4},{8,11},{9,10},{10,... | collective-permute-start | bytes 196616 | tf_op jit(solution)/shard_map/ppermute | solution.py:76
  8.8 1.4 %collective-permute-start.10 = (bf16[512,128]{1,0:T(8,128)(2,1)}, bf16[512,128]{1,0:T(8,128)(2,1)S(1)}, u32[]{:S(2)}, u32[]{:S(2)}) collective-permute-start(bf16[512,128]{1,0:T(8,128)(2,1)} %get-tuple-element.47), channel_id=1, source_target_pairs={{0,1},{1,0},{2,3},{3,2},{4,5},{5,4},{6,7},{7,6},{8,9},{9,8},{10,11... | collective-permute-start | bytes 393224 | tf_op jit(solution)/shard_map/ppermute | solution.py:76
  10.2 2.9 %collective-permute-start.11 = (bf16[512,128]{1,0:T(8,128)(2,1)}, bf16[512,128]{1,0:T(8,128)(2,1)S(1)}, u32[]{:S(2)}, u32[]{:S(2)}) collective-permute-start(bf16[512,128]{1,0:T(8,128)(2,1)} %get-tuple-element.48), channel_id=1, source_target_pairs={{0,2},{1,3},{2,0},{3,1},{4,6},{5,7},{6,4},{7,5},{8,10},{9,11},{10,... | collective-permute-start | bytes 393224 | tf_op jit(solution)/shard_map/ppermute | solution.py:76
  13.2 2.0 %collective-permute-start.12 = (bf16[512,128]{1,0:T(8,128)(2,1)}, bf16[512,128]{1,0:T(8,128)(2,1)S(1)}, u32[]{:S(2)}, u32[]{:S(2)}) collective-permute-start(bf16[512,128]{1,0:T(8,128)(2,1)} %get-tuple-element.49), channel_id=1, source_target_pairs={{0,3},{1,2},{2,1},{3,0},{4,7},{5,6},{6,5},{7,4},{8,11},{9,10},{10,... | collective-permute-start | bytes 393224 | tf_op jit(solution)/shard_map/ppermute | solution.py:76
  17.6 2.8 %collective-permute-start.8 = (bf16[256,128]{1,0:T(8,128)(2,1)S(1)}, bf16[256,128]{1,0:T(8,128)(2,1)S(1)}, u32[]{:S(2)}, u32[]{:S(2)}) collective-permute-start(bf16[256,128]{1,0:T(8,128)(2,1)S(1)} %get-tuple-element.44.refs_4_), channel_id=1, source_target_pairs={{0,24},{4,28},{8,16},{12,20},{16,8},{20,12},{24,0},{28,4},{1,25},{... | collective-permute-start | bytes 196616 | tf_op jit(solution)/shard_map/ppermute | solution.py:79
  21.4 2.0 %collective-permute-done.11.refs_2_ = bf16[512,128]{1,0:T(8,128)(2,1)S(1)} collective-permute-done((bf16[512,128]{1,0:T(8,128)(2,1)}, bf16[512,128]{1,0:T(8,128)(2,1)S(1)}, u32[]{:S(2)}, u32[]{:S(2)}) %collective-permute-start.11) | collective-permute-done | bytes 131104 | tf_op jit(solution)/shard_map/ppermute | solution.py:76
  24.7 1.6 %collective-permute-start.13 = (bf16[512,128]{1,0:T(8,128)(2,1)}, bf16[512,128]{1,0:T(8,128)(2,1)S(1)}, u32[]{:S(2)}, u32[]{:S(2)}) collective-permute-start(bf16[512,128]{1,0:T(8,128)(2,1)} %get-tuple-element.53), channel_id=1, source_target_pairs={{0,0},{1,4},{2,8},{3,12},{4,1},{5,5},{6,9},{7,13},{8,2},{9,6},{10,... | collective-permute-start | bytes 393224 | tf_op jit(solution)/shard_map/ppermute | solution.py:90
  26.2 1.7 %collective-permute-start.14 = (bf16[512,128]{1,0:T(8,128)(2,1)}, bf16[512,128]{1,0:T(8,128)(2,1)S(1)}, u32[]{:S(2)}, u32[]{:S(2)}) collective-permute-start(bf16[512,128]{1,0:T(8,128)(2,1)} %get-tuple-element.54), channel_id=1, source_target_pairs={{0,4},{1,0},{2,12},{3,8},{4,5},{5,1},{6,13},{7,9},{8,6},{9,2},{10,... | collective-permute-start | bytes 393224 | tf_op jit(solution)/shard_map/ppermute | solution.py:90
  27.9 3.5 %collective-permute-start.15 = (bf16[512,128]{1,0:T(8,128)(2,1)}, bf16[512,128]{1,0:T(8,128)(2,1)S(1)}, u32[]{:S(2)}, u32[]{:S(2)}) collective-permute-start(bf16[512,128]{1,0:T(8,128)(2,1)} %get-tuple-element.55), channel_id=1, source_target_pairs={{0,8},{1,12},{2,0},{3,4},{4,9},{5,13},{6,1},{7,5},{8,10},{9,14},{1... | collective-permute-start | bytes 393224 | tf_op jit(solution)/shard_map/ppermute | solution.py:90
  32.9 3.1 %shard_map.151 = (bf16[512,512]{1,0:T(8,128)(2,1)S(1)}, bf16[512,64]{1,0:T(8,128)(2,1)S(1)}) custom-call(s32[3]{0:T(128)S(1)} %pad_add_fusion.info, bf16[512,128]{1,0:T(8,128)(2,1)S(1)} %copy-done.2, bf16[512,128]{1,0:T(8,128)(2,1)S(1)} %collective-permute-done.10.refs_1_, bf16[512,128]{1,0:T(8,128)(2,1)S(1)} %collective-permute-done.11.refs_2_, ...), custom_call_target="tpu_custom_call" | custom-call | tf_op jit(solution)/shard_map/pallas_call | solution.py:41
  36.0 2.8 %shard_map.152 = (f32[512,512]{1,0:T(8,128)S(1)}, bf16[2,4,432,128]{3,2,1,0:T(8,128)(2,1)}) custom-call(s32[3]{0:T(128)S(1)} %pad_add_fusion.info, bf16[256,128]{1,0:T(8,128)(2,1)S(1)} %copy-done.7, bf16[256,128]{1,0:T(8,128)(2,1)S(1)} %collective-permute-done.refs_1_, bf16[256,128]{1,0:T(8,128)(2,1)S(1)} %collective-permute-done.1.refs_2_, ...), custom_call_target="tpu_custom_call" | custom-call | tf_op jit(solution)/shard_map/pallas_call | solution.py:41
  38.8 5.7 %all-to-all-start = ((bf16[8,432,128]{2,1,0:T(8,128)(2,1)}), bf16[8,432,128]{2,1,0:T(8,128)(2,1)S(1)}, u32[]{:S(2)}, u32[]{:S(2)}) async-start(bf16[8,432,128]{2,1,0:T(8,128)(2,1)} %bitcast.4), calls=%async_computation | async-start | bytes 1769472 | tf_op jit(solution)/shard_map/all_to_all | solution.py:431
  44.6 6.1 %collective-permute-done.15.refs_2_.refs_6_ = bf16[512,128]{1,0:T(8,128)(2,1)S(1)} collective-permute-done((bf16[512,128]{1,0:T(8,128)(2,1)}, bf16[512,128]{1,0:T(8,128)(2,1)S(1)}, u32[]{:S(2)}, u32[]{:S(2)}) %collective-permute-start.15) | collective-permute-done | bytes 131104 | tf_op jit(solution)/shard_map/ppermute | solution.py:90
  51.2 7.0 %all-to-all-done.incoming = bf16[8,432,128]{2,1,0:T(8,128)(2,1)S(1)} async-done(((bf16[8,432,128]{2,1,0:T(8,128)(2,1)}), bf16[8,432,128]{2,1,0:T(8,128)(2,1)S(1)}, u32[]{:S(2)}, u32[]{:S(2)}) %all-to-all-start) | async-done | bytes 884768 | tf_op jit(solution)/shard_map/all_to_all | solution.py:431
  58.2 2.4 %shard_map.154 = (bf16[512,128]{1,0:T(8,128)(2,1)S(1)}, bf16[512,128]{1,0:T(8,128)(2,1)S(1)}, bf16[512,128]{1,0:T(8,128)(2,1)S(1)}, bf16[512,128]{1,0:T(8,128)(2...) custom-call(s32[3]{0:T(128)S(1)} %pad_add_fusion.info, ...), custom_call_target="tpu_custom_call" | custom-call | flops 3000000000 | tf_op jit(solution)/shard_map/pallas_call | solution.py:41
  63.3 4.3 %collective-permute-done.18.refs_2_ = bf16[512,128]{1,0:T(8,128)(2,1)S(1)} collective-permute-done((bf16[512,128]{1,0:T(8,128)(2,1)S(1)}, bf16[512,128]{1,0:T(8,128)(2,1)S(1)}, u32[]{:S(2)}, u32[]{:S(2)}) %collective-permute-start.18) | collective-permute-done | bytes 131104 | tf_op jit(solution)/shard_map/ppermute | solution.py:79
  68.6 1.4 %shard_map.156 = (bf16[512,128]{1,0:T(8,128)(2,1)S(1)}, bf16[512,128]{1,0:T(8,128)(2,1)S(1)}, bf16[512,128]{1,0:T(8,128)(2,1)S(1)}, bf16[512,128]{1,0:T(8,128)(2,1)S(1)}) custom-call(s32[3]{0:T(128)S(1)} %pad_add_fusion.info, bf16[512,128]{1,0:T(8,128)(2,1)S(1)} %get-tuple-element.57.refs_0_, bf16[512,128]{1,0:T(8,128)(2,1)S(1)} %collective-permute-done.17.refs_1_, ...), custom_call_target="tpu_custom_call" | custom-call | flops 1500000000 | tf_op jit(solution)/shard_map/pallas_call | solution.py:41
  73.3 1.6 %collective-permute-start.31 = (bf16[512,128]{1,0:T(8,128)(2,1)S(1)}, bf16[512,128]{1,0:T(8,128)(2,1)S(1)}, u32[]{:S(2)}, u32[]{:S(2)}) collective-permute-start(bf16[512,128]{1,0:T(8,128)(2,1)S(1)} %get-tuple-element.65), channel_id=1, source_target_pairs={{0,3},{1,7},{2,11},{3,15},{4,2},{5,6},{6,10},{7,14},{8,1},{9,5},{1... | collective-permute-start | bytes 393224 | tf_op jit(solution)/shard_map/ppermute | solution.py:87
  74.9 2.3 %collective-permute-done.22.refs_2_ = bf16[512,128]{1,0:T(8,128)(2,1)S(1)} collective-permute-done((bf16[512,128]{1,0:T(8,128)(2,1)S(1)}, bf16[512,128]{1,0:T(8,128)(2,1)S(1)}, u32[]{:S(2)}, u32[]{:S(2)}) %collective-permute-start.22) | collective-permute-done | bytes 131104 | tf_op jit(solution)/shard_map/ppermute | solution.py:79
  77.8 2.6 %collective-permute-done.23.refs_3_ = bf16[512,128]{1,0:T(8,128)(2,1)S(1)} collective-permute-done((bf16[512,128]{1,0:T(8,128)(2,1)S(1)}, bf16[512,128]{1,0:T(8,128)(2,1)S(1)}, u32[]{:S(2)}, u32[]{:S(2)}) %collective-permute-start.23) | collective-permute-done | bytes 131104 | tf_op jit(solution)/shard_map/ppermute | solution.py:79
  80.5 6.2 %shard_map.157 = (bf16[512,128]{1,0:T(8,128)(2,1)}, bf16[512,128]{1,0:T(8,128)(2,1)}, bf16[512,128]{1,0:T(8,128)(2,1)S(1)}, bf16[512,128]{1,0:T(8,128)(2,1)S(1)}, bf16[8,512,128]{2,1,0:T(8,128)(2,1)}) custom-call(s32[3]{0:T(128)S(1)} %pad_add_fusion.info, bf16[512,128]{1,0:T(8,128)(2,1)S(1)} %get-tuple-element.62.refs_0_, ...), custom_call_target="tpu_custom_call" | custom-call | flops 6000000000 | tf_op jit(solution)/shard_map/pallas_call | solution.py:41
  86.6 4.7 %all-to-all-start.1 = ((bf16[8,512,128]{2,1,0:T(8,128)(2,1)}), bf16[8,512,128]{2,1,0:T(8,128)(2,1)S(1)}, u32[]{:S(2)}, u32[]{:S(2)}) async-start(bf16[8,512,128]{2,1,0:T(8,128)(2,1)} %get-tuple-element.74), calls=%async_computation.1 | async-start | bytes 2097152 | tf_op jit(solution)/shard_map/all_to_all | solution.py:477
  91.4 1.6 %collective-permute-start.24 = (bf16[512,128]{1,0:T(8,128)(2,1)}, bf16[512,128]{1,0:T(8,128)(2,1)S(1)}, u32[]{:S(2)}, u32[]{:S(2)}) collective-permute-start(bf16[512,128]{1,0:T(8,128)(2,1)} %get-tuple-element.69), channel_id=1, source_target_pairs={{0,0},{1,4},{2,8},{3,12},{4,1},{5,5},{6,9},{7,13},{8,2},{9,6},{10,... | collective-permute-start | bytes 393224 | tf_op jit(solution)/shard_map/ppermute | solution.py:87
  92.9 2.7 %collective-permute-start.25 = (bf16[512,128]{1,0:T(8,128)(2,1)}, bf16[512,128]{1,0:T(8,128)(2,1)S(1)}, u32[]{:S(2)}, u32[]{:S(2)}) collective-permute-start(bf16[512,128]{1,0:T(8,128)(2,1)} %get-tuple-element.70), channel_id=1, source_target_pairs={{0,1},{1,5},{2,9},{3,13},{4,0},{5,4},{6,8},{7,12},{8,3},{9,7},{10,... | collective-permute-start | bytes 393224 | tf_op jit(solution)/shard_map/ppermute | solution.py:87
  95.6 2.3 %collective-permute-start.26 = (bf16[512,128]{1,0:T(8,128)(2,1)S(1)}, bf16[512,128]{1,0:T(8,128)(2,1)S(1)}, u32[]{:S(2)}, u32[]{:S(2)}) collective-permute-start(bf16[512,128]{1,0:T(8,128)(2,1)S(1)} %get-tuple-element.71), channel_id=1, source_target_pairs={{0,2},{1,6},{2,10},{3,14},{4,3},{5,7},{6,11},{7,15},{8,0},{9,4},{1... | collective-permute-start | bytes 393224 | tf_op jit(solution)/shard_map/ppermute | solution.py:87
  98.7 12.8 %collective-permute-done.26.refs_2_ = bf16[512,128]{1,0:T(8,128)(2,1)S(1)} collective-permute-done((bf16[512,128]{1,0:T(8,128)(2,1)S(1)}, bf16[512,128]{1,0:T(8,128)(2,1)S(1)}, u32[]{:S(2)}, u32[]{:S(2)}) %collective-permute-start.26) | collective-permute-done | bytes 131104 | tf_op jit(solution)/shard_map/ppermute | solution.py:87
  111.5 1.8 %shard_map.158 = (bf16[512,128]{1,0:T(8,128)(2,1)S(1)}, bf16[512,128]{1,0:T(8,128)(2,1)S(1)}, bf16[512,128]{1,0:T(8,128)(2,1)S(1)}, bf16[512,128]{1,0:T(8,128)(2,1)S(1)}) custom-call(s32[3]{0:T(128)S(1)} %pad_add_fusion.info, bf16[512,128]{1,0:T(8,128)(2,1)S(1)} %collective-permute-done.24.refs_0_, bf16[512,128]{1,0:T(8,128)(2,1)S(1)} %collective-permute-done.25.refs_1_, ...), custom_call_target="tpu_custom_call" | custom-call | tf_op jit(solution)/shard_map/pallas_call | solution.py:41
  113.4 2.4 %collective-permute-start.33 = (bf16[512,128]{1,0:T(8,128)(2,1)S(1)}, bf16[512,128]{1,0:T(8,128)(2,1)S(1)}, u32[]{:S(2)}, u32[]{:S(2)}) collective-permute-start(bf16[512,128]{1,0:T(8,128)(2,1)S(1)} %get-tuple-element.78), channel_id=1, source_target_pairs={{0,2},{1,3},{2,0},{3,1},{4,6},{5,7},{6,4},{7,5},{8,10},{9,11},{10,... | collective-permute-start | bytes 393224 | tf_op jit(solution)/shard_map/ppermute | solution.py:76
  115.7 2.0 %collective-permute-start.34 = (bf16[512,128]{1,0:T(8,128)(2,1)S(1)}, bf16[512,128]{1,0:T(8,128)(2,1)S(1)}, u32[]{:S(2)}, u32[]{:S(2)}) collective-permute-start(bf16[512,128]{1,0:T(8,128)(2,1)S(1)} %get-tuple-element.79), channel_id=1, source_target_pairs={{0,3},{1,2},{2,1},{3,0},{4,7},{5,6},{6,5},{7,4},{8,11},{9,10},{10,... | collective-permute-start | bytes 393224 | tf_op jit(solution)/shard_map/ppermute | solution.py:76
  119.1 6.6 %collective-permute-done.33.refs_2_ = bf16[512,128]{1,0:T(8,128)(2,1)S(1)} collective-permute-done((bf16[512,128]{1,0:T(8,128)(2,1)S(1)}, bf16[512,128]{1,0:T(8,128)(2,1)S(1)}, u32[]{:S(2)}, u32[]{:S(2)}) %collective-permute-start.33) | collective-permute-done | bytes 131104 | tf_op jit(solution)/shard_map/ppermute | solution.py:76
  125.8 1.4 %shard_map.159 = bf16[2048,128]{1,0:T(8,128)(2,1)} custom-call(s32[3]{0:T(128)S(1)} %pad_add_fusion.info, bf16[512,128]{1,0:T(8,128)(2,1)S(1)} %get-tuple-element.76.refs_0_, bf16[512,128]{1,0:T(8,128)(2,1)S(1)} %collective-permute-done.32.refs_1_, bf16[512,128]{1,0:T(8,128)(2,1)S(1)} %collective-permute-done.33.refs_2_, ...), custom_call_target="tpu_custom_call" | custom-call | flops 1000000000 | tf_op jit(solution)/shard_map/pallas_call | solution.py:41
  (80 shorter events, 17.1 us)
Async XLA Ops:
  3.1 10.1 %collective-permute-start.2 = (bf16[256,128]{1,0:T(8,128)(2,1)}, bf16[256,128]{1,0:T(8,128)(2,1)S(1)}, u32[]{:S(2)}, u32[]{:S(2)}) collective-permute-start(bf16[256,128]{1,0:T(8,128)(2,1)} %get-tuple-element.43.refs_0_), channel_id=1, source_target_pairs={{0,3},{1,2},{2,1},{3,0},{4,7},{5,6},{6,5},{7,4},{8,11},{9,10},{10,... | collective-permute-start | bytes 196616 | tf_op jit(solution)/shard_map/ppermute | solution.py:76
  8.2 7.0 %collective-permute-start.1 = (bf16[256,128]{1,0:T(8,128)(2,1)}, bf16[256,128]{1,0:T(8,128)(2,1)S(1)}, u32[]{:S(2)}, u32[]{:S(2)}) collective-permute-start(bf16[256,128]{1,0:T(8,128)(2,1)} %get-tuple-element.43.refs_0_), channel_id=1, source_target_pairs={{0,2},{1,3},{2,0},{3,1},{4,6},{5,7},{6,4},{7,5},{8,10},{9,11},{10,... | collective-permute-start | bytes 196616 | tf_op jit(solution)/shard_map/ppermute | solution.py:76
  8.2 7.9 %collective-permute-start = (bf16[256,128]{1,0:T(8,128)(2,1)}, bf16[256,128]{1,0:T(8,128)(2,1)S(1)}, u32[]{:S(2)}, u32[]{:S(2)}) collective-permute-start(bf16[256,128]{1,0:T(8,128)(2,1)} %get-tuple-element.43.refs_0_), channel_id=1, source_target_pairs={{0,1},{1,0},{2,3},{3,2},{4,5},{5,4},{6,7},{7,6},{8,9},{9,8},{10,11... | collective-permute-start | bytes 196616 | tf_op jit(solution)/shard_map/ppermute | solution.py:76
  8.8 12.1 %collective-permute-start.10 = (bf16[512,128]{1,0:T(8,128)(2,1)}, bf16[512,128]{1,0:T(8,128)(2,1)S(1)}, u32[]{:S(2)}, u32[]{:S(2)}) collective-permute-start(bf16[512,128]{1,0:T(8,128)(2,1)} %get-tuple-element.47), channel_id=1, source_target_pairs={{0,1},{1,0},{2,3},{3,2},{4,5},{5,4},{6,7},{7,6},{8,9},{9,8},{10,11... | collective-permute-start | bytes 393224 | tf_op jit(solution)/shard_map/ppermute | solution.py:76
  10.2 13.2 %collective-permute-start.11 = (bf16[512,128]{1,0:T(8,128)(2,1)}, bf16[512,128]{1,0:T(8,128)(2,1)S(1)}, u32[]{:S(2)}, u32[]{:S(2)}) collective-permute-start(bf16[512,128]{1,0:T(8,128)(2,1)} %get-tuple-element.48), channel_id=1, source_target_pairs={{0,2},{1,3},{2,0},{3,1},{4,6},{5,7},{6,4},{7,5},{8,10},{9,11},{10,... | collective-permute-start | bytes 393224 | tf_op jit(solution)/shard_map/ppermute | solution.py:76
  13.2 11.4 %collective-permute-start.12 = (bf16[512,128]{1,0:T(8,128)(2,1)}, bf16[512,128]{1,0:T(8,128)(2,1)S(1)}, u32[]{:S(2)}, u32[]{:S(2)}) collective-permute-start(bf16[512,128]{1,0:T(8,128)(2,1)} %get-tuple-element.49), channel_id=1, source_target_pairs={{0,3},{1,2},{2,1},{3,0},{4,7},{5,6},{6,5},{7,4},{8,11},{9,10},{10,... | collective-permute-start | bytes 393224 | tf_op jit(solution)/shard_map/ppermute | solution.py:76
  17.6 5.8 %collective-permute-start.8 = (bf16[256,128]{1,0:T(8,128)(2,1)S(1)}, bf16[256,128]{1,0:T(8,128)(2,1)S(1)}, u32[]{:S(2)}, u32[]{:S(2)}) collective-permute-start(bf16[256,128]{1,0:T(8,128)(2,1)S(1)} %get-tuple-element.44.refs_4_), channel_id=1, source_target_pairs={{0,24},{4,28},{8,16},{12,20},{16,8},{20,12},{24,0},{28,4},{1,25},{... | collective-permute-start | bytes 196616 | tf_op jit(solution)/shard_map/ppermute | solution.py:79
  20.9 5.3 %collective-permute-start.4 = (bf16[256,128]{1,0:T(8,128)(2,1)S(1)}, bf16[256,128]{1,0:T(8,128)(2,1)S(1)}, u32[]{:S(2)}, u32[]{:S(2)}) collective-permute-start(bf16[256,128]{1,0:T(8,128)(2,1)S(1)} %get-tuple-element.44.refs_4_), channel_id=1, source_target_pairs={{0,8},{4,12},{8,0},{12,4},{16,24},{20,28},{24,16},{28,20},{1,9},{5... | collective-permute-start | bytes 196616 | tf_op jit(solution)/shard_map/ppermute | solution.py:79
  23.4 8.0 %collective-permute-start.9 = (bf16[256,128]{1,0:T(8,128)(2,1)S(1)}, bf16[256,128]{1,0:T(8,128)(2,1)S(1)}, u32[]{:S(2)}, u32[]{:S(2)}) collective-permute-start(bf16[256,128]{1,0:T(8,128)(2,1)S(1)} %collective-permute-done.8.refs_10_), channel_id=1, source_target_pairs={{0,4},{4,0},{8,12},{12,8},{16,20},{20,16},{24,28},{28,24},{1,5},{5... | collective-permute-start | bytes 196616 | tf_op jit(solution)/shard_map/ppermute | solution.py:79
  24.7 6.8 %collective-permute-start.7 = (bf16[256,128]{1,0:T(8,128)(2,1)S(1)}, bf16[256,128]{1,0:T(8,128)(2,1)S(1)}, u32[]{:S(2)}, u32[]{:S(2)}) collective-permute-start(bf16[256,128]{1,0:T(8,128)(2,1)S(1)} %collective-permute-done.6.refs_8_), channel_id=1, source_target_pairs={{0,4},{4,0},{8,12},{12,8},{16,20},{20,16},{24,28},{28,24},{1,5},{5... | collective-permute-start | bytes 196616 | tf_op jit(solution)/shard_map/ppermute | solution.py:79
  24.7 19.9 %collective-permute-start.13 = (bf16[512,128]{1,0:T(8,128)(2,1)}, bf16[512,128]{1,0:T(8,128)(2,1)S(1)}, u32[]{:S(2)}, u32[]{:S(2)}) collective-permute-start(bf16[512,128]{1,0:T(8,128)(2,1)} %get-tuple-element.53), channel_id=1, source_target_pairs={{0,0},{1,4},{2,8},{3,12},{4,1},{5,5},{6,9},{7,13},{8,2},{9,6},{10,... | collective-permute-start | bytes 393224 | tf_op jit(solution)/shard_map/ppermute | solution.py:90
  26.2 18.3 %collective-permute-start.14 = (bf16[512,128]{1,0:T(8,128)(2,1)}, bf16[512,128]{1,0:T(8,128)(2,1)S(1)}, u32[]{:S(2)}, u32[]{:S(2)}) collective-permute-start(bf16[512,128]{1,0:T(8,128)(2,1)} %get-tuple-element.54), channel_id=1, source_target_pairs={{0,4},{1,0},{2,12},{3,8},{4,5},{5,1},{6,13},{7,9},{8,6},{9,2},{10,... | collective-permute-start | bytes 393224 | tf_op jit(solution)/shard_map/ppermute | solution.py:90
  27.9 22.7 %collective-permute-start.15 = (bf16[512,128]{1,0:T(8,128)(2,1)}, bf16[512,128]{1,0:T(8,128)(2,1)S(1)}, u32[]{:S(2)}, u32[]{:S(2)}) collective-permute-start(bf16[512,128]{1,0:T(8,128)(2,1)} %get-tuple-element.55), channel_id=1, source_target_pairs={{0,8},{1,12},{2,0},{3,4},{4,9},{5,13},{6,1},{7,5},{8,10},{9,14},{1... | collective-permute-start | bytes 393224 | tf_op jit(solution)/shard_map/ppermute | solution.py:90
  31.4 19.3 %collective-permute-start.16 = (bf16[512,128]{1,0:T(8,128)(2,1)}, bf16[512,128]{1,0:T(8,128)(2,1)S(1)}, u32[]{:S(2)}, u32[]{:S(2)}) collective-permute-start(bf16[512,128]{1,0:T(8,128)(2,1)} %get-tuple-element.56), channel_id=1, source_target_pairs={{0,12},{1,8},{2,4},{3,0},{4,13},{5,9},{6,5},{7,1},{8,14},{9,10},{1... | collective-permute-start | bytes 393224 | tf_op jit(solution)/shard_map/ppermute | solution.py:90
  31.4 4.6 %collective-permute-start.5 = (bf16[256,128]{1,0:T(8,128)(2,1)S(1)}, bf16[256,128]{1,0:T(8,128)(2,1)S(1)}, u32[]{:S(2)}, u32[]{:S(2)}) collective-permute-start(bf16[256,128]{1,0:T(8,128)(2,1)S(1)} %collective-permute-done.4.refs_6_), channel_id=1, source_target_pairs={{0,4},{4,0},{8,12},{12,8},{16,20},{20,16},{24,28},{28,24},{1,5},{5... | collective-permute-start | bytes 196616 | tf_op jit(solution)/shard_map/ppermute | solution.py:79
  38.8 19.4 %all-to-all-start = ((bf16[8,432,128]{2,1,0:T(8,128)(2,1)}), bf16[8,432,128]{2,1,0:T(8,128)(2,1)S(1)}, u32[]{:S(2)}, u32[]{:S(2)}) async-start(bf16[8,432,128]{2,1,0:T(8,128)(2,1)} %bitcast.4), calls=%async_computation | async-start | bytes 1769472 | tf_op jit(solution)/shard_map/all_to_all | solution.py:431
  61.2 6.4 %collective-permute-start.18 = (bf16[512,128]{1,0:T(8,128)(2,1)S(1)}, bf16[512,128]{1,0:T(8,128)(2,1)S(1)}, u32[]{:S(2)}, u32[]{:S(2)}) collective-permute-start(bf16[512,128]{1,0:T(8,128)(2,1)S(1)} %get-tuple-element.59), channel_id=1, source_target_pairs={{0,8},{4,12},{8,0},{12,4},{16,24},{20,28},{24,16},{28,20},{1,9},{5... | collective-permute-start | bytes 393224 | tf_op jit(solution)/shard_map/ppermute | solution.py:79
  61.7 6.9 %collective-permute-start.19 = (bf16[512,128]{1,0:T(8,128)(2,1)S(1)}, bf16[512,128]{1,0:T(8,128)(2,1)S(1)}, u32[]{:S(2)}, u32[]{:S(2)}) collective-permute-start(bf16[512,128]{1,0:T(8,128)(2,1)S(1)} %get-tuple-element.60), channel_id=1, source_target_pairs={{0,12},{4,8},{8,4},{12,0},{16,28},{20,24},{24,20},{28,16},{1,13},{... | collective-permute-start | bytes 393224 | tf_op jit(solution)/shard_map/ppermute | solution.py:79
  70.8 6.4 %collective-permute-start.22 = (bf16[512,128]{1,0:T(8,128)(2,1)S(1)}, bf16[512,128]{1,0:T(8,128)(2,1)S(1)}, u32[]{:S(2)}, u32[]{:S(2)}) collective-permute-start(bf16[512,128]{1,0:T(8,128)(2,1)S(1)} %get-tuple-element.64), channel_id=1, source_target_pairs={{0,8},{4,12},{8,0},{12,4},{16,24},{20,28},{24,16},{28,20},{1,9},{5... | collective-permute-start | bytes 393224 | tf_op jit(solution)/shard_map/ppermute | solution.py:79
  71.3 9.1 %collective-permute-start.23 = (bf16[512,128]{1,0:T(8,128)(2,1)S(1)}, bf16[512,128]{1,0:T(8,128)(2,1)S(1)}, u32[]{:S(2)}, u32[]{:S(2)}) collective-permute-start(bf16[512,128]{1,0:T(8,128)(2,1)S(1)} %get-tuple-element.65), channel_id=1, source_target_pairs={{0,12},{4,8},{8,4},{12,0},{16,28},{20,24},{24,20},{28,16},{1,13},{... | collective-permute-start | bytes 393224 | tf_op jit(solution)/shard_map/ppermute | solution.py:79
  72.2 14.4 %collective-permute-start.29 = (bf16[512,128]{1,0:T(8,128)(2,1)S(1)}, bf16[512,128]{1,0:T(8,128)(2,1)S(1)}, u32[]{:S(2)}, u32[]{:S(2)}) collective-permute-start(bf16[512,128]{1,0:T(8,128)(2,1)S(1)} %get-tuple-element.63), channel_id=1, source_target_pairs={{0,1},{1,5},{2,9},{3,13},{4,0},{5,4},{6,8},{7,12},{8,3},{9,7},{10,... | collective-permute-start | bytes 393224 | tf_op jit(solution)/shard_map/ppermute | solution.py:87
  72.2 14.4 %collective-permute-start.30 = (bf16[512,128]{1,0:T(8,128)(2,1)S(1)}, bf16[512,128]{1,0:T(8,128)(2,1)S(1)}, u32[]{:S(2)}, u32[]{:S(2)}) collective-permute-start(bf16[512,128]{1,0:T(8,128)(2,1)S(1)} %get-tuple-element.64), channel_id=1, source_target_pairs={{0,2},{1,6},{2,10},{3,14},{4,3},{5,7},{6,11},{7,15},{8,0},{9,4},{1... | collective-permute-start | bytes 393224 | tf_op jit(solution)/shard_map/ppermute | solution.py:87
  73.3 13.4 %collective-permute-start.31 = (bf16[512,128]{1,0:T(8,128)(2,1)S(1)}, bf16[512,128]{1,0:T(8,128)(2,1)S(1)}, u32[]{:S(2)}, u32[]{:S(2)}) collective-permute-start(bf16[512,128]{1,0:T(8,128)(2,1)S(1)} %get-tuple-element.65), channel_id=1, source_target_pairs={{0,3},{1,7},{2,11},{3,15},{4,2},{5,6},{6,10},{7,14},{8,1},{9,5},{1... | collective-permute-start | bytes 393224 | tf_op jit(solution)/shard_map/ppermute | solution.py:87
  77.2 9.5 %collective-permute-start.28 = (bf16[512,128]{1,0:T(8,128)(2,1)S(1)}, bf16[512,128]{1,0:T(8,128)(2,1)S(1)}, u32[]{:S(2)}, u32[]{:S(2)}) collective-permute-start(bf16[512,128]{1,0:T(8,128)(2,1)S(1)} %get-tuple-element.62.refs_0_), channel_id=1, source_target_pairs={{0,0},{1,4},{2,8},{3,12},{4,1},{5,5},{6,9},{7,13},{8,2},{9,6},{10,... | collective-permute-start | bytes 393224 | tf_op jit(solution)/shard_map/ppermute | solution.py:87
  86.6 24.8 %all-to-all-start.1 = ((bf16[8,512,128]{2,1,0:T(8,128)(2,1)}), bf16[8,512,128]{2,1,0:T(8,128)(2,1)S(1)}, u32[]{:S(2)}, u32[]{:S(2)}) async-start(bf16[8,512,128]{2,1,0:T(8,128)(2,1)} %get-tuple-element.74), calls=%async_computation.1 | async-start | bytes 2097152 | tf_op jit(solution)/shard_map/all_to_all | solution.py:477
  91.4 7.3 %collective-permute-start.24 = (bf16[512,128]{1,0:T(8,128)(2,1)}, bf16[512,128]{1,0:T(8,128)(2,1)S(1)}, u32[]{:S(2)}, u32[]{:S(2)}) collective-permute-start(bf16[512,128]{1,0:T(8,128)(2,1)} %get-tuple-element.69), channel_id=1, source_target_pairs={{0,0},{1,4},{2,8},{3,12},{4,1},{5,5},{6,9},{7,13},{8,2},{9,6},{10,... | collective-permute-start | bytes 393224 | tf_op jit(solution)/shard_map/ppermute | solution.py:87
  92.9 5.8 %collective-permute-start.25 = (bf16[512,128]{1,0:T(8,128)(2,1)}, bf16[512,128]{1,0:T(8,128)(2,1)S(1)}, u32[]{:S(2)}, u32[]{:S(2)}) collective-permute-start(bf16[512,128]{1,0:T(8,128)(2,1)} %get-tuple-element.70), channel_id=1, source_target_pairs={{0,1},{1,5},{2,9},{3,13},{4,0},{5,4},{6,8},{7,12},{8,3},{9,7},{10,... | collective-permute-start | bytes 393224 | tf_op jit(solution)/shard_map/ppermute | solution.py:87
  95.6 15.8 %collective-permute-start.26 = (bf16[512,128]{1,0:T(8,128)(2,1)S(1)}, bf16[512,128]{1,0:T(8,128)(2,1)S(1)}, u32[]{:S(2)}, u32[]{:S(2)}) collective-permute-start(bf16[512,128]{1,0:T(8,128)(2,1)S(1)} %get-tuple-element.71), channel_id=1, source_target_pairs={{0,2},{1,6},{2,10},{3,14},{4,3},{5,7},{6,11},{7,15},{8,0},{9,4},{1... | collective-permute-start | bytes 393224 | tf_op jit(solution)/shard_map/ppermute | solution.py:87
  98.0 13.5 %collective-permute-start.27 = (bf16[512,128]{1,0:T(8,128)(2,1)S(1)}, bf16[512,128]{1,0:T(8,128)(2,1)S(1)}, u32[]{:S(2)}, u32[]{:S(2)}) collective-permute-start(bf16[512,128]{1,0:T(8,128)(2,1)S(1)} %get-tuple-element.72), channel_id=1, source_target_pairs={{0,3},{1,7},{2,11},{3,15},{4,2},{5,6},{6,10},{7,14},{8,1},{9,5},{1... | collective-permute-start | bytes 393224 | tf_op jit(solution)/shard_map/ppermute | solution.py:87
  113.3 5.8 %collective-permute-start.32 = (bf16[512,128]{1,0:T(8,128)(2,1)S(1)}, bf16[512,128]{1,0:T(8,128)(2,1)S(1)}, u32[]{:S(2)}, u32[]{:S(2)}) collective-permute-start(bf16[512,128]{1,0:T(8,128)(2,1)S(1)} %get-tuple-element.77), channel_id=1, source_target_pairs={{0,1},{1,0},{2,3},{3,2},{4,5},{5,4},{6,7},{7,6},{8,9},{9,8},{10,11... | collective-permute-start | bytes 393224 | tf_op jit(solution)/shard_map/ppermute | solution.py:76
  113.4 12.4 %collective-permute-start.33 = (bf16[512,128]{1,0:T(8,128)(2,1)S(1)}, bf16[512,128]{1,0:T(8,128)(2,1)S(1)}, u32[]{:S(2)}, u32[]{:S(2)}) collective-permute-start(bf16[512,128]{1,0:T(8,128)(2,1)S(1)} %get-tuple-element.78), channel_id=1, source_target_pairs={{0,2},{1,3},{2,0},{3,1},{4,6},{5,7},{6,4},{7,5},{8,10},{9,11},{10,... | collective-permute-start | bytes 393224 | tf_op jit(solution)/shard_map/ppermute | solution.py:76
  115.7 10.0 %collective-permute-start.34 = (bf16[512,128]{1,0:T(8,128)(2,1)S(1)}, bf16[512,128]{1,0:T(8,128)(2,1)S(1)}, u32[]{:S(2)}, u32[]{:S(2)}) collective-permute-start(bf16[512,128]{1,0:T(8,128)(2,1)S(1)} %get-tuple-element.79), channel_id=1, source_target_pairs={{0,3},{1,2},{2,1},{3,0},{4,7},{5,6},{6,5},{7,4},{8,11},{9,10},{10,... | collective-permute-start | bytes 393224 | tf_op jit(solution)/shard_map/ppermute | solution.py:76
  (16 other events, 135.8 us)
